TPU v7x, 32 devices: a whole 2x2x4 slice. The times are simulated.
32 devices in a mesh: dp: 4 (over y, x), seq: 8 (over z, core).
Axes of the slice: x: 2, y: 2, z: 4, core: 2. Of those that a mesh axis runs over, the one named last changes fastest.
Arguments:
- block_input: bfloat16 [8192, 2048], P(('dp', 'seq')), may hold values from -6 to 6
- lengths: int32 [4, 2], P('dp'), may hold values from 1024 to 1024, as said below
- norm_gain: float32 [2048], replicated, may hold values from 0.25 to 1.75
- w_q: bfloat16 [2048, 2048], P('seq'), may hold values from -0.125 to 0.125
- w_f: bfloat16 [2048, 2048], P('seq'), may hold values from -0.125 to 0.125
- w_i: bfloat16 [2048, 2048], P('seq'), may hold values from -0.125 to 0.125
- w_g: bfloat16 [2048, 2048], P('seq'), may hold values from -0.125 to 0.125
- lower_bound: float32 [2048], replicated, may hold values from 0.7 to 1
- group_gain: float32 [128], replicated, may hold values from 0.25 to 1.75
- w_o: bfloat16 [2048, 2048], P('seq'), may hold values from -0.1875 to 0.1875
- ffn_norm_gain: float32 [2048], replicated, may hold values from 0.25 to 1.75
- w_gate: bfloat16 [2048, 5632], P('seq'), may hold values from -0.125 to 0.125
- w_up: bfloat16 [2048, 5632], P('seq'), may hold values from -0.125 to 0.125
- w_down: bfloat16 [5632, 2048], P('seq'), may hold values from -0.109375 to 0.109375
- out_grad: bfloat16 [8192, 2048], P(('dp', 'seq')), may hold values from -6 to 6
Outputs:
- out: bfloat16 [8192, 2048], P(('dp', 'seq'))
- input_grad: bfloat16 [8192, 2048], P(('dp', 'seq'))
- norm_gain_grad: float32 [2048], replicated
- w_q_grad: float32 [2048, 2048], P('seq')
- w_f_grad: float32 [2048, 2048], P('seq')
- w_i_grad: float32 [2048, 2048], P('seq')
- w_g_grad: float32 [2048, 2048], P('seq')
- lower_bound_grad: float32 [2048], replicated
- group_gain_grad: float32 [128], replicated
- w_o_grad: float32 [2048, 2048], P('seq')
- ffn_norm_gain_grad: float32 [2048], replicated
- w_gate_grad: float32 [2048, 5632], P('seq')
- w_up_grad: float32 [2048, 5632], P('seq')
- w_down_grad: float32 [5632, 2048], P('seq')
Inputs may be any that keep to these rules, and one draw needn't show every extreme that they name: The lengths of each group sum to 2048.
All inputs are finite; a program needn't handle non-finite values.
Results may differ from a plain program's by a relative error of at most 0.02.
The roundings to bfloat16 on the way count: a program that leaves them out, or rounds other values in their place, can miss the bound.
Values may be sent and summed in bfloat16 or wider, within the bound.
No kernel may reach another device: no remote copies, remote signals or barrier semaphores. Data moves between devices by JAX's collectives and lax.ppermute only.
A program may use at most 512 MiB of HBM per device.

v0:
```python
import jax
import jax.numpy as jnp
from jax import lax
from jax.sharding import PartitionSpec as P

SPAN = 128


EPS = 1e-06
HIGH = lax.Precision.HIGHEST


def entering(array, axis, join, neutral):
    place = lax.axis_index(axis)
    gathered = jax.tree.map(
        lambda a, kind: lax.all_gather(a.astype(kind), axis), array, (jnp.bfloat16, jnp.bfloat16)
    )
    state = jax.tree.map(lambda a, e: jnp.zeros_like(a) + jnp.asarray(e, a.dtype), array, neutral)

    def one(hop, state):
        return join(
            state,
            jax.tree.map(
                lambda a, own: lax.dynamic_index_in_dim(a, hop, 0, False).astype(own.dtype),
                gathered,
                array,
            ),
        )

    return lax.fori_loop(0, place, one, state)


def carried_in(array, axis, combine, identity):
    devices, position = (lax.axis_size(axis), lax.axis_index(axis))
    everything = jax.tree.map(
        lambda part, kind: lax.all_gather(part.astype(kind), axis),
        array,
        jax.tree.map(lambda a: jnp.bfloat16 if a.dtype == jnp.float32 else a.dtype, array),
    )
    start = jax.tree.map(
        lambda part, zero: jnp.broadcast_to(jnp.asarray(zero, part.dtype), part.shape),
        array,
        identity,
    )

    def hop(k, before):
        at = devices - 1 - k
        reached = at > position
        new = combine(
            before, jax.tree.map(lambda part, own: part[at].astype(own.dtype), everything, array)
        )
        return jax.tree.map(lambda a, b: jnp.where(reached, a, b), new, before)

    return lax.fori_loop(0, devices, hop, start)


def silu(value):
    return value * jax.nn.sigmoid(value)


def rms_scale(value, gain):
    return value * lax.rsqrt(jnp.mean(value * value, axis=-1, keepdims=True) + EPS) * gain


def swiglu(gate, upper):
    return silu(gate) * upper


def span_step(carry, block):
    state, decay = carry
    q_blk, k_blk, a_blk, v_blk, sid_blk, start_blk = block
    size = q_blk.shape[0]
    cumul = jnp.cumsum(a_blk, axis=0)
    inherit = (jnp.cumsum(start_blk) == 0).astype(jnp.float32)
    rows = lax.broadcasted_iota(jnp.int32, (size, size), 0)
    cols = lax.broadcasted_iota(jnp.int32, (size, size), 1)
    allowed = (sid_blk[:, None] == sid_blk[None, :]) & (cols <= rows)
    q_dec = q_blk * jnp.exp(cumul)
    k_dec = k_blk * jnp.exp(-cumul)
    scores = jnp.einsum("thi,shi->hts", q_dec, k_dec, precision=HIGH)
    scores = jnp.where(allowed[None], scores, 0.0)
    carried = jnp.einsum("thi,hij->thj", q_dec, state, precision=HIGH)
    out_blk = (
        jnp.einsum("hts,shj->thj", scores, v_blk, precision=HIGH) + inherit[:, None, None] * carried
    )
    from_start = q_dec * (decay[None] * inherit[:, None, None])
    last = cumul[-1]
    same_last = (sid_blk == sid_blk[-1]).astype(jnp.float32)
    tail = k_blk * jnp.exp(last[None] - cumul) * same_last[:, None, None]
    keep = inherit[-1]
    new_state = keep * jnp.exp(last)[:, :, None] * state + jnp.einsum(
        "shi,shj->hij", tail, v_blk, precision=HIGH
    )
    new_decay = decay * jnp.exp(last) * keep
    return ((new_state, new_decay), (out_blk, from_start))


def combine(earlier, later):
    return (earlier[0] * later[0], later[0][..., None] * earlier[1] + later[1])


def dot_first(left, right):
    return lax.dot_general(
        left, right, (((0,), (0,)), ((), ())), preferred_element_type=jnp.float32
    )


def dot_last(left, right):
    return lax.dot_general(
        left, right, (((1,), (1,)), ((), ())), preferred_element_type=jnp.float32
    )


def shards(
    block_input,
    lengths,
    norm_gain,
    w_q,
    w_f,
    w_i,
    w_g,
    lower_bound,
    group_gain,
    w_o,
    ffn_norm_gain,
    w_gate,
    w_up,
    w_down,
    out_grad,
):
    tok_count = block_input.shape[0]
    width = block_input.shape[1]
    head_dim = group_gain.shape[0]
    head_count = width // head_dim
    full_q, full_f, full_i, full_g, full_o, full_gate, full_up, full_down = (
        lax.all_gather(w_q, "seq", axis=0, tiled=True),
        lax.all_gather(w_f, "seq", axis=0, tiled=True),
        lax.all_gather(w_i, "seq", axis=0, tiled=True),
        lax.all_gather(w_g, "seq", axis=0, tiled=True),
        lax.all_gather(w_o, "seq", axis=0, tiled=True),
        lax.all_gather(w_gate, "seq", axis=0, tiled=True),
        lax.all_gather(w_up, "seq", axis=0, tiled=True),
        lax.all_gather(w_down, "seq", axis=0, tiled=True),
    )
    positions = lax.axis_index("seq") * tok_count + lax.iota(jnp.int32, tok_count)
    lengths_row = lengths[0]
    offsets = jnp.cumsum(lengths_row) - lengths_row
    seq_ids = jnp.sum((positions[:, None] >= offsets[None, :]).astype(jnp.int32), axis=1) - 1
    begins = jnp.sum((positions[:, None] == offsets[None, :]).astype(jnp.float32), axis=1)
    input_float = block_input.astype(jnp.float32)
    hnorm, norm_back = jax.vjp(rms_scale, input_float, norm_gain)
    hnorm_low = hnorm.astype(jnp.bfloat16)
    qz = jnp.dot(hnorm_low, full_q, preferred_element_type=jnp.float32)
    fz = jnp.dot(hnorm_low, full_f, preferred_element_type=jnp.float32)
    vz = jnp.dot(hnorm_low, full_i, preferred_element_type=jnp.float32)
    gz = jnp.dot(hnorm_low, full_g, preferred_element_type=jnp.float32)

    def mixer_local(qz_in, fz_in, vz_in, bound):
        query = silu(qz_in)
        forget = bound + (1.0 - bound) * jax.nn.sigmoid(fz_in)
        keyed = 1.0 - forget
        log_forget = jnp.log(forget)

        def split(value):
            return value.reshape(tok_count // SPAN, SPAN, head_count, head_dim)

        blocks = (
            split(query),
            split(keyed),
            split(log_forget),
            split(vz_in),
            seq_ids.reshape(-1, SPAN),
            begins.reshape(-1, SPAN),
        )
        start_carry = (
            jnp.zeros((head_count, head_dim, head_dim), jnp.float32),
            jnp.ones((head_count, head_dim), jnp.float32),
        )
        (end_state, end_decay), (outs, from_start) = lax.scan(
            jax.checkpoint(span_step), start_carry, blocks
        )
        shape = (tok_count, head_count, head_dim)
        return (outs.reshape(shape), from_start.reshape(shape), end_decay, end_state)

    (local_out, from_start, end_decay, end_state), mixer_back = jax.vjp(
        mixer_local, qz, fz, vz, lower_bound
    )
    identity = (
        jnp.ones((head_count, head_dim), jnp.float32),
        jnp.zeros((head_count, head_dim, head_dim), jnp.float32),
    )
    enter_decay, enter_state = entering((end_decay, end_state), "seq", combine, identity)

    def gated_norm(local_in, start_in, state_in, gz_in, gain_in):
        mixed = local_in + jnp.einsum("thi,hij->thj", start_in, state_in, precision=HIGH)
        normed = mixed * lax.rsqrt(jnp.mean(mixed * mixed, axis=-1, keepdims=True) + EPS) * gain_in
        return normed.reshape(tok_count, width) * silu(gz_in)

    gated, gate_back = jax.vjp(gated_norm, local_out, from_start, enter_state, gz, group_gain)
    gated_low = gated.astype(jnp.bfloat16)
    resid = input_float + jnp.dot(gated_low, full_o, preferred_element_type=jnp.float32)
    hnorm_two, ffn_norm_back = jax.vjp(rms_scale, resid, ffn_norm_gain)
    hnorm_two_low = hnorm_two.astype(jnp.bfloat16)
    gate = jnp.dot(hnorm_two_low, full_gate, preferred_element_type=jnp.float32)
    upper = jnp.dot(hnorm_two_low, full_up, preferred_element_type=jnp.float32)
    hidden, swiglu_back = jax.vjp(swiglu, gate, upper)
    hidden_low = hidden.astype(jnp.bfloat16)
    result = (resid + jnp.dot(hidden_low, full_down, preferred_element_type=jnp.float32)).astype(
        jnp.bfloat16
    )
    grad_float = out_grad.astype(jnp.float32)
    d_hidden = dot_last(out_grad, full_down)
    d_gate, d_upper = swiglu_back(d_hidden)
    d_gate_low = d_gate.astype(jnp.bfloat16)
    d_upper_low = d_upper.astype(jnp.bfloat16)
    d_hnorm_two = dot_last(d_gate_low, full_gate) + dot_last(d_upper_low, full_up)
    d_resid_norm, d_ffn_gain = ffn_norm_back(d_hnorm_two)
    d_resid = grad_float + d_resid_norm
    ffn_terms = (
        dot_first(hnorm_two_low, d_gate_low),
        dot_first(hnorm_two_low, d_upper_low),
        dot_first(hidden_low, out_grad),
    )
    ffn_rows = (
        lax.psum_scatter(
            ffn_terms[0].astype(jnp.bfloat16), "seq", scatter_dimension=0, tiled=True
        ).astype(jnp.float32),
        lax.psum_scatter(
            ffn_terms[1].astype(jnp.bfloat16), "seq", scatter_dimension=0, tiled=True
        ).astype(jnp.float32),
        lax.psum_scatter(
            ffn_terms[2].astype(jnp.bfloat16), "seq", scatter_dimension=0, tiled=True
        ).astype(jnp.float32),
    )
    d_branch = d_resid.astype(jnp.bfloat16)
    d_gated = dot_last(d_branch, full_o)
    d_local, d_start, d_enter, d_gz, d_group_gain = gate_back(d_gated)
    later_decay, later_grad = carried_in((end_decay, d_enter), "seq", combine, identity)
    d_decay = jnp.sum(later_grad * enter_state, axis=-1)
    d_qz, d_fz, d_vz, d_bound = mixer_back((d_local, d_start, d_decay, later_grad))
    d_qz_low = d_qz.astype(jnp.bfloat16)
    d_fz_low = d_fz.astype(jnp.bfloat16)
    d_vz_low = d_vz.astype(jnp.bfloat16)
    d_gz_low = d_gz.astype(jnp.bfloat16)
    d_hnorm = (
        dot_last(d_qz_low, full_q)
        + dot_last(d_fz_low, full_f)
        + dot_last(d_vz_low, full_i)
        + dot_last(d_gz_low, full_g)
    )
    d_input_norm, d_norm_gain = norm_back(d_hnorm)
    input_grad = (d_resid + d_input_norm).astype(jnp.bfloat16)
    mixer_terms = (
        dot_first(hnorm_low, d_qz_low),
        dot_first(hnorm_low, d_fz_low),
        dot_first(hnorm_low, d_vz_low),
        dot_first(hnorm_low, d_gz_low),
        dot_first(gated_low, d_branch),
    )
    mixer_rows = (
        lax.psum_scatter(
            mixer_terms[0].astype(jnp.bfloat16), "seq", scatter_dimension=0, tiled=True
        ).astype(jnp.float32),
        lax.psum_scatter(
            mixer_terms[1].astype(jnp.bfloat16), "seq", scatter_dimension=0, tiled=True
        ).astype(jnp.float32),
        lax.psum_scatter(
            mixer_terms[2].astype(jnp.bfloat16), "seq", scatter_dimension=0, tiled=True
        ).astype(jnp.float32),
        lax.psum_scatter(
            mixer_terms[3].astype(jnp.bfloat16), "seq", scatter_dimension=0, tiled=True
        ).astype(jnp.float32),
        lax.psum_scatter(
            mixer_terms[4].astype(jnp.bfloat16), "seq", scatter_dimension=0, tiled=True
        ).astype(jnp.float32),
    )
    summed = (
        lax.psum(mixer_rows[0].astype(jnp.bfloat16), "dp").astype(jnp.float32),
        lax.psum(mixer_rows[1].astype(jnp.bfloat16), "dp").astype(jnp.float32),
        lax.psum(mixer_rows[2].astype(jnp.bfloat16), "dp").astype(jnp.float32),
        lax.psum(mixer_rows[3].astype(jnp.bfloat16), "dp").astype(jnp.float32),
        lax.psum(mixer_rows[4].astype(jnp.bfloat16), "dp").astype(jnp.float32),
        lax.psum(ffn_rows[0].astype(jnp.bfloat16), "dp").astype(jnp.float32),
        lax.psum(ffn_rows[1].astype(jnp.bfloat16), "dp").astype(jnp.float32),
        lax.psum(ffn_rows[2].astype(jnp.bfloat16), "dp").astype(jnp.float32),
    )
    small = lax.psum((d_norm_gain, d_ffn_gain, d_group_gain, d_bound), ("dp", "seq"))
    return (
        result,
        input_grad,
        small[0],
        summed[0],
        summed[1],
        summed[2],
        summed[3],
        small[3],
        small[2],
        summed[4],
        small[1],
        summed[5],
        summed[6],
        summed[7],
    )


def solution(mesh):
    placed = (
        P(("dp", "seq"), None),
        P("dp", None),
        P(),
        P("seq", None),
        P("seq", None),
        P("seq", None),
        P("seq", None),
        P(),
        P(),
        P("seq", None),
        P(),
        P("seq", None),
        P("seq", None),
        P("seq", None),
        P(("dp", "seq"), None),
    )
    return jax.shard_map(
        shards,
        mesh=mesh,
        in_specs=placed,
        out_specs=(
            P(("dp", "seq"), None),
            P(("dp", "seq"), None),
            P(),
            P("seq", None),
            P("seq", None),
            P("seq", None),
            P("seq", None),
            P(),
            P(),
            P("seq", None),
            P(),
            P("seq", None),
            P("seq", None),
            P("seq", None),
        ),
        check_vma=False,
    )
```

profile of v0, /device:TPU:0, one launch (start us, length us, event | category | flops | bytes accessed | tf_op | source)
XLA Modules:
  0.0 2731.3 jit_solution(3198580454335646547)
XLA Ops:
  10.7 83.7 %all-gather.14.cloned.1.call-done = bf16[2048,2048]{1,0:T(8,128)(2,1)} async-done(((bf16[256,2048]{1,0:T(8,128)(2,1)}), bf16[2048,2048]{1,0:T(8,128)(2,1)}) %all-gather.14.cloned.1.call-update) | async-done | bytes 8388624 | tf_op jit(solution)/shard_map/all_gather | solution.py:137
  105.0 71.6 %all-gather.16.cloned.1.call-done = bf16[2048,2048]{1,0:T(8,128)(2,1)} async-done(((bf16[256,2048]{1,0:T(8,128)(2,1)}), bf16[2048,2048]{1,0:T(8,128)(2,1)}) %all-gather.16.cloned.1.call-update) | async-done | bytes 8388624 | tf_op jit(solution)/shard_map/all_gather | solution.py:138
  184.8 74.1 %all-gather.18.cloned.1.call-done = bf16[2048,2048]{1,0:T(8,128)(2,1)} async-done(((bf16[256,2048]{1,0:T(8,128)(2,1)}), bf16[2048,2048]{1,0:T(8,128)(2,1)}) %all-gather.18.cloned.1.call-update) | async-done | bytes 8388624 | tf_op jit(solution)/shard_map/all_gather | solution.py:136
  269.1 94.8 %while.76 = (s32[]{:T(128)}, f32[16,128,128]{2,1,0:T(8,128)S(1)}, f32[16,128]{1,0:T(8,128)S(1)}, f32[2,128,16,128]{1,0,3,2:T(2,128)}, f32[2,128,16,128]{3,2,1,0:...) while((s32[]{:T(128)}, f32[16,128,128]{2,1,0:T(8,128)S(1)}, ...), condition=%wide.region_7.8_spmd.clone, body=%wide.region_4.7_spmd.clone.sunk | while | flops 1648435840 | bytes 29502700 | solution.py:179
  290.0 26.6 dynamic_update_slice.85
  337.3 26.6 dynamic_update_slice.85
  374.2 14.0 all-gather
  388.2 22.7 all-gather.30.cloned.1.call-done
  428.8 64.4 %all-gather.20.cloned.1.call-done = bf16[2048,2048]{1,0:T(8,128)(2,1)} async-done(((bf16[256,2048]{1,0:T(8,128)(2,1)}), bf16[2048,2048]{1,0:T(8,128)(2,1)}) %all-gather.20.cloned.1.call-update) | async-done | bytes 8388624 | tf_op jit(solution)/shard_map/all_gather | solution.py:139
  501.0 74.3 %all-gather.22.cloned.1.call-done = bf16[2048,2048]{1,0:T(8,128)(2,1)} async-done(((bf16[256,2048]{1,0:T(8,128)(2,1)}), bf16[2048,2048]{1,0:T(8,128)(2,1)}) %all-gather.22.cloned.1.call-update) | async-done | bytes 8388624 | tf_op jit(solution)/shard_map/all_gather | solution.py:140
  582.7 195.4 %all-gather.24.cloned.1.call-done = bf16[2048,5632]{1,0:T(8,128)(2,1)} async-done(((bf16[256,5632]{1,0:T(8,128)(2,1)}), bf16[2048,5632]{1,0:T(8,128)(2,1)}) %all-gather.24.cloned.1.call-update) | async-done | bytes 23068688 | tf_op jit(solution)/shard_map/all_gather | solution.py:141
  778.2 14.9 fusion.118
  793.0 187.7 %all-gather.26.cloned.1.call-done = bf16[2048,5632]{1,0:T(8,128)(2,1)} async-done(((bf16[256,5632]{1,0:T(8,128)(2,1)}), bf16[2048,5632]{1,0:T(8,128)(2,1)}) %all-gather.26.cloned.1.call-update) | async-done | bytes 23068688 | tf_op jit(solution)/shard_map/all_gather | solution.py:142
  980.7 14.9 fusion.119
  995.5 187.7 %all-gather.28.cloned.1.call-done = bf16[5632,2048]{1,0:T(8,128)(2,1)} async-done(((bf16[704,2048]{1,0:T(8,128)(2,1)}), bf16[5632,2048]{1,0:T(8,128)(2,1)}) %all-gather.28.cloned.1.call-update) | async-done | bytes 23068688 | tf_op jit(solution)/shard_map/all_gather | solution.py:143
  1183.2 18.7 multiply_convert_fusion
  1214.6 14.5 multiply_reduce_fusion.2
  1275.5 23.1 all-gather.32.cloned.1.call-done
  1298.6 13.9 while.77
  1318.6 146.2 %while.75 = (s32[]{:T(128)}, f32[16,128,128]{2,1,0:T(8,128)S(1)}, f32[16,128]{1,0:T(8,128)S(1)}, f32[2,128,16,128]{3,2,1,0:T(8,128)}, f32[2,128,16,128]{3,1,2,0:...) while((s32[]{:T(128)}, f32[16,128,128]{2,1,0:T(8,128)S(1)}, ...), condition=%wide.region_24.25_spmd, body=%wide.region_17.24_spmd.sunk | while | flops 3703124480 | bytes 178506512 | solution.py:179
  1334.5 23.2 fusion.240
  1407.2 23.2 fusion.240
  1498.1 12.9 convolution_convert_fusion.2
  1538.2 31.5 %reduce-scatter.9.cloned.1.call-done = bf16[256,2048]{1,0:T(8,128)(2,1)} async-done(((bf16[2048,2048]{1,0:T(8,128)(2,1)}), bf16[256,2048]{1,0:T(8,128)(2,1)}) %reduce-scatter.9.cloned.1.call-update) | async-done | bytes 1048592 | tf_op jit(solution)/shard_map/reduce_scatter | solution.py:261
  1569.7 90.1 %reduce-scatter.11.cloned.1.call-done = bf16[256,2048]{1,0:T(8,128)(2,1)} async-done(((bf16[2048,2048]{1,0:T(8,128)(2,1)}), bf16[256,2048]{1,0:T(8,128)(2,1)}) %reduce-scatter.11.cloned.1.call-update) | async-done | bytes 1048592 | tf_op jit(solution)/shard_map/reduce_scatter | solution.py:264
  1659.9 90.1 %reduce-scatter.13.cloned.1.call-done = bf16[256,2048]{1,0:T(8,128)(2,1)} async-done(((bf16[2048,2048]{1,0:T(8,128)(2,1)}), bf16[256,2048]{1,0:T(8,128)(2,1)}) %reduce-scatter.13.cloned.1.call-update) | async-done | bytes 1048592 | tf_op jit(solution)/shard_map/reduce_scatter | solution.py:267
  1750.0 228.0 %reduce-scatter.19.cloned.1.call-done = bf16[256,5632]{1,0:T(8,128)(2,1)} async-done(((bf16[2048,5632]{1,0:T(8,128)(2,1)}), bf16[256,5632]{1,0:T(8,128)(2,1)}) %reduce-scatter.19.cloned.1.call-update) | async-done | bytes 2883600 | tf_op jit(solution)/shard_map/reduce_scatter | solution.py:225
  1978.0 228.0 %reduce-scatter.21.cloned.1.call-done = bf16[256,5632]{1,0:T(8,128)(2,1)} async-done(((bf16[2048,5632]{1,0:T(8,128)(2,1)}), bf16[256,5632]{1,0:T(8,128)(2,1)}) %reduce-scatter.21.cloned.1.call-update) | async-done | bytes 2883600 | tf_op jit(solution)/shard_map/reduce_scatter | solution.py:228
  2206.1 228.0 %reduce-scatter.23.cloned.1.call-done = bf16[704,2048]{1,0:T(8,128)(2,1)} async-done(((bf16[5632,2048]{1,0:T(8,128)(2,1)}), bf16[704,2048]{1,0:T(8,128)(2,1)}) %reduce-scatter.23.cloned.1.call-update) | async-done | bytes 2883600 | tf_op jit(solution)/shard_map/reduce_scatter | solution.py:231
  2435.7 13.7 fusion.65
  2468.7 38.9 %all-reduce.1 = (f32[2048]{0:T(1024)}, f32[2048]{0:T(1024)}, f32[128]{0:T(128)}, f32[2048]{0:T(1024)}) all-reduce(f32[2048]{0:T(1024)S(1)} %get-tuple-element.856, f32[2048]{0:T(1024)S(1)} %negate_add_fusion, f32[128]{0:T(128)S(1)} %copy-done.72, f32[2048]{0:T(1024)S(1)} %copy-done.70), channel_id=1, replica_groups=mesh['dp'=4,'seq'=8] {'dp','seq'}, use_global_device_ids=true, to_apply=%region_27.28 | all-reduce | flops 6272 | bytes 50176 | tf_op jit(solution)/shard_map/psum | solution.py:287
  2510.8 193.6 %all-reduce.5.cloned.1.call-done = (bf16[256,2048]{1,0:T(8,128)(2,1)}, bf16[256,2048]{1,0:T(8,128)(2,1)}, bf16[256,2048]{1,0:T(8,128)(2,1)}, bf16[256,2048]{1,0:...) async-done(((bf16[256,2048]{1,0:T(8,128)(2,1)}, bf16[256,2048]{1,0:T(8,128)(2,1)}, ...) | async-done | bytes 13893648 | tf_op jit(solution)/shard_map/psum | solution.py:278
  (448 shorter events, 397.8 us)
Async XLA Ops:
  7.2 87.2 %copy-start.52 = (f32[2048]{0:T(1024)S(1)}, f32[2048]{0:T(1024)}, u32[]{:S(2)}) copy-start(f32[2048]{0:T(1024)} %param.25) | copy-start | bytes 24580
  7.2 87.2 %all-gather.14.cloned.1.call-start = ((), (), s32[]{:S(2)}) async-start(), calls=%async_computation.8 | async-start | bytes 9437184 | tf_op jit(solution)/shard_map/all_gather | solution.py:137
  8.0 168.7 %all-gather.16.cloned.1.call-start = ((), (), s32[]{:S(2)}) async-start(), calls=%async_computation.9 | async-start | bytes 9437184 | tf_op jit(solution)/shard_map/all_gather | solution.py:138
  8.7 250.2 %all-gather.18.cloned.1.call-start = ((), (), s32[]{:S(2)}) async-start(), calls=%async_computation.10 | async-start | bytes 9437184 | tf_op jit(solution)/shard_map/all_gather | solution.py:136
  9.4 401.4 %all-gather.30.cloned.1.call-start = ((), (), s32[]{:S(2)}) async-start(), calls=%async_computation.24 | async-start | bytes 4718592 | tf_op jit(solution)/shard_map/all_gather | solution.py:16
  10.7 89.6 %copy-start.59 = (f32[2048]{0:T(1024)}, f32[2048]{0:T(1024)S(1)}, u32[]{:S(2)}) copy-start(f32[2048]{0:T(1024)S(1)} %broadcast_subtract_fusion) | copy-start | bytes 24580
  364.8 128.3 %all-gather.20.cloned.1.call-start = ((), (), s32[]{:S(2)}) async-start(), calls=%async_computation.11 | async-start | bytes 9437184 | tf_op jit(solution)/shard_map/all_gather | solution.py:139
  365.4 209.8 %all-gather.22.cloned.1.call-start = ((), (), s32[]{:S(2)}) async-start(), calls=%async_computation.12 | async-start | bytes 9437184 | tf_op jit(solution)/shard_map/all_gather | solution.py:140
  366.0 412.1 %all-gather.24.cloned.1.call-start = ((), (), s32[]{:S(2)}) async-start(), calls=%async_computation.13 | async-start | bytes 25952256 | tf_op jit(solution)/shard_map/all_gather | solution.py:141
  366.8 613.9 %all-gather.26.cloned.1.call-start = ((), (), s32[]{:S(2)}) async-start(), calls=%async_computation.14 | async-start | bytes 25952256 | tf_op jit(solution)/shard_map/all_gather | solution.py:142
  367.5 815.7 %all-gather.28.cloned.1.call-start = ((), (), s32[]{:S(2)}) async-start(), calls=%async_computation.15 | async-start | bytes 25952256 | tf_op jit(solution)/shard_map/all_gather | solution.py:143
  368.3 930.4 %all-gather.32.cloned.1.call-start = ((), (), s32[]{:S(2)}) async-start(), calls=%async_computation.25 | async-start | bytes 4718592 | tf_op jit(solution)/shard_map/all_gather | solution.py:36
  501.0 80.1 %copy-start.50 = (bf16[256,2048]{1,0:T(8,128)(2,1)}, bf16[256,2048]{1,0:T(8,128)(2,1)S(1)}, u32[]{:S(2)}) copy-start(bf16[256,2048]{1,0:T(8,128)(2,1)S(1)} %get-tuple-element.986) | copy-start | bytes 3145732
  582.7 398.0 %copy-start.21 = (bf16[256,2048]{1,0:T(8,128)(2,1)}, bf16[256,2048]{1,0:T(8,128)(2,1)S(1)}, u32[]{:S(2)}) copy-start(bf16[256,2048]{1,0:T(8,128)(2,1)S(1)} %multiply_convert_fusion.2) | copy-start | bytes 3145732
  1214.6 14.5 copy-start.35
  1232.2 8.6 copy-start.15
  1240.8 12.9 copy-start.57
  1253.2 285.0 %reduce-scatter.15.cloned.1.call-start = ((), (), s32[]{:S(2)}) async-start(), calls=%async_computation.19 | async-start | bytes 9437184 | tf_op jit(solution)/shard_map/reduce_scatter | solution.py:270
  1259.4 278.8 %reduce-scatter.17.cloned.1.call-start = ((), (), s32[]{:S(2)}) async-start(), calls=%async_computation.20 | async-start | bytes 9437184 | tf_op jit(solution)/shard_map/reduce_scatter | solution.py:273
  1275.5 294.3 %reduce-scatter.9.cloned.1.call-start = ((), (), s32[]{:S(2)}) async-start(), calls=%async_computation.16 | async-start | bytes 9437184 | tf_op jit(solution)/shard_map/reduce_scatter | solution.py:261
  1332.0 27.0 copy-start
  1404.8 27.0 copy-start
  1475.2 184.7 %reduce-scatter.11.cloned.1.call-start = ((), (), s32[]{:S(2)}) async-start(), calls=%async_computation.17 | async-start | bytes 9437184 | tf_op jit(solution)/shard_map/reduce_scatter | solution.py:264
  1488.7 261.3 %reduce-scatter.13.cloned.1.call-start = ((), (), s32[]{:S(2)}) async-start(), calls=%async_computation.18 | async-start | bytes 9437184 | tf_op jit(solution)/shard_map/reduce_scatter | solution.py:267
  1496.9 481.2 %reduce-scatter.19.cloned.1.call-start = ((), (), s32[]{:S(2)}) async-start(), calls=%async_computation.21 | async-start | bytes 25952256 | tf_op jit(solution)/shard_map/reduce_scatter | solution.py:225
  1511.0 695.1 %reduce-scatter.21.cloned.1.call-start = ((), (), s32[]{:S(2)}) async-start(), calls=%async_computation.22 | async-start | bytes 25952256 | tf_op jit(solution)/shard_map/reduce_scatter | solution.py:228
  1523.8 910.3 %reduce-scatter.23.cloned.1.call-start = ((), (), s32[]{:S(2)}) async-start(), calls=%async_computation.23 | async-start | bytes 25952256 | tf_op jit(solution)/shard_map/reduce_scatter | solution.py:231
  1537.9 1166.5 %all-reduce.5.cloned.1.call-start = ((), (), s32[]{:S(2)}) async-start(), calls=%async_computation.26 | async-start | bytes 27787264 | tf_op jit(solution)/shard_map/psum | solution.py:278
  2435.7 13.7 copy-start.41
  2449.4 12.5 slice-start
  2464.6 43.0 %copy-start.69 = (f32[256]{0:T(256)S(1)}, f32[256]{0:T(256)}, u32[]{:S(2)}) copy-start(f32[256]{0:T(256)} %copy-done.68) | copy-start | bytes 3076
  2464.6 43.1 %copy-start.17 = (f32[256,2048]{1,0:T(8,128)S(1)}, f32[256,2048]{1,0:T(8,128)}, u32[]{:S(2)}) copy-start(f32[256,2048]{1,0:T(8,128)} %copy-done.15) | copy-start | bytes 6291460
  (85 other events, 255.3 us)
Sparse Core Ops, SparseCore 0:
  9.7 84.7 all-gather.13
  96.0 80.5 all-gather.15
  178.3 80.5 all-gather.17
  364.9 45.8 all-gather.29
  412.3 80.7 all-gather.19
  494.6 80.5 all-gather.21
  576.9 201.2 all-gather.23
  779.8 200.8 all-gather.25
  982.3 200.8 all-gather.27
  1253.3 45.3 all-gather.31
  1300.9 88.3 reduce-scatter.14
  1391.4 87.9 reduce-scatter.16
  1481.7 87.9 reduce-scatter.8
  1571.9 87.9 reduce-scatter.10
  1662.0 87.9 reduce-scatter.12
  1752.2 225.7 reduce-scatter.18
  1980.2 225.7 reduce-scatter.20
  2208.3 225.7 reduce-scatter.22
  2438.8 265.6 all-reduce.4
where the time goes:
time: 2740 us; the launch traced here: 2730 us
  waiting for transfers between devices  2080 us (76%)
  matrix products  303 us (11%)
  local copies, waits for them, and re-layouts  151 us (6%)
  other arithmetic  126 us (5%)
  blocking collectives  52.9 us (2%)
    reduce_scatter x1, waiting for transfers between devices, shards(): lax.psum_scatter(ffn_terms[0].astype(jnp.bfloat16), 'seq', scatter_dimens...  228 us
    reduce_scatter x1, waiting for transfers between devices, shards(): lax.psum_scatter(ffn_terms[2].astype(jnp.bfloat16), 'seq', scatter_dimens...  228 us
    reduce_scatter x1, waiting for transfers between devices, shards(): lax.psum_scatter(ffn_terms[1].astype(jnp.bfloat16), 'seq', scatter_dimens...  228 us
    all_gather x1, waiting for transfers between devices, shards(): lax.all_gather(w_gate, 'seq', axis=0, tiled=True)  195 us
    psum x1, waiting for transfers between devices, shards(): lax.psum(mixer_rows[0].astype(jnp.bfloat16), 'dp').astype(jnp.float32)  194 us
    all_gather x1, waiting for transfers between devices, shards(): lax.all_gather(w_down, 'seq', axis=0, tiled=True)  188 us
    all_gather x1, waiting for transfers between devices, shards(): lax.all_gather(w_up, 'seq', axis=0, tiled=True)  188 us
    reduce_scatter x1, waiting for transfers between devices, shards(): lax.psum_scatter(mixer_terms[1].astype(jnp.bfloat16), 'seq', scatter_dime...  90.1 us
  transfers between devices with their start and end apart: 19, of which 17 were waited for; matrix products, arithmetic and copies ran while one was open for 14% of the time, Pallas kernels for 0%

commit v1 on v0

v1 whole, which is shorter than its diff:
```python
import functools

import jax
import jax.numpy as jnp
from jax import lax
from jax.experimental import pallas as pl
from jax.experimental.pallas import tpu as pltpu
from jax.sharding import PartitionSpec as P

EPS = 1e-06
MIN_LEN = 1024
BF = jnp.bfloat16
F32 = jnp.float32


def sigmoid(value):
    return jax.nn.sigmoid(value)


def silu(value):
    return value * sigmoid(value)


def silu_grad(value):
    s = sigmoid(value)
    return s * (1.0 + value * (1.0 - s))


def mm(left, right, kind=F32):
    return jnp.dot(left, right, preferred_element_type=F32).astype(kind)


def dot_first(left, right, kind=F32):
    return lax.dot_general(
        left, right, (((0,), (0,)), ((), ())), preferred_element_type=F32
    ).astype(kind)


def dot_last(left, right, kind=F32):
    return lax.dot_general(
        left, right, (((1,), (1,)), ((), ())), preferred_element_type=F32
    ).astype(kind)


def swap(value, bits):
    count = lax.axis_size("dp")
    return lax.ppermute(value, "dp", [(s, s ^ bits) for s in range(count)])


def gather_dp(own):
    half = own.shape[0] // 2
    one, two = swap(own, 1), swap(own, 2)
    top, bottom = swap(one[:half], 2), swap(two[half:], 1)
    return jnp.concatenate([own, one, two, top, bottom], axis=0)


def scatter_dp(parts):
    rows = parts.shape[0] // 4
    half = rows // 2
    p0, p1, p2, p3 = (parts[k * rows : (k + 1) * rows] for k in range(4))
    top, bottom = swap(p3[:half], 1), swap(p3[half:], 2)
    one_a, two_b = swap(p1[:half], 1), swap(p2[half:], 2)
    two_a = swap((p2[:half].astype(F32) + top.astype(F32)).astype(BF), 2)
    one_b = swap((p1[half:].astype(F32) + bottom.astype(F32)).astype(BF), 1)
    one = jnp.concatenate([one_a, one_b], axis=0).astype(F32)
    two = jnp.concatenate([two_a, two_b], axis=0).astype(F32)
    return p0.astype(F32) + one + two


def absolute(blocks):
    place = lax.axis_index("dp")
    odd, high = (place & 1) == 1, (place & 2) == 2
    a, b, c, d = blocks
    a, b = jnp.where(odd, b, a), jnp.where(odd, a, b)
    c, d = jnp.where(odd, d, c), jnp.where(odd, c, d)
    return (
        jnp.where(high, c, a),
        jnp.where(high, d, b),
        jnp.where(high, a, c),
        jnp.where(high, b, d),
    )


def marks(starts_ref, slot, size, count):
    col = lax.broadcasted_iota(jnp.int32, (size, 1), 0)
    row = lax.broadcasted_iota(jnp.int32, (1, size), 1)
    sid_c = jnp.zeros((size, 1), jnp.int32)
    sid_r = jnp.zeros((1, size), jnp.int32)
    sid_last = jnp.int32(0)
    begun = jnp.zeros((size, 1), jnp.int32)
    ended = jnp.int32(0)
    for j in range(count):
        at = starts_ref[slot, j]
        sid_c += (col >= at).astype(jnp.int32)
        sid_r += (row >= at).astype(jnp.int32)
        sid_last += (size - 1 >= at).astype(jnp.int32)
        begun += ((col >= at) & (at >= 0)).astype(jnp.int32)
        ended += ((size - 1 >= at) & (at >= 0)).astype(jnp.int32)
    inherit = (begun == 0).astype(F32)
    same_last = (sid_c == sid_last).astype(F32)
    keep = (ended == 0).astype(F32)
    return sid_c, sid_r, inherit, same_last, keep


def split_dot(left, value):
    high = value.astype(BF)
    low = (value - high.astype(F32)).astype(BF)
    return mm(left, high) + mm(left, low)


def gates(f, bound):
    sg = sigmoid(f)
    forget = bound + (1.0 - bound) * sg
    return sg, forget, (1.0 - bound) * (1.0 - sg), jnp.log(forget)


def about_middle(size):
    rows = lax.broadcasted_iota(jnp.int32, (size, size), 0)
    cols = lax.broadcasted_iota(jnp.int32, (size, size), 1)
    return (cols <= rows).astype(BF) - (cols < size // 2).astype(BF)


def end_kernel(count, starts, f_ref, v_ref, b_ref, pack_ref):
    size = f_ref.shape[0]
    slot = pl.program_id(1)
    _, _, _, same_last, keep = marks(starts, slot, size, count)
    _, _, k, a = gates(f_ref[...], b_ref[...])
    cm = split_dot(about_middle(size), a)
    last = cm[size - 1 :]
    total = jnp.sum(a, axis=0, keepdims=True)
    tail = (k * jnp.exp(last - cm) * same_last).astype(BF)
    pack_ref[0, :128] = dot_first(v_ref[...].astype(BF), tail).astype(BF)
    pack_ref[0, 128:] = jnp.broadcast_to(jnp.exp(total) * keep, (16, 128)).astype(BF)


def intra_kernel(count, starts, q_ref, f_ref, v_ref, b_ref, out_ref, qs_ref):
    size = f_ref.shape[0]
    slot = pl.program_id(1)
    sid_c, sid_r, inherit, _, _ = marks(starts, slot, size, count)
    _, _, k, a = gates(f_ref[...], b_ref[...])
    cm = split_dot(about_middle(size), a)
    mid = jnp.sum(a[: size // 2], axis=0, keepdims=True)
    q = silu(q_ref[...])
    qd = q * jnp.exp(cm)
    kd = k * jnp.exp(-cm)
    rows = lax.broadcasted_iota(jnp.int32, (size, size), 0)
    cols = lax.broadcasted_iota(jnp.int32, (size, size), 1)
    scores = jnp.where((cols <= rows) & (sid_c == sid_r), dot_last(qd.astype(BF), kd.astype(BF)), 0.0)
    out_ref[...] = mm(scores.astype(BF), v_ref[...].astype(BF))
    qs_ref[...] = (q * jnp.exp(cm + mid) * inherit).astype(BF)


def chained(packs):
    total = packs[-1][0, :128].astype(F32)
    for p in packs[-2::-1]:
        total = p[0, :128].astype(F32) + p[0, 128:].astype(F32)[:1] * total
    return total


def mixed_kernel(hops, out_ref, qs_ref, g_ref, gain_ref, *rest):
    packs, (mixed_ref, on_ref, enter_ref) = rest[:hops], rest[hops:]
    enter = chained(packs)
    enter_ref[0] = enter
    mixed = out_ref[...] + dot_last(qs_ref[...], enter.astype(BF))
    mixed_ref[...] = mixed
    r = lax.rsqrt(jnp.mean(mixed * mixed, axis=-1, keepdims=True) + EPS)
    on_ref[...] = (mixed * r * gain_ref[...] * silu(g_ref[...])).astype(BF)


def norm_back_kernel(
    don_ref, g_ref, mixed_ref, qs_ref, gain_ref, pack_ref, dmix_ref, dg_ref, dpack_ref, dgain_ref
):
    don, gz, mixed, gain = don_ref[...], g_ref[...], mixed_ref[...], gain_ref[...]
    sg = sigmoid(gz)
    s = gz * sg
    r = lax.rsqrt(jnp.mean(mixed * mixed, axis=-1, keepdims=True) + EPS)
    n = mixed * r
    w = don * gain * s
    dmix = (r * (w - n * jnp.mean(w * n, axis=-1, keepdims=True))).astype(BF)
    dmix_ref[...] = dmix
    dg_ref[...] = (don * gain * n * (sg * (1.0 + gz * (1.0 - sg)))).astype(BF)
    dpack_ref[0, :128] = dot_first(dmix, qs_ref[...]).astype(BF)
    dpack_ref[0, 128:] = pack_ref[0, 128:]

    @pl.when((pl.program_id(0) == 0) & (pl.program_id(1) == 0))
    def _():
        dgain_ref[...] = jnp.zeros_like(dgain_ref)

    dgain_ref[...] += jnp.sum(don * s * n, axis=0, keepdims=True)


def back_kernel(count, hops, starts, q_ref, f_ref, v_ref, b_ref, dmix_ref, enter_ref, *rest):
    packs, (dq_ref, df_ref, dv_ref, db_ref) = rest[:hops], rest[hops:]
    size = f_ref.shape[0]
    slot = pl.program_id(1)
    sid_c, sid_r, inherit, same_last, keep = marks(starts, slot, size, count)
    bound = b_ref[...]
    sg, forget, k, a = gates(f_ref[...], bound)
    cm = split_dot(about_middle(size), a)
    last = cm[size - 1 :]
    mid = jnp.sum(a[: size // 2], axis=0, keepdims=True)
    qz = q_ref[...]
    sq = sigmoid(qz)
    up, down = jnp.exp(cm), jnp.exp(-cm)
    qd = (qz * sq * up).astype(BF)
    kd = (k * down).astype(BF)
    v = v_ref[...].astype(BF)
    dmix = dmix_ref[...]
    rows = lax.broadcasted_iota(jnp.int32, (size, size), 0)
    cols = lax.broadcasted_iota(jnp.int32, (size, size), 1)
    same = sid_c == sid_r
    allowed = (cols <= rows) & same
    scores = jnp.where(allowed, dot_last(qd, kd), 0.0).astype(BF)
    dscores = jnp.where(allowed, dot_last(dmix, v), 0.0).astype(BF)
    enter = enter_ref[0]
    leave = chained(packs)
    leave_low = (leave * jnp.exp(last)).astype(BF)
    enter_low = (enter * jnp.exp(mid)).astype(BF)
    dqd = mm(dscores, kd) + inherit * mm(dmix, enter_low)
    dkd_tail = same_last * mm(v, leave_low)
    dkd = dot_first(dscores, qd) + dkd_tail
    dv = dot_first(scores, dmix) + same_last * dot_last(kd, leave_low)
    qd, kd = qd.astype(F32), kd.astype(F32)
    dlog = dqd * qd - dkd * kd
    whole = jnp.sum(dkd_tail * kd, axis=0, keepdims=True) + keep * jnp.exp(mid + last) * jnp.sum(
        leave * enter, axis=0, keepdims=True
    )
    after = ((cols >= rows) & same).astype(BF)
    da = split_dot(after, dlog) + same_last * whole
    dforget = da / forget - dkd * down
    dq_ref[...] = (dqd * up * (sq * (1.0 + qz * (1.0 - sq)))).astype(BF)
    df_ref[...] = (dforget * (1.0 - bound) * sg * (1.0 - sg)).astype(BF)
    dv_ref[...] = dv.astype(BF)

    @pl.when(slot == 0)
    def _():
        db_ref[...] = jnp.zeros_like(db_ref)

    db_ref[0] += jnp.sum(dforget * (1.0 - sg), axis=0, keepdims=True)


def tile(size, base):
    return pl.BlockSpec((size, 128), lambda h, s, *_: (s, h + base))


def state(rows, heads):
    return pl.BlockSpec((1, rows, 128), lambda h, s, *_: (s * heads + h, 0, 0))


def per_head():
    return pl.BlockSpec((1, 128), lambda h, s, *_: (0, h))


def fixed():
    return pl.BlockSpec((1, 128), lambda h, s, *_: (0, 0))


def call(kernel, grid, scalars, in_specs, out_specs, out_shape, args):
    params = pltpu.CompilerParams(vmem_limit_bytes=48 * 1024 * 1024)
    return pl.pallas_call(
        kernel,
        grid_spec=pltpu.PrefetchScalarGridSpec(
            num_scalar_prefetch=len(scalars), grid=grid, in_specs=in_specs, out_specs=out_specs
        ),
        out_shape=out_shape,
        compiler_params=params,
    )(*scalars, *args)


def reached(pack, forward, tokens):
    count = lax.axis_size("seq")
    if count * tokens == 2 * MIN_LEN and MIN_LEN % tokens == 0:
        span = MIN_LEN // tokens
        out = []
        for hop in range(1, span):
            pairs = [(s, s + hop) for s in range(count) if s // span == (s + hop) // span]
            if not forward:
                pairs = [(b, a) for a, b in pairs]
            out.append(lax.ppermute(pack, "seq", pairs))
        return out
    place = lax.axis_index("seq")
    every = lax.all_gather(pack, "seq")
    shape = (pack.shape[0], 128, pack.shape[2])

    def one(k, total):
        at = k if forward else count - 1 - k
        there = lax.dynamic_index_in_dim(every, at, 0, False).astype(F32)
        new = there[:, :128] + there[:, 128:129] * total
        return jnp.where((at < place) if forward else (at > place), new, total)

    total = lax.fori_loop(0, count, one, jnp.zeros(shape, F32))
    return [jnp.concatenate([total, jnp.zeros_like(total[:, :16])], axis=1).astype(BF)]


def shards(
    block_input,
    lengths,
    norm_gain,
    w_q,
    w_f,
    w_i,
    w_g,
    lower_bound,
    group_gain,
    w_o,
    ffn_norm_gain,
    w_gate,
    w_up,
    w_down,
    out_grad,
):
    tokens, width = block_input.shape
    head_dim = group_gain.shape[0]
    heads = width // head_dim // 4
    mine = heads * head_dim
    seqs = lax.axis_size("seq")
    dp = lax.axis_index("dp")
    low_bit, high_bit = dp & 1, dp >> 1

    def of_heads(value, axis):
        shape = value.shape
        cut = value.reshape(shape[:axis] + (2, heads, 2, head_dim) + shape[axis + 1 :])
        cut = lax.dynamic_index_in_dim(cut, high_bit, axis + 2, False)
        cut = lax.dynamic_index_in_dim(cut, low_bit, axis, False)
        return cut.reshape(shape[:axis] + (mine,) + shape[axis + 1 :])

    def to_heads(blocks, axis):
        a, b, c, d = absolute(blocks)
        shape = a.shape
        cut = [v.reshape(shape[:axis] + (heads, head_dim) + shape[axis + 1 :]) for v in (a, b, c, d)]
        pair = [jnp.stack([cut[k], cut[k + 2]], axis=axis + 1) for k in range(2)]
        full = jnp.stack(pair, axis=axis)
        return full.reshape(shape[:axis] + (4 * mine,) + shape[axis + 1 :])

    chunk = w_down.shape[0] // 4
    ff = chunk * seqs

    def of_hidden(value):
        cut = value.reshape(value.shape[0], seqs, 4, chunk)
        return lax.dynamic_index_in_dim(cut, dp, 2, False).reshape(value.shape[0], ff)

    def to_hidden(blocks):
        cut = [v.reshape(v.shape[0], seqs, 1, chunk) for v in absolute(blocks)]
        return jnp.concatenate(cut, axis=2).reshape(blocks[0].shape[0], 4 * ff)

    def gather_seq(value):
        return lax.all_gather(value, "seq", axis=0, tiled=True)

    def scatter_seq(value):
        return lax.psum_scatter(value.astype(BF), "seq", scatter_dimension=0, tiled=True)

    def blocks_dp(value):
        rows = value.shape[0]
        full = gather_dp(value)
        return [full[k * rows : (k + 1) * rows] for k in range(4)]

    wfv = gather_seq(jnp.concatenate([of_heads(w_f, 1), of_heads(w_i, 1)], axis=1))
    wqg = gather_seq(jnp.concatenate([of_heads(w_q, 1), of_heads(w_g, 1)], axis=1))
    natural = w_o.shape[0] == 2 * head_dim
    if natural:
        part = lax.dynamic_slice_in_dim(w_o, high_bit * head_dim, head_dim, 0)
        wo = lax.dynamic_slice_in_dim(gather_seq(part), low_bit * mine, mine, 0)
    else:
        wo = of_heads(gather_seq(w_o), 0)
    wgu = gather_seq(jnp.concatenate([of_hidden(w_gate), of_hidden(w_up)], axis=1))
    wd = gather_seq(lax.dynamic_slice_in_dim(w_down, dp * chunk, chunk, 0))

    x = block_input.astype(F32)
    r1 = lax.rsqrt(jnp.mean(x * x, axis=-1, keepdims=True) + EPS)
    h = (x * r1 * norm_gain).astype(BF)
    h_all = gather_dp(h)

    starts = jnp.cumsum(lengths[0]) - lengths[0] - lax.axis_index("seq") * tokens
    starts = jnp.stack([starts] + [swap(starts, k) for k in (1, 2, 3)])
    count = lengths.shape[1]
    bound = of_heads(lower_bound, 0)[None]
    gain = group_gain[None]

    zfv = mm(h_all, wfv)
    zqg = mm(h_all, wqg)
    og_all = gather_dp(out_grad)

    grid = (heads, 4)
    pairs = heads * 4
    rows = 4 * tokens
    wide = jax.ShapeDtypeStruct((rows, mine), F32)
    thin = jax.ShapeDtypeStruct((rows, mine), BF)
    packed = jax.ShapeDtypeStruct((pairs, 144, 128), BF)
    ql, fl, vl, gl = tile(tokens, 0), tile(tokens, 0), tile(tokens, heads), tile(tokens, heads)
    plain = tile(tokens, 0)
    pack_spec, state_spec = state(144, heads), state(128, heads)

    pack = call(
        functools.partial(end_kernel, count), grid, (starts,),
        [fl, vl, per_head()], pack_spec, packed, (zfv, zfv, bound),
    )
    before = reached(pack, True, tokens)
    intra, qs = call(
        functools.partial(intra_kernel, count), grid, (starts,),
        [ql, fl, vl, per_head()], [plain, plain], [wide, thin], (zqg, zfv, zfv, bound),
    )
    mixed, on, enter = call(
        functools.partial(mixed_kernel, len(before)), grid, (),
        [plain, plain, gl, fixed()] + [pack_spec] * len(before),
        [plain, plain, state_spec],
        [wide, thin, jax.ShapeDtypeStruct((pairs, 128, 128), F32)],
        (intra, qs, zqg, gain, *before),
    )

    y = x + scatter_dp(mm(on, wo, BF))
    r2 = lax.rsqrt(jnp.mean(y * y, axis=-1, keepdims=True) + EPS)
    h2_all = gather_dp((y * r2 * ffn_norm_gain).astype(BF))

    gu = mm(h2_all, wgu)
    gate, upper = gu[:, :ff], gu[:, ff:]
    hidden = (silu(gate) * upper).astype(BF)
    d_hidden = dot_last(og_all, wd)
    d_gate = (d_hidden * upper * silu_grad(gate)).astype(BF)
    d_upper = (d_hidden * silu(gate)).astype(BF)
    d_gu = jnp.concatenate([d_gate, d_upper], axis=1)
    d_h2 = scatter_dp(dot_last(d_gu, wgu, BF))
    result = (y + scatter_dp(mm(hidden, wd, BF))).astype(BF)

    down_rows = scatter_seq(dot_first(hidden, og_all, BF))
    gate_rows = scatter_seq(dot_first(h2_all, d_gate, BF))
    up_rows = scatter_seq(dot_first(h2_all, d_upper, BF))

    og = out_grad.astype(F32)
    d_ffn_gain = jnp.sum(d_h2 * y * r2, axis=0)
    u2 = d_h2 * ffn_norm_gain
    d_y = og + r2 * u2 - y * (r2 * r2 * r2) * jnp.mean(u2 * y, axis=-1, keepdims=True)
    d_branch = gather_dp(d_y.astype(BF))

    d_on = dot_last(d_branch, wo)
    d_mixed, d_gz, d_pack, d_gain = call(
        norm_back_kernel, grid, (),
        [plain, gl, plain, plain, fixed(), pack_spec],
        [plain, plain, pack_spec, fixed()],
        [thin, thin, packed, jax.ShapeDtypeStruct((1, 128), F32)],
        (d_on, zqg, mixed, qs, gain, pack),
    )
    after = reached(d_pack, False, tokens)
    d_qz, d_fz, d_vz, d_bound = call(
        functools.partial(back_kernel, count, len(after)), grid, (starts,),
        [ql, fl, vl, per_head(), plain, state_spec] + [pack_spec] * len(after),
        [plain, plain, plain, pl.BlockSpec((1, 1, 128), lambda h, s, *_: (h, 0, 0))],
        [thin, thin, thin, jax.ShapeDtypeStruct((heads, 1, 128), F32)],
        (zqg, zfv, zfv, bound, d_mixed, enter, *after),
    )

    d_fv = jnp.concatenate([d_fz, d_vz], axis=1)
    d_qg = jnp.concatenate([d_qz, d_gz], axis=1)
    d_h = scatter_dp((dot_last(d_fv, wfv) + dot_last(d_qg, wqg)).astype(BF))

    o_part = dot_first(on, d_branch, BF)
    if natural:
        none = jnp.zeros_like(o_part)
        o_full = jnp.where(
            low_bit == 0,
            jnp.concatenate([o_part, none], axis=0),
            jnp.concatenate([none, o_part], axis=0),
        )
        o_rows = scatter_seq(o_full)
        o_mine = o_rows + swap(o_rows, 1)
        o_other = swap(o_mine, 2)
        grad_o = jnp.where(
            high_bit == 0,
            jnp.concatenate([o_mine, o_other], axis=0),
            jnp.concatenate([o_other, o_mine], axis=0),
        ).astype(F32)
    else:
        none = jnp.zeros_like(o_part)
        o_full = to_heads([o_part, none, none, none], 0)
        grad_o = lax.psum(scatter_seq(o_full).astype(F32), "dp")

    grad_down = jnp.concatenate(absolute(blocks_dp(down_rows)), axis=0).astype(F32)
    grad_gate = to_hidden(blocks_dp(gate_rows)).astype(F32)
    grad_up = to_hidden(blocks_dp(up_rows)).astype(F32)

    def head_grad(value):
        return to_heads(blocks_dp(scatter_seq(dot_first(h_all, value, BF))), 1).astype(F32)

    grad_g = head_grad(d_gz)
    grad_f = head_grad(d_fz)
    grad_i = head_grad(d_vz)
    grad_q = head_grad(d_qz)

    d_norm_gain = jnp.sum(d_h * x * r1, axis=0)
    u1 = d_h * norm_gain
    d_x = d_y + r1 * u1 - x * (r1 * r1 * r1) * jnp.mean(u1 * x, axis=-1, keepdims=True)

    zero = jnp.zeros((mine,), F32)
    d_bound = to_heads([d_bound.reshape(mine), zero, zero, zero], 0)
    small = lax.psum((d_norm_gain, d_ffn_gain, d_gain[0], d_bound), ("dp", "seq"))
    return (
        result,
        d_x.astype(BF),
        small[0],
        grad_q,
        grad_f,
        grad_i,
        grad_g,
        small[3],
        small[2],
        grad_o,
        small[1],
        grad_gate,
        grad_up,
        grad_down,
    )


def solution(mesh):
    both = P(("dp", "seq"), None)
    rows = P("seq", None)
    return jax.shard_map(
        shards,
        mesh=mesh,
        in_specs=(
            both, P("dp", None), P(), rows, rows, rows, rows, P(), P(), rows, P(), rows, rows, rows, both,
        ),
        out_specs=(
            both, both, P(), rows, rows, rows, rows, P(), P(), rows, P(), rows, rows, rows,
        ),
        check_vma=False,
    )
```

time: 2740 us -> 1050 us (0.38)
  waiting for transfers between devices: 2080 us -> 461 us
  matrix products: 303 us -> 154 us
  starting transfers between devices: 1.44 us -> 101 us
  Pallas kernels: 0 us -> 67.8 us
  other arithmetic: 126 us -> 61.8 us
    all_gather x10 -> x5, waiting for transfers between devices: 985 us -> 57.4 us  [gather_seq(): return lax.all_gather(value, 'seq', axis=0, tiled=True)]
    reduce_scatter x8, waiting for transfers between devices: 896 us -> 148 us  [scatter_seq(): lax.psum_scatter(value.astype(BF), 'seq', scatter_dimension=0, tiled=True)]
    ppermute x0 -> x79, waiting for transfers between devices: none -> 255 us  [the longest x73 206 us: swap(): return lax.ppermute(value, 'dp', [(s, s ^ bits) for s in range(count)])]
    psum x1 -> x0, waiting for transfers between devices: 194 us -> none  [shards(): lax.psum(mixer_rows[0].astype(jnp.bfloat16), 'dp').astype(jnp.float32)]
    dot_general x37 -> x5, matrix products: 163 us -> 47.6 us  [mm(): return jnp.dot(left, right, preferred_element_type=F32).astype(kind)]
    ppermute x0 -> x79, starting transfers between devices: none -> 100 us  [the longest x73 89.5 us: swap(): return lax.ppermute(value, 'dp', [(s, s ^ bits) for s in range(count)])]
    pallas_call x0 -> x5, Pallas kernels: none -> 67.8 us  [call(): pl.pallas_call(kernel, grid_spec=pltpu.PrefetchScalarGridSpec(num_scalar_...]
    dynamic_update_slice x4 -> x0, local copies, waits for them, and re-layouts: 54.6 us -> none  [mixer_local(): lax.scan(jax.checkpoint(span_step), start_carry, blocks)]
  transfers between devices with their start and end apart: 19 -> 92, of which waited for: 17 -> 46; matrix products, arithmetic and copies ran while one was open for 14% -> 27% of each run, Pallas kernels for 0% -> 5%
where the time goes in v1:
time: 1050 us; the launch traced here: 1040 us
  waiting for transfers between devices  461 us (44%)
  matrix products  154 us (15%)
  local copies, waits for them, and re-layouts  133 us (13%)
  starting transfers between devices  101 us (10%)
  Pallas kernels  67.8 us (6%)
  other arithmetic  61.8 us (6%)
  blocking collectives  47.4 us (5%)
  between operations  15.8 us (2%)
    ppermute x73, waiting for transfers between devices, swap(): return lax.ppermute(value, 'dp', [(s, s ^ bits) for s in range(count)])  206 us
    reduce_scatter x8, waiting for transfers between devices, scatter_seq(): lax.psum_scatter(value.astype(BF), 'seq', scatter_dimension=0, tiled=True)  148 us
    ppermute x73, starting transfers between devices, swap(): return lax.ppermute(value, 'dp', [(s, s ^ bits) for s in range(count)])  89.5 us
    unnamed x150, local copies, waits for them, and re-layouts  69.1 us
    pallas_call x5, Pallas kernels, call(): pl.pallas_call(kernel, grid_spec=pltpu.PrefetchScalarGridSpec(num_scalar_...  67.8 us
    all_gather x5, waiting for transfers between devices, gather_seq(): return lax.all_gather(value, 'seq', axis=0, tiled=True)  57.4 us
    dot_general x8, matrix products, dot_first(): lax.dot_general(left, right, (((0,), (0,)), ((), ())), preferred_element_...  56.5 us
    dot_general x5, matrix products, dot_last(): lax.dot_general(left, right, (((1,), (1,)), ((), ())), preferred_element_...  49.5 us
  transfers between devices with their start and end apart: 92, of which 46 were waited for; matrix products, arithmetic and copies ran while one was open for 27% of the time, Pallas kernels for 5%

profile of v1, /device:TPU:0, one launch (start us, length us, event | category | flops | bytes accessed | tf_op | source)
XLA Modules:
  0.0 1041.8 jit_solution(15576773419341907575)
XLA Ops:
  49.0 16.6 %collective-permute-done.3 = bf16[256,2048]{1,0:T(8,128)(2,1)} collective-permute-done((bf16[256,2048]{1,0:T(8,128)(2,1)}, bf16[256,2048]{1,0:T(8,128)(2,1)}, u32[]{:S(2)}, u32[]{:S(2)}) %collective-permute-start.3) | collective-permute-done | bytes 1048608 | tf_op jit(solution)/shard_map/ppermute | solution.py:47
  90.7 8.9 shard_map.255.pack_ref
  113.4 10.0 fusion.41.q_ref.g_ref
  123.5 15.2 %shard_map.254 = (f32[1024,512]{1,0:T(8,128)S(1)}, bf16[1024,512]{1,0:T(8,128)(2,1)S(1)}) custom-call(s32[4,2]{1,0:T(4,128)S(1)} %pad_add_fusion.starts, f32[1024,1024]{1,0:T(8,128)} %fusion.41.q_ref.g_ref, f32[1024,1024]{1,0:T(8,128)} %copy-done.2, f32[1024,1024]{1,0:T(8,128)} %copy-done.2, f32[1,512]{1,0:T(1,128)S(1)} %fusion.30.b_ref), custom_call_target="tpu_custom_call" | custom-call | tf_op jit(solution)/shard_map/pallas_call | solution.py:260
  144.8 11.5 %shard_map.256 = (f32[1024,512]{1,0:T(8,128)}, bf16[1024,512]{1,0:T(8,128)(2,1)S(1)}, f32[16,128,128]{2,1,0:T(8,128)S(1)}) custom-call(f32[1024,512]{1,0:T(8,128)} %copy-done.3, bf16[1024,512]{1,0:T(8,128)(2,1)S(1)} %get-tuple-element.28.qs_ref, f32[1024,1024]{1,0:T(8,128)} %fusion.41.q_ref.g_ref, f32[1,128]{1,0:T(1,128)S(1)} %bitcast.113, ...), custom_call_target="tpu_custom_call" | custom-call | tf_op jit(solution)/shard_map/pallas_call | solution.py:260
  158.3 9.7 all-gather.10.cloned.1.call-done
  176.6 10.7 %collective-permute-done.11 = bf16[128,2048]{1,0:T(8,128)(2,1)S(1)} collective-permute-done((bf16[128,2048]{1,0:T(8,128)(2,1)S(1)}, bf16[128,2048]{1,0:T(8,128)(2,1)S(1)}, u32[]{:S(2)}, u32[]{:S(2)}) %collective-permute-start.11) | collective-permute-done | bytes 524320 | tf_op jit(solution)/shard_map/ppermute | solution.py:47
  198.7 11.1 %collective-permute-done.14 = bf16[128,2048]{1,0:T(8,128)(2,1)S(1)} collective-permute-done((bf16[128,2048]{1,0:T(8,128)(2,1)S(1)}, bf16[128,2048]{1,0:T(8,128)(2,1)S(1)}, u32[]{:S(2)}, u32[]{:S(2)}) %collective-permute-start.14) | collective-permute-done | bytes 524320 | tf_op jit(solution)/shard_map/ppermute | solution.py:47
  213.8 18.6 %collective-permute-done.26 = bf16[256,2048]{1,0:T(8,128)(2,1)S(1)} collective-permute-done((bf16[256,2048]{1,0:T(8,128)(2,1)S(1)}, bf16[256,2048]{1,0:T(8,128)(2,1)S(1)}, u32[]{:S(2)}, u32[]{:S(2)}) %collective-permute-start.26) | collective-permute-done | bytes 1048608 | tf_op jit(solution)/shard_map/ppermute | solution.py:47
  236.4 11.0 %collective-permute-done.28 = bf16[128,2048]{1,0:T(8,128)(2,1)S(1)} collective-permute-done((bf16[128,2048]{1,0:T(8,128)(2,1)S(1)}, bf16[128,2048]{1,0:T(8,128)(2,1)S(1)}, u32[]{:S(2)}, u32[]{:S(2)}) %collective-permute-start.28) | collective-permute-done | bytes 524320 | tf_op jit(solution)/shard_map/ppermute | solution.py:47
  256.9 8.3 collective-permute-done.29
  281.3 18.9 %fusion.43 = f32[1024,2816]{1,0:T(8,128)} fusion(bf16[1024,2048]{1,0:T(8,128)(2,1)} %constant_dynamic-update-slice_fusion.5, bf16[2048,2816]{0,1:T(8,128)(2,1)} %all-gather.12.cloned.1.call-done), kind=kOutput, calls=%fused_computation.214 | convolution fusion | flops 11811160064 | bytes 27262976 | tf_op jit(solution)/shard_map/dot_general | solution.py:30
  300.2 40.8 %all-gather.14.cloned.1.call-done = bf16[1408,2048]{1,0:T(8,128)(2,1)} async-done(((bf16[176,2048]{1,0:T(8,128)(2,1)}), bf16[1408,2048]{1,0:T(8,128)(2,1)}) %all-gather.14.cloned.1.call-update) | async-done | bytes 5767184 | tf_op jit(solution)/shard_map/all_gather | solution.py:347
  341.0 16.4 %multiply_convert_fusion.1 = (bf16[1024,1408]{1,0:T(8,128)(2,1)}, bf16[1024,1408]{1,0:T(8,128)(2,1)S(1)}, bf16[1024,1408]{1,0:T(8,128)(2,1)S(1)}) fusion(f32[1024,2816]{1,0:T(8,128)} %fusion.43, bf16[1024,2048]{1,0:T(8,128)(2,1)} %copy-done.43, bf16[1408,2048]{1,0:T(8,128)(2,1)} %all-gather.14.cloned.1.call-done), kind=kOutput, calls=%fused_computation.9 | convolution fusion | flops 5927206912 | bytes 30146560 | tf_op jit(solution)/shard_map/dot_general | solution.py:40
  357.4 17.9 %fusion.5 = bf16[1024,2048]{1,0:T(8,128)(2,1)S(1)} fusion(bf16[2048,2816]{0,1:T(8,128)(2,1)} %all-gather.12.cloned.1.call-done, bf16[1024,1408]{1,0:T(8,128)(2,1)S(1)} %get-tuple-element.114, bf16[1024,1408]{1,0:T(8,128)(2,1)} %get-tuple-element.113), kind=kOutput, calls=%fused_computation.20 | convolution fusion | flops 11824791552 | bytes 21495808 | tf_op jit(solution)/shard_map/dot_general | solution.py:40
  393.6 9.4 collective-permute-done.23
  415.7 8.3 collective-permute-done.25
  425.5 9.7 collective-permute-done.34
  436.8 9.0 collective-permute-done.24
  453.6 22.1 %collective-permute-done.36 = bf16[256,2048]{1,0:T(8,128)(2,1)S(1)} collective-permute-done((bf16[256,2048]{1,0:T(8,128)(2,1)S(1)}, bf16[256,2048]{1,0:T(8,128)(2,1)S(1)}, u32[]{:S(2)}, u32[]{:S(2)}) %collective-permute-start.36) | collective-permute-done | bytes 1048608 | tf_op jit(solution)/shard_map/ppermute | solution.py:47
  478.2 9.9 collective-permute-done.38
  492.6 12.8 %shard_map.257 = (bf16[1024,512]{1,0:T(8,128)(2,1)S(1)}, bf16[1024,512]{1,0:T(8,128)(2,1)S(1)}, bf16[16,144,128]{2,1,0:T(8,128)(2,1)S(1)}, f32[1,128]{1,0:T(1,128)S(1)}) custom-call(f32[1024,512]{1,0:T(8,128)} %fusion.24.don_ref, f32[1024,1024]{1,0:T(8,128)} %fusion.41.q_ref.g_ref, f32[1024,512]{1,0:T(8,128)} %get-tuple-element.30.mixed_ref, ...), custom_call_target="tpu_custom_call" | custom-call | tf_op jit(solution)/shard_map/pallas_call | solution.py:260
  514.0 38.0 %collective-permute-done.41.rest_1_ = bf16[16,144,128]{2,1,0:T(8,128)(2,1)S(1)} collective-permute-done((bf16[16,144,128]{2,1,0:T(8,128)(2,1)S(1)}, bf16[16,144,128]{2,1,0:T(8,128)(2,1)S(1)}, u32[]{:S(2)}, u32[]{:S(2)}) %collective-permute-start.41) | collective-permute-done | bytes 589856 | tf_op jit(solution)/shard_map/ppermute | solution.py:279
  558.0 19.4 %shard_map.258 = (bf16[1024,512]{1,0:T(8,128)(2,1)S(1)}, bf16[1024,512]{1,0:T(8,128)(2,1)S(1)}, bf16[1024,512]{1,0:T(8,128)(2,1)S(1)}, f32[4,1,128]{2,1,0:T(1,128)S(1)}) custom-call(s32[4,2]{1,0:T(4,128)S(1)} %pad_add_fusion.starts, f32[1024,1024]{1,0:T(8,128)} %fusion.41.q_ref.g_ref, f32[1024,1024]{1,0:T(8,128)} %copy-done.2, f32[1024,1024]{1,0:T(8,128)} %copy-done.2, ...), custom_call_target="tpu_custom_call" | custom-call | tf_op jit(solution)/shard_map/pallas_call | solution.py:260
  603.5 11.1 %convolution_convert_fusion.2 = bf16[2048,1408]{1,0:T(8,128)(2,1)} fusion(bf16[1024,2048]{1,0:T(8,128)(2,1)} %constant_dynamic-update-slice_fusion.5, bf16[1024,1408]{1,0:T(8,128)(2,1)} %get-tuple-element.113), kind=kOutput, calls=%fused_computation.3 | convolution fusion | flops 5908463616 | bytes 12845056 | tf_op jit(solution)/shard_map/dot_general | solution.py:34
  614.8 11.1 %convolution_convert_fusion.1 = bf16[2048,1408]{1,0:T(8,128)(2,1)} fusion(bf16[1024,2048]{1,0:T(8,128)(2,1)} %constant_dynamic-update-slice_fusion.5, bf16[1024,1408]{1,0:T(8,128)(2,1)} %copy-done.56), kind=kOutput, calls=%fused_computation.2 | convolution fusion | flops 5908463616 | bytes 12845056 | tf_op jit(solution)/shard_map/dot_general | solution.py:34
  625.9 10.5 %convolution_convert_fusion = bf16[1408,2048]{1,0:T(8,128)(2,1)} fusion(bf16[1024,1408]{1,0:T(8,128)(2,1)} %copy-done.55, bf16[1024,2048]{1,0:T(8,128)(2,1)} %copy-done.43), kind=kOutput, calls=%fused_computation.1 | convolution fusion | flops 5908463616 | bytes 12845056 | tf_op jit(solution)/shard_map/dot_general | solution.py:34
  656.6 8.5 collective-permute-done.44
  690.0 47.4 %all-reduce.2 = (f32[2048]{0:T(1024)}, f32[2048]{0:T(1024)}, f32[128]{0:T(128)}, f32[2048]{0:T(1024)}) all-reduce(f32[2048]{0:T(1024)S(1)} %get-tuple-element.98, f32[2048]{0:T(1024)S(1)} %bitcast.158, f32[128]{0:T(128)S(1)} %bitcast.115, f32[2048]{0:T(1024)S(1)} %get-tuple-element.96), channel_id=1, replica_groups=mesh['dp'=4,'seq'=8] {'dp','seq'}, use_global_device_ids=true, to_apply=%region_6.7 | all-reduce | flops 6272 | bytes 50176 | tf_op jit(solution)/shard_map/psum | solution.py:494
  775.6 35.2 %reduce-scatter.19.cloned.1.call-done = bf16[256,1408]{1,0:T(8,128)(2,1)} async-done(((bf16[2048,1408]{1,0:T(8,128)(2,1)}), bf16[256,1408]{1,0:T(8,128)(2,1)}) %reduce-scatter.19.cloned.1.call-update) | async-done | bytes 720912 | tf_op jit(solution)/shard_map/reduce_scatter | solution.py:350
  824.7 52.0 %reduce-scatter.21.cloned.1.call-done = bf16[256,1408]{1,0:T(8,128)(2,1)} async-done(((bf16[2048,1408]{1,0:T(8,128)(2,1)}), bf16[256,1408]{1,0:T(8,128)(2,1)}) %reduce-scatter.21.cloned.1.call-update) | async-done | bytes 720912 | tf_op jit(solution)/shard_map/reduce_scatter | solution.py:350
  881.8 61.1 %reduce-scatter.23.cloned.1.call-done = bf16[176,2048]{1,0:T(8,128)(2,1)} async-done(((bf16[1408,2048]{1,0:T(8,128)(2,1)}), bf16[176,2048]{1,0:T(8,128)(2,1)}) %reduce-scatter.23.cloned.1.call-update) | async-done | bytes 720912 | tf_op jit(solution)/shard_map/reduce_scatter | solution.py:350
  (481 shorter events, 424.9 us)
Async XLA Ops:
  7.2 75.8 %all-gather.8.cloned.1.call-start = ((), (), s32[]{:S(2)}) async-start(), calls=%async_computation.9 | async-start | bytes 4718592 | tf_op jit(solution)/shard_map/all_gather | solution.py:347
  13.8 99.6 %all-gather.6.cloned.1.call-start = ((), (), s32[]{:S(2)}) async-start(), calls=%async_computation.8 | async-start | bytes 4718592 | tf_op jit(solution)/shard_map/all_gather | solution.py:347
  20.3 147.6 %all-gather.10.cloned.1.call-start = ((), (), s32[]{:S(2)}) async-start(), calls=%async_computation.10 | async-start | bytes 4718592 | tf_op jit(solution)/shard_map/all_gather | solution.py:347
  22.3 259.0 %all-gather.12.cloned.1.call-start = ((), (), s32[]{:S(2)}) async-start(), calls=%async_computation.11 | async-start | bytes 12976128 | tf_op jit(solution)/shard_map/all_gather | solution.py:347
  34.3 306.7 %all-gather.14.cloned.1.call-start = ((), (), s32[]{:S(2)}) async-start(), calls=%async_computation.12 | async-start | bytes 6488064 | tf_op jit(solution)/shard_map/all_gather | solution.py:347
  48.3 622.8 %reduce-scatter.15.cloned.1.call-start = ((), (), s32[]{:S(2)}) async-start(), calls=%async_computation.16 | async-start | bytes 2359296 | tf_op jit(solution)/shard_map/reduce_scatter | solution.py:350
  99.6 40.4 %collective-permute-start.7 = (bf16[16,144,128]{2,1,0:T(8,128)(2,1)S(1)}, bf16[16,144,128]{2,1,0:T(8,128)(2,1)S(1)}, u32[]{:S(2)}, u32[]{:S(2)}) collective-permute-start(bf16[16,144,128]{2,1,0:T(8,128)(2,1)S(1)} %shard_map.255.pack_ref), channel_id=1, source_target_pairs={{0,1},{1,2},{2,3},{4,5},{5,6},{6,7},{8,9},{9,10},{10,11},{12,13},{... | collective-permute-start | bytes 1769480 | tf_op jit(solution)/shard_map/ppermute | solution.py:279
  100.9 39.0 %collective-permute-start.8 = (bf16[16,144,128]{2,1,0:T(8,128)(2,1)S(1)}, bf16[16,144,128]{2,1,0:T(8,128)(2,1)S(1)}, u32[]{:S(2)}, u32[]{:S(2)}) collective-permute-start(bf16[16,144,128]{2,1,0:T(8,128)(2,1)S(1)} %shard_map.255.pack_ref), channel_id=1, source_target_pairs={{0,2},{1,3},{4,6},{5,7},{8,10},{9,11},{12,14},{13,15},{16,18},{17,... | collective-permute-start | bytes 1769480 | tf_op jit(solution)/shard_map/ppermute | solution.py:279
  105.2 39.6 %collective-permute-start.9 = (bf16[16,144,128]{2,1,0:T(8,128)(2,1)S(1)}, bf16[16,144,128]{2,1,0:T(8,128)(2,1)S(1)}, u32[]{:S(2)}, u32[]{:S(2)}) collective-permute-start(bf16[16,144,128]{2,1,0:T(8,128)(2,1)S(1)} %shard_map.255.pack_ref), channel_id=1, source_target_pairs={{0,3},{4,7},{8,11},{12,15},{16,19},{20,23},{24,27},{28,31}} | collective-permute-start | bytes 1769480 | tf_op jit(solution)/shard_map/ppermute | solution.py:279
  190.0 42.5 %collective-permute-start.26 = (bf16[256,2048]{1,0:T(8,128)(2,1)S(1)}, bf16[256,2048]{1,0:T(8,128)(2,1)S(1)}, u32[]{:S(2)}, u32[]{:S(2)}) collective-permute-start(bf16[256,2048]{1,0:T(8,128)(2,1)S(1)} %copy-done.23), channel_id=1, source_target_pairs={{0,8},{8,0},{16,24},{24,16},{1,9},{9,1},{17,25},{25,17},{2,10},{10... | collective-permute-start | bytes 3145736 | tf_op jit(solution)/shard_map/ppermute | solution.py:47
  198.6 36.0 %collective-permute-start.27 = (bf16[256,2048]{1,0:T(8,128)(2,1)S(1)}, bf16[256,2048]{1,0:T(8,128)(2,1)S(1)}, u32[]{:S(2)}, u32[]{:S(2)}) collective-permute-start(bf16[256,2048]{1,0:T(8,128)(2,1)S(1)} %copy-done.23), channel_id=1, source_target_pairs={{0,16},{8,24},{16,0},{24,8},{1,17},{9,25},{17,1},{25,9},{2,18},{10... | collective-permute-start | bytes 3145736 | tf_op jit(solution)/shard_map/ppermute | solution.py:47
  212.3 42.6 %collective-permute-start.16 = (bf16[256,2048]{1,0:T(8,128)(2,1)S(1)}, bf16[256,2048]{1,0:T(8,128)(2,1)S(1)}, u32[]{:S(2)}, u32[]{:S(2)}) collective-permute-start(bf16[256,2048]{1,0:T(8,128)(2,1)S(1)} %get-tuple-element.108), channel_id=1, source_target_pairs={{0,8},{8,0},{16,24},{24,16},{1,9},{9,1},{17,25},{25,17},{2,10},{10... | collective-permute-start | bytes 3145736 | tf_op jit(solution)/shard_map/ppermute | solution.py:47
  510.0 228.3 %reduce-scatter.9.cloned.1.call-start = ((), (), s32[]{:S(2)}) async-start(), calls=%async_computation.13 | async-start | bytes 2359296 | tf_op jit(solution)/shard_map/reduce_scatter | solution.py:350
  511.4 40.6 %collective-permute-start.41 = (bf16[16,144,128]{2,1,0:T(8,128)(2,1)S(1)}, bf16[16,144,128]{2,1,0:T(8,128)(2,1)S(1)}, u32[]{:S(2)}, u32[]{:S(2)}) collective-permute-start(bf16[16,144,128]{2,1,0:T(8,128)(2,1)S(1)} %get-tuple-element.33), channel_id=1, source_target_pairs={{2,0},{3,1},{6,4},{7,5},{10,8},{11,9},{14,12},{15,13},{18,16},{19,... | collective-permute-start | bytes 1769480 | tf_op jit(solution)/shard_map/ppermute | solution.py:279
  512.7 45.3 %collective-permute-start.42 = (bf16[16,144,128]{2,1,0:T(8,128)(2,1)S(1)}, bf16[16,144,128]{2,1,0:T(8,128)(2,1)S(1)}, u32[]{:S(2)}, u32[]{:S(2)}) collective-permute-start(bf16[16,144,128]{2,1,0:T(8,128)(2,1)S(1)} %get-tuple-element.33), channel_id=1, source_target_pairs={{3,0},{7,4},{11,8},{15,12},{19,16},{23,20},{27,24},{31,28}} | collective-permute-start | bytes 1769480 | tf_op jit(solution)/shard_map/ppermute | solution.py:279
  583.1 158.8 %reduce-scatter.11.cloned.1.call-start = ((), (), s32[]{:S(2)}) async-start(), calls=%async_computation.14 | async-start | bytes 2359296 | tf_op jit(solution)/shard_map/reduce_scatter | solution.py:350
  589.6 156.0 %reduce-scatter.13.cloned.1.call-start = ((), (), s32[]{:S(2)}) async-start(), calls=%async_computation.15 | async-start | bytes 2359296 | tf_op jit(solution)/shard_map/reduce_scatter | solution.py:350
  595.6 175.8 %reduce-scatter.17.cloned.1.call-start = ((), (), s32[]{:S(2)}) async-start(), calls=%async_computation.17 | async-start | bytes 4718592 | tf_op jit(solution)/shard_map/reduce_scatter | solution.py:350
  603.5 207.3 %reduce-scatter.19.cloned.1.call-start = ((), (), s32[]{:S(2)}) async-start(), calls=%async_computation.18 | async-start | bytes 6488064 | tf_op jit(solution)/shard_map/reduce_scatter | solution.py:350
  614.6 262.1 %reduce-scatter.21.cloned.1.call-start = ((), (), s32[]{:S(2)}) async-start(), calls=%async_computation.19 | async-start | bytes 6488064 | tf_op jit(solution)/shard_map/reduce_scatter | solution.py:350
  625.9 317.0 %reduce-scatter.23.cloned.1.call-start = ((), (), s32[]{:S(2)}) async-start(), calls=%async_computation.20 | async-start | bytes 6488064 | tf_op jit(solution)/shard_map/reduce_scatter | solution.py:350
  682.3 55.1 %collective-permute-start.62 = (bf16[128,512]{1,0:T(8,128)(2,1)S(1)}, bf16[128,512]{1,0:T(8,128)(2,1)S(1)}, u32[]{:S(2)}, u32[]{:S(2)}) collective-permute-start(bf16[128,512]{1,0:T(8,128)(2,1)S(1)} %slice.288), channel_id=1, source_target_pairs={{0,16},{8,24},{16,0},{24,8},{1,17},{9,25},{17,1},{25,9},{2,18},{10... | collective-permute-start | bytes 393224 | tf_op jit(solution)/shard_map/ppermute | solution.py:47
  685.0 52.4 %collective-permute-start.64 = (bf16[128,512]{1,0:T(8,128)(2,1)}, bf16[128,512]{1,0:T(8,128)(2,1)}, u32[]{:S(2)}, u32[]{:S(2)}) collective-permute-start(bf16[128,512]{1,0:T(8,128)(2,1)} %slice.289), channel_id=1, source_target_pairs={{0,8},{8,0},{16,24},{24,16},{1,9},{9,1},{17,25},{25,17},{2,10},{10... | collective-permute-start | bytes 393224 | tf_op jit(solution)/shard_map/ppermute | solution.py:47
  771.4 44.4 %collective-permute-start.65 = (bf16[128,2048]{1,0:T(8,128)(2,1)}, bf16[128,2048]{1,0:T(8,128)(2,1)}, u32[]{:S(2)}, u32[]{:S(2)}) collective-permute-start(bf16[128,2048]{1,0:T(8,128)(2,1)} %reduce-scatter.17.cloned.1.call-done), channel_id=1, source_target_pairs={{0,8},{8,0},{16,24},{24,16},{1,9},{9,1},{17,25},{25,17},{2,10},{10... | collective-permute-start | bytes 1572872 | tf_op jit(solution)/shard_map/ppermute | solution.py:47
  810.8 133.6 %collective-permute-start.67 = (bf16[256,1408]{1,0:T(8,128)(2,1)}, bf16[256,1408]{1,0:T(8,128)(2,1)}, u32[]{:S(2)}, u32[]{:S(2)}) collective-permute-start(bf16[256,1408]{1,0:T(8,128)(2,1)} %reduce-scatter.19.cloned.1.call-done), channel_id=1, source_target_pairs={{0,8},{8,0},{16,24},{24,16},{1,9},{9,1},{17,25},{25,17},{2,10},{10... | collective-permute-start | bytes 2162696 | tf_op jit(solution)/shard_map/ppermute | solution.py:47
  814.4 136.8 %collective-permute-start.69 = (bf16[256,1408]{1,0:T(8,128)(2,1)}, bf16[256,1408]{1,0:T(8,128)(2,1)}, u32[]{:S(2)}, u32[]{:S(2)}) collective-permute-start(bf16[256,1408]{1,0:T(8,128)(2,1)} %reduce-scatter.19.cloned.1.call-done), channel_id=1, source_target_pairs={{0,16},{8,24},{16,0},{24,8},{1,17},{9,25},{17,1},{25,9},{2,18},{10... | collective-permute-start | bytes 2162696 | tf_op jit(solution)/shard_map/ppermute | solution.py:47
  817.2 125.6 %collective-permute-start.66 = (bf16[128,2048]{1,0:T(8,128)(2,1)S(1)}, bf16[128,2048]{1,0:T(8,128)(2,1)}, u32[]{:S(2)}, u32[]{:S(2)}) collective-permute-start(bf16[128,2048]{1,0:T(8,128)(2,1)S(1)} %add.211), channel_id=1, source_target_pairs={{0,16},{8,24},{16,0},{24,8},{1,17},{9,25},{17,1},{25,9},{2,18},{10... | collective-permute-start | bytes 1572872 | tf_op jit(solution)/shard_map/ppermute | solution.py:47
  876.7 92.2 %collective-permute-start.71 = (bf16[256,1408]{1,0:T(8,128)(2,1)}, bf16[256,1408]{1,0:T(8,128)(2,1)}, u32[]{:S(2)}, u32[]{:S(2)}) collective-permute-start(bf16[256,1408]{1,0:T(8,128)(2,1)} %reduce-scatter.21.cloned.1.call-done), channel_id=1, source_target_pairs={{0,8},{8,0},{16,24},{24,16},{1,9},{9,1},{17,25},{25,17},{2,10},{10... | collective-permute-start | bytes 2162696 | tf_op jit(solution)/shard_map/ppermute | solution.py:47
  880.2 93.9 %collective-permute-start.73 = (bf16[256,1408]{1,0:T(8,128)(2,1)}, bf16[256,1408]{1,0:T(8,128)(2,1)}, u32[]{:S(2)}, u32[]{:S(2)}) collective-permute-start(bf16[256,1408]{1,0:T(8,128)(2,1)} %reduce-scatter.21.cloned.1.call-done), channel_id=1, source_target_pairs={{0,16},{8,24},{16,0},{24,8},{1,17},{9,25},{17,1},{25,9},{2,18},{10... | collective-permute-start | bytes 2162696 | tf_op jit(solution)/shard_map/ppermute | solution.py:47
  944.3 35.6 %collective-permute-start.77 = (bf16[176,2048]{1,0:T(8,128)(2,1)}, bf16[176,2048]{1,0:T(8,128)(2,1)}, u32[]{:S(2)}, u32[]{:S(2)}) collective-permute-start(bf16[176,2048]{1,0:T(8,128)(2,1)} %reduce-scatter.23.cloned.1.call-done), channel_id=1, source_target_pairs={{0,16},{8,24},{16,0},{24,8},{1,17},{9,25},{17,1},{25,9},{2,18},{10... | collective-permute-start | bytes 2162696 | tf_op jit(solution)/shard_map/ppermute | solution.py:47
  979.9 48.3 %collective-permute-start.76 = (bf16[88,2048]{1,0:T(8,128)(2,1)S(1)}, bf16[88,2048]{1,0:T(8,128)(2,1)}, u32[]{:S(2)}, u32[]{:S(2)}) collective-permute-start(bf16[88,2048]{1,0:T(8,128)(2,1)S(1)} %slice.294), channel_id=1, source_target_pairs={{0,16},{8,24},{16,0},{24,8},{1,17},{9,25},{17,1},{25,9},{2,18},{10... | collective-permute-start | bytes 1081352 | tf_op jit(solution)/shard_map/ppermute | solution.py:47
  982.3 46.9 %collective-permute-start.78 = (bf16[88,2048]{1,0:T(8,128)(2,1)}, bf16[88,2048]{1,0:T(8,128)(2,1)}, u32[]{:S(2)}, u32[]{:S(2)}) collective-permute-start(bf16[88,2048]{1,0:T(8,128)(2,1)} %slice.295), channel_id=1, source_target_pairs={{0,8},{8,0},{16,24},{24,16},{1,9},{9,1},{17,25},{25,17},{2,10},{10... | collective-permute-start | bytes 1081352 | tf_op jit(solution)/shard_map/ppermute | solution.py:47
  (119 other events, 2018.4 us)
Sparse Core Ops, SparseCore 0:
  14.0 50.4 all-gather.7
  66.7 46.7 all-gather.5
  115.6 52.3 all-gather.9
  170.0 110.2 all-gather.11
  282.3 58.5 all-gather.13
  510.1 47.6 reduce-scatter.14
  583.2 34.8 reduce-scatter.8
  621.0 34.4 reduce-scatter.10
  658.4 34.3 reduce-scatter.12
  694.9 49.9 reduce-scatter.16
  747.7 62.9 reduce-scatter.18
  813.5 63.1 reduce-scatter.20
  879.6 63.2 reduce-scatter.22

commit v2 on v1

v2 whole, which is shorter than its diff:
```python
import functools

import jax
import jax.numpy as jnp
from jax import lax
from jax.experimental import pallas as pl
from jax.experimental.pallas import tpu as pltpu
from jax.sharding import PartitionSpec as P

EPS = 1e-06
MIN_LEN = 1024
BF = jnp.bfloat16
F32 = jnp.float32


def sigmoid(value):
    return jax.nn.sigmoid(value)


def silu(value):
    return value * sigmoid(value)


def silu_grad(value):
    s = sigmoid(value)
    return s * (1.0 + value * (1.0 - s))


def mm(left, right, kind=F32):
    return jnp.dot(left, right, preferred_element_type=F32).astype(kind)


def dot_first(left, right, kind=F32):
    return lax.dot_general(
        left, right, (((0,), (0,)), ((), ())), preferred_element_type=F32
    ).astype(kind)


def dot_last(left, right, kind=F32):
    return lax.dot_general(
        left, right, (((1,), (1,)), ((), ())), preferred_element_type=F32
    ).astype(kind)


def swap(value, bits):
    count = lax.axis_size("dp")
    return lax.ppermute(value, "dp", [(s, s ^ bits) for s in range(count)])


def gather_parts(own):
    half = own.shape[0] // 2
    one, two = swap(own, 1), swap(own, 2)
    top, bottom = swap(one[:half], 2), swap(two[half:], 1)
    return own, one, two, top, bottom


def gather_dp(own):
    return jnp.concatenate(gather_parts(own), axis=0)


def scatter_begin(parts):
    rows = parts.shape[0] // 4
    half = rows // 2
    p0, p1, p2, p3 = (parts[k * rows : (k + 1) * rows] for k in range(4))
    top, bottom = swap(p3[:half], 1), swap(p3[half:], 2)
    one_a, two_b = swap(p1[:half], 1), swap(p2[half:], 2)
    two_a = (p2[:half].astype(F32) + top.astype(F32)).astype(BF)
    one_b = (p1[half:].astype(F32) + bottom.astype(F32)).astype(BF)
    return (two_a, one_b), (p0, one_a, two_b)


def scatter_end(onward, at_hand):
    p0, one_a, two_b = at_hand
    two_a, one_b = swap(onward[0], 2), swap(onward[1], 1)
    one = jnp.concatenate([one_a, one_b], axis=0).astype(F32)
    two = jnp.concatenate([two_a, two_b], axis=0).astype(F32)
    return p0.astype(F32) + one + two


def scatter_dp(parts):
    return scatter_end(*scatter_begin(parts))


def later(value, *needed):
    return lax.optimization_barrier((value, needed))[0]


def pair_halves(own, other, place, heads):
    width = own.shape[1]
    own, other = (v.reshape(heads, 1, -1, width) for v in (own, other))
    both = jnp.where(
        place == 0,
        jnp.concatenate([own, other], axis=1),
        jnp.concatenate([other, own], axis=1),
    )
    return both.reshape(-1, width)


def absolute(blocks):
    place = lax.axis_index("dp")
    odd, high = (place & 1) == 1, (place & 2) == 2
    a, b, c, d = blocks
    a, b = jnp.where(odd, b, a), jnp.where(odd, a, b)
    c, d = jnp.where(odd, d, c), jnp.where(odd, c, d)
    return (
        jnp.where(high, c, a),
        jnp.where(high, d, b),
        jnp.where(high, a, c),
        jnp.where(high, b, d),
    )


def marks(starts_ref, size, count):
    slot = pl.program_id(0)
    col = lax.broadcasted_iota(jnp.int32, (size, 1), 0)
    row = lax.broadcasted_iota(jnp.int32, (1, size), 1)
    sid_c = jnp.zeros((size, 1), jnp.int32)
    sid_r = jnp.zeros((1, size), jnp.int32)
    sid_last = jnp.int32(0)
    begun = jnp.zeros((size, 1), jnp.int32)
    ended = jnp.int32(0)
    for j in range(count):
        at = starts_ref[slot, j]
        sid_c += (col >= at).astype(jnp.int32)
        sid_r += (row >= at).astype(jnp.int32)
        sid_last += (size - 1 >= at).astype(jnp.int32)
        begun += ((col >= at) & (at >= 0)).astype(jnp.int32)
        ended += ((size - 1 >= at) & (at >= 0)).astype(jnp.int32)
    inherit = (begun == 0).astype(F32)
    same_last = (sid_c == sid_last).astype(F32)
    keep = (ended == 0).astype(F32)
    return sid_c == sid_r, inherit, same_last, keep


def split_dot(left, value):
    high = value.astype(BF)
    low = (value - high.astype(F32)).astype(BF)
    return mm(left, high) + mm(left, low)


def halves_of(value):
    high = value.astype(BF)
    return high, (value - high.astype(F32)).astype(BF)


def scores_of(qd, kd):
    (qh, ql), (kh, kl) = halves_of(qd), halves_of(kd)
    return dot_last(qh, kh) + (dot_last(qh, kl) + dot_last(ql, kh)), qh, kh


def gates(f, bound):
    sg = sigmoid(f)
    forget = bound + (1.0 - bound) * sg
    return sg, forget, (1.0 - bound) * (1.0 - sg), jnp.log(forget)


def positions(size):
    rows = lax.broadcasted_iota(jnp.int32, (size, size), 0)
    cols = lax.broadcasted_iota(jnp.int32, (size, size), 1)
    return rows, cols


def about_middle(size):
    rows, cols = positions(size)
    return (cols <= rows).astype(BF) - (cols < size // 2).astype(BF)


def each(heads):
    return [(k, slice(128 * k, 128 * (k + 1))) for k in range(heads)]


def end_kernel(count, heads, starts, f_ref, v_ref, b_ref, pack_ref):
    size = f_ref.shape[0]
    _, _, same_last, keep = marks(starts, size, count)
    middle = about_middle(size)
    for k, at in each(heads):
        _, _, key, a = gates(f_ref[:, at], b_ref[:, at])
        cm = split_dot(middle, a)
        total = jnp.sum(a, axis=0, keepdims=True)
        tail = (key * jnp.exp(cm[size - 1 :] - cm) * same_last).astype(BF)
        pack_ref[k, :128] = dot_first(v_ref[:, at].astype(BF), tail).astype(BF)
        pack_ref[k, 128:] = jnp.broadcast_to(jnp.exp(total) * keep, (16, 128)).astype(BF)


def intra_kernel(count, heads, starts, f_ref, v_ref, q_ref, b_ref, out_ref, qs_ref):
    size = f_ref.shape[0]
    same, inherit, _, _ = marks(starts, size, count)
    middle = about_middle(size)
    rows, cols = positions(size)
    allowed = (cols <= rows) & same
    for _, at in each(heads):
        _, _, key, a = gates(f_ref[:, at], b_ref[:, at])
        cm = split_dot(middle, a)
        mid = jnp.sum(a[: size // 2], axis=0, keepdims=True)
        q = silu(q_ref[:, at])
        scores = jnp.where(allowed, scores_of(q * jnp.exp(cm), key * jnp.exp(-cm))[0], 0.0)
        out_ref[:, at] = mm(scores.astype(BF), v_ref[:, at].astype(BF))
        qs_ref[:, at] = (q * jnp.exp(cm + mid) * inherit).astype(BF)


def join_kernel(near_ref, far_ref, out_ref):
    near, far = near_ref[...].astype(F32), far_ref[...].astype(F32)
    decay = near[:, 128:129]
    out_ref[:, :128] = (near[:, :128] + decay * far[:, :128]).astype(BF)
    out_ref[:, 128:] = (near[:, 128:] * far[:, 128:]).astype(BF)


def reach(near_ref, far_ref, whole_ref, k):
    decay = jnp.where(whole_ref[0] == 1, near_ref[k, 128:].astype(F32)[:1], 1.0)
    return near_ref[k, :128].astype(F32) + decay * far_ref[k, :128].astype(F32)


def mixed_kernel(
    heads, whole, out_ref, qs_ref, g_ref, gain_ref, near_ref, far_ref, mixed_ref, on_ref, enter_ref
):
    for k, at in each(heads):
        enter = reach(near_ref, far_ref, whole, k)
        enter_ref[k] = enter
        mixed = out_ref[:, at] + dot_last(qs_ref[:, at], enter.astype(BF))
        mixed_ref[:, at] = mixed
        r = lax.rsqrt(jnp.mean(mixed * mixed, axis=-1, keepdims=True) + EPS)
        on_ref[:, at] = (mixed * r * gain_ref[...] * silu(g_ref[:, at])).astype(BF)


def norm_back_kernel(
    heads, don_ref, g_ref, mixed_ref, qs_ref, gain_ref, pack_ref, dmix_ref, dg_ref, dpack_ref, dgain_ref
):
    @pl.when(pl.program_id(0) == 0)
    def _():
        dgain_ref[...] = jnp.zeros_like(dgain_ref)

    gain = gain_ref[...]
    for k, at in each(heads):
        don, gz, mixed = don_ref[:, at], g_ref[:, at], mixed_ref[:, at]
        sg = sigmoid(gz)
        s = gz * sg
        r = lax.rsqrt(jnp.mean(mixed * mixed, axis=-1, keepdims=True) + EPS)
        n = mixed * r
        w = don * gain * s
        dmix = r * (w - n * jnp.mean(w * n, axis=-1, keepdims=True))
        dmix_ref[:, at] = dmix
        dg_ref[:, at] = (don * gain * n * (sg * (1.0 + gz * (1.0 - sg)))).astype(BF)
        dpack_ref[k, :128] = dot_first(dmix.astype(BF), qs_ref[:, at]).astype(BF)
        dpack_ref[k, 128:] = pack_ref[k, 128:]
        dgain_ref[...] += jnp.sum(don * s * n, axis=0, keepdims=True)


def back_kernel(
    count, heads, starts, whole, f_ref, v_ref, q_ref, b_ref, dg_ref, dmix_ref, enter_ref, near_ref,
    far_ref, dz_ref, db_ref,
):
    @pl.when(pl.program_id(0) == 0)
    def _():
        db_ref[...] = jnp.zeros_like(db_ref)

    size = f_ref.shape[0]
    same, inherit, same_last, keep = marks(starts, size, count)
    middle = about_middle(size)
    rows, cols = positions(size)
    allowed = (cols <= rows) & same
    after = ((cols >= rows) & same).astype(BF)
    mine = heads * 128
    dz_ref[:, 3 * mine :] = dg_ref[...]
    for k, at in each(heads):
        bound = b_ref[:, at]
        sg, forget, key, a = gates(f_ref[:, at], bound)
        cm = split_dot(middle, a)
        last = cm[size - 1 :]
        mid = jnp.sum(a[: size // 2], axis=0, keepdims=True)
        qz = q_ref[:, at]
        sq = sigmoid(qz)
        up, down = jnp.exp(cm), jnp.exp(-cm)
        v = v_ref[:, at].astype(BF)
        scores, qd, kd = scores_of(qz * sq * up, key * down)
        scores = jnp.where(allowed, scores, 0.0).astype(BF)
        dmix, dmix_low = halves_of(dmix_ref[:, at])
        dscores = jnp.where(allowed, dot_last(dmix, v) + dot_last(dmix_low, v), 0.0).astype(BF)
        enter = enter_ref[k]
        leave = reach(near_ref, far_ref, whole, k)
        leave_low = (leave * jnp.exp(last)).astype(BF)
        enter_low = (enter * jnp.exp(mid)).astype(BF)
        dqd = mm(dscores, kd) + inherit * mm(dmix, enter_low)
        dkd_tail = same_last * mm(v, leave_low)
        dkd = dot_first(dscores, qd) + dkd_tail
        dv = dot_first(scores, dmix) + same_last * dot_last(kd, leave_low)
        qd, kd = qd.astype(F32), kd.astype(F32)
        dlog = dqd * qd - dkd * kd
        rest = jnp.sum(dkd_tail * kd, axis=0, keepdims=True) + keep * jnp.exp(mid + last) * jnp.sum(
            leave * enter, axis=0, keepdims=True
        )
        da = split_dot(after, dlog) + same_last * rest
        dforget = da / forget - dkd * down
        dq = dqd * up * (sq * (1.0 + qz * (1.0 - sq)))
        df = dforget * (1.0 - bound) * sg * (1.0 - sg)
        for n, value in enumerate((df, dv, dq)):
            dz_ref[:, n * mine + 128 * k : n * mine + 128 * (k + 1)] = value.astype(BF)
        db_ref[:, at] += jnp.sum(dforget * (1.0 - sg), axis=0, keepdims=True)


def heads_kernel(heads, order, blocks_ref, *outs):
    for g in range(4):
        here = order[g]
        for n, out_ref in enumerate(outs):
            for k in range(heads):
                to = ((g & 1) * heads + k) * 2 + (g >> 1)
                at = n * heads + k
                out_ref[:, 128 * to : 128 * (to + 1)] = blocks_ref[
                    here, :, 128 * at : 128 * (at + 1)
                ].astype(F32)


def hidden_kernel(chunk, seqs, order, blocks_ref, *outs):
    for g in range(4):
        here = order[g]
        for n, out_ref in enumerate(outs):
            part = blocks_ref[here, :, n * seqs * chunk : (n + 1) * seqs * chunk].astype(F32)
            for j in range(seqs):
                to = (4 * j + g) * chunk
                out_ref[:, to : to + chunk] = part[:, j * chunk : (j + 1) * chunk]


def across(size, width, base=0):
    return pl.BlockSpec((size, width), lambda s, *_: (s, base))


def states(rows, heads):
    return pl.BlockSpec((heads, rows, 128), lambda s, *_: (s, 0, 0))


def fixed(width):
    return pl.BlockSpec((1, width), lambda s, *_: (0, 0))


def call(kernel, grid, scalars, in_specs, out_specs, out_shape, args, flops=1e9):
    params = pltpu.CompilerParams(vmem_limit_bytes=48 * 1024 * 1024)
    return pl.pallas_call(
        kernel,
        grid_spec=pltpu.PrefetchScalarGridSpec(
            num_scalar_prefetch=len(scalars), grid=grid, in_specs=in_specs, out_specs=out_specs
        ),
        out_shape=out_shape,
        compiler_params=params,
        cost_estimate=pl.CostEstimate(flops=int(flops / 100), bytes_accessed=1 << 16, transcendentals=0),
    )(*scalars, *args)


def join(near, far):
    pairs = near.shape[0]
    block = pl.BlockSpec((pairs // 2,) + near.shape[1:], lambda s: (s, 0, 0))
    return call(join_kernel, (2,), (), [block, block], block, jax.ShapeDtypeStruct(near.shape, BF), (near, far))


def equal_halves(tokens):
    return lax.axis_size("seq") * tokens == 2 * MIN_LEN and MIN_LEN == 4 * tokens


def reached(pack, forward, tokens):
    count = lax.axis_size("seq")
    place = lax.axis_index("seq")
    if equal_halves(tokens):
        first = [s for s in range(0, count, 4)]
        order = (0, 1, 2, 3) if forward else (3, 2, 1, 0)

        def hop(value, moves):
            return lax.ppermute(
                value, "seq", [(f + order[a], f + order[b]) for f in first for a, b in moves]
            )

        near = hop(pack, ((0, 1), (2, 3)))
        pair = join(pack, near)
        third = hop(pair, ((1, 3),))
        second = hop(third, ((3, 2),))
        far = jnp.where((place & 3) == order[3], third, second)
        there = (place & 1) == (order[1] & 1)
        return near, far, there.astype(jnp.int32)[None], (pair, third)
    every = lax.all_gather(pack, "seq")
    shape = (pack.shape[0], 128, pack.shape[2])

    def one(k, total):
        at = k if forward else count - 1 - k
        there = lax.dynamic_index_in_dim(every, at, 0, False).astype(F32)
        new = there[:, :128] + there[:, 128:129] * total
        return jnp.where((at < place) if forward else (at > place), new, total)

    total = lax.fori_loop(0, count, one, jnp.zeros(shape, F32))
    total = jnp.concatenate([total, jnp.zeros_like(total[:, :16])], axis=1).astype(BF)
    return total, jnp.zeros_like(total), jnp.ones((1,), jnp.int32), (total, total)


def everywhere(value):
    for axis in ("seq", "dp"):
        bit = 1
        while bit < lax.axis_size(axis):
            pairs = [(s, s ^ bit) for s in range(lax.axis_size(axis))]
            value = value + lax.ppermute(value, axis, pairs)
            bit *= 2
    return value


def shards(
    block_input,
    lengths,
    norm_gain,
    w_q,
    w_f,
    w_i,
    w_g,
    lower_bound,
    group_gain,
    w_o,
    ffn_norm_gain,
    w_gate,
    w_up,
    w_down,
    out_grad,
):
    tokens, width = block_input.shape
    head_dim = group_gain.shape[0]
    heads = width // head_dim // 4
    mine = heads * head_dim
    seqs = lax.axis_size("seq")
    dp = lax.axis_index("dp")
    low_bit, high_bit = dp & 1, dp >> 1

    def of_heads(value, axis):
        shape = value.shape
        cut = value.reshape(shape[:axis] + (2, heads, 2, head_dim) + shape[axis + 1 :])
        cut = lax.dynamic_index_in_dim(cut, high_bit, axis + 2, False)
        cut = lax.dynamic_index_in_dim(cut, low_bit, axis, False)
        return cut.reshape(shape[:axis] + (mine,) + shape[axis + 1 :])

    def to_heads(blocks, axis):
        a, b, c, d = absolute(blocks)
        shape = a.shape
        cut = [v.reshape(shape[:axis] + (heads, head_dim) + shape[axis + 1 :]) for v in (a, b, c, d)]
        pair = [jnp.stack([cut[k], cut[k + 2]], axis=axis + 1) for k in range(2)]
        full = jnp.stack(pair, axis=axis)
        return full.reshape(shape[:axis] + (4 * mine,) + shape[axis + 1 :])

    chunk = w_down.shape[0] // 4
    ff = chunk * seqs

    def of_hidden(value):
        cut = value.reshape(value.shape[0], seqs, 4, chunk)
        return lax.dynamic_index_in_dim(cut, dp, 2, False).reshape(value.shape[0], ff)

    def to_hidden(blocks):
        cut = [v.reshape(v.shape[0], seqs, 1, chunk) for v in absolute(blocks)]
        return jnp.concatenate(cut, axis=2).reshape(blocks[0].shape[0], 4 * ff)

    def gather_seq(value):
        return lax.all_gather(value, "seq", axis=0, tiled=True)

    def scatter_seq(value):
        return lax.psum_scatter(value.astype(BF), "seq", scatter_dimension=0, tiled=True)

    def blocks_dp(value):
        rows = value.shape[0]
        full = gather_dp(value)
        return [full[k * rows : (k + 1) * rows] for k in range(4)]

    w4 = gather_seq(jnp.concatenate([of_heads(w, 1) for w in (w_f, w_i, w_q, w_g)], axis=1))

    x = block_input.astype(F32)
    r1 = lax.rsqrt(jnp.mean(x * x, axis=-1, keepdims=True) + EPS)
    h = (x * r1 * norm_gain).astype(BF)

    starts = jnp.cumsum(lengths[0]) - lengths[0] - lax.axis_index("seq") * tokens
    count = lengths.shape[1]
    if equal_halves(tokens):
        starts = jnp.broadcast_to(starts[None], (4, count))
    else:
        starts = jnp.stack([starts] + [swap(starts, k) for k in (1, 2, 3)])
        h = later(h, starts)
    h_all = gather_dp(h)
    w_o, out_own = later((w_o, out_grad), h_all)
    natural = w_o.shape[0] == 2 * head_dim
    if natural:
        part = lax.dynamic_slice_in_dim(w_o, dp * (head_dim // 2), head_dim // 2, 0)
        wo = gather_seq(part)
    else:
        wo = of_heads(gather_seq(w_o), 0)

    og_all = gather_dp(out_own)
    z = mm(h_all, w4)
    w_gate, w_up = later((w_gate, w_up), h_all)
    wgu = gather_seq(jnp.concatenate([of_hidden(w_gate), of_hidden(w_up)], axis=1))
    w_down = later(w_down, z)
    wd = gather_seq(lax.dynamic_slice_in_dim(w_down, dp * chunk, chunk, 0))

    bound = of_heads(lower_bound, 0)[None]
    gain = group_gain[None]

    grid = (4,)
    pairs = heads * 4
    rows = 4 * tokens
    wide = jax.ShapeDtypeStruct((rows, mine), F32)
    thin = jax.ShapeDtypeStruct((rows, mine), BF)
    packed = jax.ShapeDtypeStruct((pairs, 144, 128), BF)
    one = across(tokens, mine)
    fl, vl, ql, gl = (across(tokens, mine, k) for k in range(4))
    pack_spec, state_spec = states(144, heads), states(128, heads)

    pack = call(
        functools.partial(end_kernel, count, heads), grid, (starts,),
        [fl, vl, fixed(mine)], pack_spec, packed, (z, z, bound), 2e9,
    )
    near, far, whole, _ = reached(pack, True, tokens)
    intra, qs = call(
        functools.partial(intra_kernel, count, heads), grid, (starts,),
        [fl, vl, ql, fixed(mine)], [one, one], [wide, thin], (z, z, z, bound), 3e9,
    )
    if natural:
        halves = later(wo, pack)
        own = lax.dynamic_slice_in_dim(halves, low_bit * (mine // 2), mine // 2, 0)
        give = lax.dynamic_slice_in_dim(halves, (1 - low_bit) * (mine // 2), mine // 2, 0)
        wo = pair_halves(own, swap(give, 1), low_bit, heads)
    mixed, on, enter = call(
        functools.partial(mixed_kernel, heads), grid, (whole,),
        [one, one, gl, fixed(128), pack_spec, pack_spec],
        [one, one, state_spec],
        [wide, thin, jax.ShapeDtypeStruct((pairs, 128, 128), F32)],
        (intra, qs, z, gain, near, far),
    )

    branch = scatter_dp(mm(on, wo, BF))
    branch, og_all = lax.optimization_barrier((branch, og_all))
    y = x + branch
    r2 = lax.rsqrt(jnp.mean(y * y, axis=-1, keepdims=True) + EPS)
    h2_all = gather_dp((y * r2 * ffn_norm_gain).astype(BF))

    gu = mm(h2_all, wgu)
    gate, upper = gu[:, :ff], gu[:, ff:]
    hidden = (silu(gate) * upper).astype(BF)
    down_part = dot_first(hidden, og_all, BF)
    down_rows = scatter_seq(down_part)
    d_hidden = dot_last(og_all, later(wd, down_part))
    d_gate = (d_hidden * upper * silu_grad(gate)).astype(BF)
    d_upper = (d_hidden * silu(gate)).astype(BF)
    d_gu = jnp.concatenate([d_gate, d_upper], axis=1)
    h2_part = dot_last(d_gu, wgu, BF)
    gu_part = dot_first(h2_all, later(d_gu, h2_part), BF)
    gu_rows = scatter_seq(gu_part)
    d_h2 = later(scatter_dp(h2_part), gu_part)

    og = out_grad.astype(F32)
    d_ffn_gain = jnp.sum(d_h2 * y * r2, axis=0)
    u2 = d_h2 * ffn_norm_gain
    d_y = og + r2 * u2 - y * (r2 * r2 * r2) * jnp.mean(u2 * y, axis=-1, keepdims=True)
    d_y_low, down_rows = lax.optimization_barrier((d_y.astype(BF), down_rows))
    out_part = mm(later(hidden, d_y_low), wd, BF)
    d_branch, out_part = lax.optimization_barrier((gather_dp(d_y_low), out_part))

    o_part = dot_first(on, d_branch, BF)
    d_on = dot_last(later(d_branch, o_part), wo)
    d_mixed, d_gz, d_pack, d_gain = call(
        functools.partial(norm_back_kernel, heads), grid, (),
        [one, gl, one, one, fixed(128), pack_spec],
        [one, one, pack_spec, fixed(128)],
        [wide, thin, packed, jax.ShapeDtypeStruct((1, 128), F32)],
        (d_on, z, mixed, qs, gain, pack),
    )
    near, far, whole, passed = reached(d_pack, False, tokens)
    out_part, o_part = later((out_part, o_part), passed[0])
    onward, at_hand = scatter_begin(out_part)
    result = (y + scatter_end(later(onward, passed[1]), at_hand)).astype(BF)

    if natural:
        cut = o_part.reshape(heads, 2, head_dim // 2, width)
        own = lax.dynamic_index_in_dim(cut, low_bit, 1, False).reshape(mine // 2, width)
        give = lax.dynamic_index_in_dim(cut, 1 - low_bit, 1, False).reshape(mine // 2, width)
        got = later(swap(give, 1), result)
        o_full = jnp.where(
            low_bit == 0,
            jnp.concatenate([own, got], axis=0),
            jnp.concatenate([got, own], axis=0),
        )
    else:
        none = jnp.zeros_like(o_part)
        o_full = to_heads([o_part, none, none, none], 0)
    o_rows = scatter_seq(o_full)

    near, far = later((near, far), result, o_full, gu_rows)
    dz, d_bound = call(
        functools.partial(back_kernel, count, heads), grid, (starts, whole),
        [fl, vl, ql, fixed(mine), one, one, state_spec, pack_spec, pack_spec],
        [across(tokens, 4 * mine), fixed(mine)],
        [jax.ShapeDtypeStruct((rows, 4 * mine), BF), jax.ShapeDtypeStruct((1, mine), F32)],
        (z, z, z, bound, d_gz, d_mixed, enter, near, far), 8e9,
    )

    gate_parts, up_parts = gather_parts(gu_rows[:, :ff]), gather_parts(gu_rows[:, ff:])
    fv_part = dot_first(h_all, later(dz, gate_parts[1:3])[:, : 2 * mine], BF)
    fv_rows = scatter_seq(fv_part)
    h_part = dot_last(later(dz, fv_part, up_parts[1:3]), w4, BF)
    d_h = scatter_dp(h_part)
    dz, o_rows = later((dz, o_rows), h_part)
    qg_part = dot_first(h_all, dz[:, 2 * mine :], BF)
    qg_rows = scatter_seq(qg_part)
    fv_rows = later(fv_rows, gate_parts[1:], up_parts[1:], d_h)
    down_parts = gather_parts(later(down_rows, d_h))

    order = jnp.arange(4, dtype=jnp.int32) ^ dp.astype(jnp.int32)

    def whole_rows(parts, kernel, columns, flat):
        part, total = parts[0].shape[0], 4 * columns
        count = parts[0].shape[1] // columns
        blocks = jnp.concatenate(parts, axis=0).reshape(4, part, count * columns)
        if not flat:
            return [to_hidden([blocks[k] for k in range(4)]).astype(F32)]
        tall = min(64, part)
        out = jax.ShapeDtypeStruct((part, total), F32)
        return call(
            kernel, (part // tall,), (order,),
            [pl.BlockSpec((4, tall, count * columns), lambda s, *_: (0, s, 0))],
            [pl.BlockSpec((tall, total), lambda s, *_: (s, 0))] * count, [out] * count, (blocks,),
        )

    if natural:
        grad_o = jnp.concatenate(absolute(blocks_dp(o_rows)), axis=0).astype(F32)
    else:
        grad_o = lax.psum(o_rows.astype(F32), "dp")
    down_all = down_parts[:3] + (jnp.concatenate(down_parts[3:], axis=0),)
    grad_down = jnp.concatenate(absolute(down_all), axis=0).astype(F32)
    join_hidden = functools.partial(hidden_kernel, chunk, seqs)
    [grad_gate] = whole_rows(gate_parts, join_hidden, ff, chunk % 16 == 0)
    [grad_up] = whole_rows(up_parts, join_hidden, ff, chunk % 16 == 0)
    join_heads = functools.partial(heads_kernel, heads)
    grad_f, grad_i = whole_rows(gather_parts(fv_rows), join_heads, mine, True)
    grad_q, grad_g = whole_rows(gather_parts(later(qg_rows, fv_rows)), join_heads, mine, True)

    d_norm_gain = jnp.sum(d_h * x * r1, axis=0)
    u1 = d_h * norm_gain
    d_x = d_y + r1 * u1 - x * (r1 * r1 * r1) * jnp.mean(u1 * x, axis=-1, keepdims=True)

    zero = jnp.zeros((mine,), F32)
    d_bound = to_heads([d_bound[0], zero, zero, zero], 0)
    small = everywhere(jnp.concatenate([d_norm_gain, d_ffn_gain, d_bound, d_gain[0]]))
    return (
        result,
        d_x.astype(BF),
        small[:width],
        grad_q,
        grad_f,
        grad_i,
        grad_g,
        small[2 * width : 3 * width],
        small[3 * width :],
        grad_o,
        small[width : 2 * width],
        grad_gate,
        grad_up,
        grad_down,
    )


def solution(mesh):
    both = P(("dp", "seq"), None)
    rows = P("seq", None)
    return jax.shard_map(
        shards,
        mesh=mesh,
        in_specs=(
            both, P("dp", None), P(), rows, rows, rows, rows, P(), P(), rows, P(), rows, rows, rows, both,
        ),
        out_specs=(
            both, both, P(), rows, rows, rows, rows, P(), P(), rows, P(), rows, rows, rows,
        ),
        check_vma=False,
    )
```

time: 1050 us -> 747 us (0.71)
  waiting for transfers between devices: 461 us -> 307 us
  local copies, waits for them, and re-layouts: 133 us -> 79 us
  blocking collectives: 47.4 us -> 0 us
  other arithmetic: 61.8 us -> 41.4 us
  matrix products: 154 us -> 139 us
    reduce_scatter x8 -> x5, waiting for transfers between devices: 148 us -> 0.03 us  [scatter_seq(): lax.psum_scatter(value.astype(BF), 'seq', scatter_dimension=0, tiled=True)]
    psum x1 -> x0, blocking collectives: 47.4 us -> none  [shards(): lax.psum((d_norm_gain, d_ffn_gain, d_gain[0], d_bound), ('dp', 'seq'))]
    ppermute x73 -> x66, waiting for transfers between devices: 206 us -> 250 us  [swap(): return lax.ppermute(value, 'dp', [(s, s ^ bits) for s in range(count)])]
    all_gather x5 -> x4, waiting for transfers between devices: 57.4 us -> 28.6 us  [gather_seq(): return lax.all_gather(value, 'seq', axis=0, tiled=True)]
    unnamed x150 -> x125, local copies, waits for them, and re-layouts: 69.1 us -> 41.9 us
    ppermute x6 -> x11, waiting for transfers between devices: 48.9 us -> 28.2 us  [the longest x5 16.3 us: everywhere(): value = value + lax.ppermute(value, axis, pairs)]
    convert_element_type x6 -> x0, local copies, waits for them, and re-layouts: 18.6 us -> none  [the longest x4 7.23 us: head_grad(): to_heads(blocks_dp(scatter_seq(dot_first(h_all, value, BF))), 1).astype(F32)]
    select_n x24 -> x0, local copies, waits for them, and re-layouts: 11.5 us -> none  [the longest x6 3.76 us: absolute(): jnp.where(high, b, d)]
  transfers between devices with their start and end apart: 92 -> 86, of which waited for: 46 -> 47; matrix products, arithmetic and copies ran while one was open for 27% -> 31% of each run, Pallas kernels for 5% -> 8%
where the time goes in v2:
time: 747 us; the launch traced here: 740 us
  waiting for transfers between devices  307 us (41%)
  matrix products  139 us (19%)
  starting transfers between devices  96.7 us (13%)
  local copies, waits for them, and re-layouts  79 us (11%)
  Pallas kernels  61 us (8%)
  other arithmetic  41.4 us (6%)
  between operations  15.5 us (2%)
    ppermute x66, waiting for transfers between devices, swap(): return lax.ppermute(value, 'dp', [(s, s ^ bits) for s in range(count)])  250 us
    ppermute x66, starting transfers between devices, swap(): return lax.ppermute(value, 'dp', [(s, s ^ bits) for s in range(count)])  81.4 us
    pallas_call x11, Pallas kernels, call(): pl.pallas_call(kernel, grid_spec=pltpu.PrefetchScalarGridSpec(num_scalar_...  61 us
    dot_general x4, matrix products, dot_last(): lax.dot_general(left, right, (((1,), (1,)), ((), ())), preferred_element_...  48.2 us
    dot_general x5, matrix products, dot_first(): lax.dot_general(left, right, (((0,), (0,)), ((), ())), preferred_element_...  47.1 us
    dot_general x4, matrix products, mm(): return jnp.dot(left, right, preferred_element_type=F32).astype(kind)  43.9 us
    unnamed x125, local copies, waits for them, and re-layouts  41.9 us
    all_gather x4, waiting for transfers between devices, gather_seq(): return lax.all_gather(value, 'seq', axis=0, tiled=True)  28.6 us
  transfers between devices with their start and end apart: 86, of which 47 were waited for; matrix products, arithmetic and copies ran while one was open for 31% of the time, Pallas kernels for 8%

profile of v2, /device:TPU:0, one launch (start us, length us, event | category | flops | bytes accessed | tf_op | source)
XLA Modules:
  0.0 739.7 jit_solution(6324263161073536374)
XLA Ops:
  29.1 21.8 %collective-permute-done = bf16[256,2048]{1,0:T(8,128)(2,1)S(1)} collective-permute-done((bf16[256,2048]{1,0:T(8,128)(2,1)}, bf16[256,2048]{1,0:T(8,128)(2,1)S(1)}, u32[]{:S(2)}, u32[]{:S(2)}) %collective-permute-start) | collective-permute-done | bytes 1048608 | tf_op jit(solution)/shard_map/ppermute | solution.py:47
  83.6 21.5 %all-gather.5.cloned.1.call-done = bf16[2048,2048]{0,1:T(8,128)(2,1)} async-done(((bf16[256,2048]{0,1:T(8,128)(2,1)}), bf16[2048,2048]{0,1:T(8,128)(2,1)}) %all-gather.5.cloned.1.call-update) | async-done | bytes 8388624 | tf_op jit(solution)/shard_map/all_gather | solution.py:452
  105.0 14.6 %fusion.25.f_ref.v_ref.q_ref.g_ref = f32[1024,2048]{1,0:T(8,128)} fusion(bf16[1024,2048]{1,0:T(8,128)(2,1)} %constant_dynamic-update-slice_fusion, bf16[2048,2048]{0,1:T(8,128)(2,1)} %all-gather.5.cloned.1.call-done), kind=kOutput, calls=%fused_computation.160 | convolution fusion | flops 8589934592 | bytes 20971520 | tf_op jit(solution)/shard_map/dot_general | solution.py:30
  119.7 6.9 shard_map.255.near_ref.pack_ref
  145.5 12.0 %shard_map.254 = (f32[1024,512]{1,0:T(8,128)S(1)}, bf16[1024,512]{1,0:T(8,128)(2,1)S(1)}) custom-call(s32[4,2]{1,0:T(4,128)S(1)} %broadcast_in_dim.33.starts, f32[1024,2048]{1,0:T(8,128)} %fusion.25.f_ref.v_ref.q_ref.g_ref, f32[1024,2048]{1,0:T(8,128)} %fusion.25.f_ref.v_ref.q_ref.g_ref, f32[1024,2048]{1,0:T(8,128)} %fusion.25.f_ref.v_ref.q_ref.g_ref, ...), custom_call_target="tpu_custom_call" | custom-call | flops 30000000 | bytes 65536 | tf_op jit(solution)/shard_map/pallas_call | solution.py:336
  215.8 11.2 %collective-permute-done.10 = bf16[128,2048]{1,0:T(8,128)(2,1)} collective-permute-done((bf16[128,2048]{1,0:T(8,128)(2,1)}, bf16[128,2048]{1,0:T(8,128)(2,1)}, u32[]{:S(2)}, u32[]{:S(2)}) %collective-permute-start.10) | collective-permute-done | bytes 524320 | tf_op jit(solution)/shard_map/ppermute | solution.py:47
  235.6 20.4 %collective-permute-done.18 = bf16[256,2048]{1,0:T(8,128)(2,1)S(1)} collective-permute-done((bf16[256,2048]{1,0:T(8,128)(2,1)S(1)}, bf16[256,2048]{1,0:T(8,128)(2,1)S(1)}, u32[]{:S(2)}, u32[]{:S(2)}) %collective-permute-start.18) | collective-permute-done | bytes 1048608 | tf_op jit(solution)/shard_map/ppermute | solution.py:47
  261.5 8.5 %collective-permute-done.20 = bf16[128,2048]{1,0:T(8,128)(2,1)S(1)} collective-permute-done((bf16[128,2048]{1,0:T(8,128)(2,1)S(1)}, bf16[128,2048]{1,0:T(8,128)(2,1)S(1)}, u32[]{:S(2)}, u32[]{:S(2)}) %collective-permute-start.20) | collective-permute-done | bytes 524320 | tf_op jit(solution)/shard_map/ppermute | solution.py:47
  273.6 17.4 %fusion.26 = f32[1024,2816]{1,0:T(8,128)S(1)} fusion(bf16[1024,2048]{1,0:T(8,128)(2,1)} %constant_dynamic-update-slice_fusion.10, bf16[2048,2816]{0,1:T(8,128)(2,1)} %all-gather.11.cloned.1.call-done), kind=kOutput, calls=%fused_computation.161 | convolution fusion | flops 11811160064 | bytes 27262976 | tf_op jit(solution)/shard_map/dot_general | solution.py:30
  298.5 8.1 %convolution_convert_fusion.1 = bf16[1408,2048]{1,0:T(8,128)(2,1)} fusion(bf16[1024,1408]{1,0:T(8,128)(2,1)S(1)} %multiply_convert_fusion.2, bf16[1024,2048]{1,0:T(8,128)(2,1)S(1)} %copy-done.37), kind=kOutput, calls=%fused_computation.1 | convolution fusion | flops 5908463616 | bytes 12845056 | tf_op jit(solution)/shard_map/dot_general | solution.py:34
  309.2 14.3 %multiply_convert_fusion.1 = (bf16[1024,1408]{1,0:T(8,128)(2,1)S(1)}, bf16[1024,1408]{1,0:T(8,128)(2,1)S(1)}) fusion(f32[1024,2816]{1,0:T(8,128)} %copy-done.17, bf16[1024,2048]{1,0:T(8,128)(2,1)} %copy-done.36, bf16[1408,2048]{1,0:T(8,128)(2,1)} %all-gather.9.cloned.1.call-done), kind=kOutput, calls=%fused_computation.4 | convolution fusion | flops 5924323328 | bytes 27262976 | tf_op jit(solution)/shard_map/dot_general | solution.py:40
  323.9 16.4 %convolution_convert_fusion.2 = bf16[1024,2048]{1,0:T(8,128)(2,1)} fusion(bf16[2048,2816]{0,1:T(8,128)(2,1)} %all-gather.11.cloned.1.call-done, bf16[1024,1408]{1,0:T(8,128)(2,1)S(1)} %get-tuple-element.120, bf16[1024,1408]{1,0:T(8,128)(2,1)S(1)} %get-tuple-element.119), kind=kOutput, calls=%fused_computation.14 | convolution fusion | flops 11824791552 | bytes 21495808 | tf_op jit(solution)/shard_map/dot_general | solution.py:40
  340.3 17.8 %convolution_convert_fusion = bf16[2048,2816]{1,0:T(8,128)(2,1)} fusion(bf16[1024,2048]{1,0:T(8,128)(2,1)} %constant_dynamic-update-slice_fusion.10, bf16[1024,2816]{1,0:T(8,128)(2,1)S(1)} %pad_maximum_fusion), kind=kOutput, calls=%fused_computation | convolution fusion | flops 11816927232 | bytes 21495808 | tf_op jit(solution)/shard_map/dot_general | solution.py:34
  364.4 10.7 %collective-permute-done.23 = bf16[128,2048]{1,0:T(8,128)(2,1)S(1)} collective-permute-done((bf16[128,2048]{1,0:T(8,128)(2,1)S(1)}, bf16[128,2048]{1,0:T(8,128)(2,1)S(1)}, u32[]{:S(2)}, u32[]{:S(2)}) %collective-permute-start.23) | collective-permute-done | bytes 524320 | tf_op jit(solution)/shard_map/ppermute | solution.py:47
  379.1 8.7 %collective-permute-done.22 = bf16[128,2048]{1,0:T(8,128)(2,1)S(1)} collective-permute-done((bf16[128,2048]{1,0:T(8,128)(2,1)S(1)}, bf16[128,2048]{1,0:T(8,128)(2,1)S(1)}, u32[]{:S(2)}, u32[]{:S(2)}) %collective-permute-start.22) | collective-permute-done | bytes 524320 | tf_op jit(solution)/shard_map/ppermute | solution.py:47
  387.8 10.2 %collective-permute-done.24 = bf16[128,2048]{1,0:T(8,128)(2,1)S(1)} collective-permute-done((bf16[128,2048]{1,0:T(8,128)(2,1)S(1)}, bf16[128,2048]{1,0:T(8,128)(2,1)S(1)}, u32[]{:S(2)}, u32[]{:S(2)}) %collective-permute-start.24) | collective-permute-done | bytes 524320 | tf_op jit(solution)/shard_map/ppermute | solution.py:47
  404.1 9.6 %convolution_convert_fusion.4 = bf16[1024,2048]{1,0:T(8,128)(2,1)S(1)} fusion(bf16[1024,1408]{1,0:T(8,128)(2,1)} %copy-done.27, bf16[1408,2048]{1,0:T(8,128)(2,1)} %all-gather.9.cloned.1.call-done), kind=kOutput, calls=%fused_computation.16 | convolution fusion | flops 5907677184 | bytes 12845056 | tf_op jit(solution)/shard_map/dot_general | solution.py:30
  413.7 12.9 %collective-permute-done.28 = bf16[256,2048]{1,0:T(8,128)(2,1)S(1)} collective-permute-done((bf16[256,2048]{1,0:T(8,128)(2,1)}, bf16[256,2048]{1,0:T(8,128)(2,1)S(1)}, u32[]{:S(2)}, u32[]{:S(2)}) %collective-permute-start.28) | collective-permute-done | bytes 1048608 | tf_op jit(solution)/shard_map/ppermute | solution.py:47
  429.1 9.9 %collective-permute-done.30 = bf16[128,2048]{1,0:T(8,128)(2,1)S(1)} collective-permute-done((bf16[128,2048]{1,0:T(8,128)(2,1)S(1)}, bf16[128,2048]{1,0:T(8,128)(2,1)S(1)}, u32[]{:S(2)}, u32[]{:S(2)}) %collective-permute-start.30) | collective-permute-done | bytes 524320 | tf_op jit(solution)/shard_map/ppermute | solution.py:47
  465.0 9.5 %collective-permute-done.34 = bf16[128,2048]{1,0:T(8,128)(2,1)} collective-permute-done((bf16[128,2048]{1,0:T(8,128)(2,1)}, bf16[128,2048]{1,0:T(8,128)(2,1)}, u32[]{:S(2)}, u32[]{:S(2)}) %collective-permute-start.34) | collective-permute-done | bytes 524320 | tf_op jit(solution)/shard_map/ppermute | solution.py:47
  477.5 9.2 %collective-permute-done.36 = bf16[16,144,128]{2,1,0:T(8,128)(2,1)} collective-permute-done((bf16[16,144,128]{2,1,0:T(8,128)(2,1)S(1)}, bf16[16,144,128]{2,1,0:T(8,128)(2,1)}, u32[]{:S(2)}, u32[]{:S(2)}) %collective-permute-start.36) | collective-permute-done | bytes 589856 | tf_op jit(solution)/shard_map/ppermute | solution.py:365
  489.9 11.7 %collective-permute-done.37 = bf16[128,2048]{1,0:T(8,128)(2,1)S(1)} collective-permute-done((bf16[128,2048]{1,0:T(8,128)(2,1)S(1)}, bf16[128,2048]{1,0:T(8,128)(2,1)S(1)}, u32[]{:S(2)}, u32[]{:S(2)}) %collective-permute-start.37) | collective-permute-done | bytes 524320 | tf_op jit(solution)/shard_map/ppermute | solution.py:47
  504.4 14.0 %collective-permute-done.41 = bf16[256,2048]{1,0:T(8,128)(2,1)S(1)} collective-permute-done((bf16[256,2048]{1,0:T(8,128)(2,1)S(1)}, bf16[256,2048]{1,0:T(8,128)(2,1)S(1)}, u32[]{:S(2)}, u32[]{:S(2)}) %collective-permute-start.41) | collective-permute-done | bytes 1048608 | tf_op jit(solution)/shard_map/ppermute | solution.py:47
  533.5 16.2 %shard_map.260 = (bf16[1024,2048]{1,0:T(8,128)(2,1)}, f32[1,512]{1,0:T(1,128)S(1)}) custom-call(s32[4,2]{1,0:T(4,128)S(1)} %broadcast_in_dim.33.starts, s32[1]{0:T(128)} %bitcast.20.whole, f32[1024,2048]{1,0:T(8,128)} %fusion.25.f_ref.v_ref.q_ref.g_ref, f32[1024,2048]{1,0:T(8,128)} %fusion.25.f_ref.v_ref.q_ref.g_ref, ...), custom_call_target="tpu_custom_call" | custom-call | flops 80000000 | bytes 65536 | tf_op jit(solution)/shard_map/pallas_call | solution.py:336
  549.7 7.8 %convolution_convert_fusion.7 = bf16[2048,1024]{1,0:T(8,128)(2,1)} fusion(bf16[1024,2048]{1,0:T(8,128)(2,1)S(1)} %copy-done.35, bf16[1024,2048]{1,0:T(8,128)(2,1)} %get-tuple-element.96), kind=kOutput, calls=%fused_computation.19 | convolution fusion | flops 4297064448 | bytes 10485760 | tf_op jit(solution)/shard_map/dot_general | solution.py:34
  559.5 13.1 %collective-permute-done.44 = bf16[256,1408]{1,0:T(8,128)(2,1)} collective-permute-done((bf16[256,1408]{1,0:T(8,128)(2,1)}, bf16[256,1408]{1,0:T(8,128)(2,1)}, u32[]{:S(2)}, u32[]{:S(2)}) %collective-permute-start.44) | collective-permute-done | bytes 720928 | tf_op jit(solution)/shard_map/ppermute | solution.py:47
  573.5 13.9 %convolution_convert_fusion.3 = bf16[1024,2048]{1,0:T(8,128)(2,1)} fusion(bf16[1024,2048]{1,0:T(8,128)(2,1)} %get-tuple-element.96, bf16[2048,2048]{0,1:T(8,128)(2,1)} %all-gather.5.cloned.1.call-done), kind=kOutput, calls=%fused_computation.15 | convolution fusion | flops 8592031744 | bytes 16777216 | tf_op jit(solution)/shard_map/dot_general | solution.py:40
  587.4 9.6 %convolution_convert_fusion.6 = bf16[2048,1024]{1,0:T(8,128)(2,1)} fusion(bf16[1024,2048]{1,0:T(8,128)(2,1)} %constant_dynamic-update-slice_fusion, bf16[1024,2048]{1,0:T(8,128)(2,1)} %get-tuple-element.96), kind=kOutput, calls=%fused_computation.18 | convolution fusion | flops 4297064448 | bytes 10485760 | tf_op jit(solution)/shard_map/dot_general | solution.py:34
  629.5 13.7 %collective-permute-done.57 = bf16[128,1408]{1,0:T(8,128)(2,1)S(1)} collective-permute-done((bf16[128,1408]{1,0:T(8,128)(2,1)S(1)}, bf16[128,1408]{1,0:T(8,128)(2,1)S(1)}, u32[]{:S(2)}, u32[]{:S(2)}) %collective-permute-start.57) | collective-permute-done | bytes 360480 | tf_op jit(solution)/shard_map/ppermute | solution.py:47
  680.8 6.5 collective-permute-done.56
  691.6 7.7 %collective-permute-done.76 = bf16[88,2048]{1,0:T(8,128)(2,1)S(1)} collective-permute-done((bf16[88,2048]{1,0:T(8,128)(2,1)S(1)}, bf16[88,2048]{1,0:T(8,128)(2,1)S(1)}, u32[]{:S(2)}, u32[]{:S(2)}) %collective-permute-start.76) | collective-permute-done | bytes 360480 | tf_op jit(solution)/shard_map/ppermute | solution.py:47
  706.8 8.1 %collective-permute-done.65 = bf16[256,1024]{1,0:T(8,128)(2,1)S(1)} collective-permute-done((bf16[256,1024]{1,0:T(8,128)(2,1)}, bf16[256,1024]{1,0:T(8,128)(2,1)S(1)}, u32[]{:S(2)}, u32[]{:S(2)}) %collective-permute-start.65) | collective-permute-done | bytes 524320 | tf_op jit(solution)/shard_map/ppermute | solution.py:47
  (389 shorter events, 330.4 us)
Async XLA Ops:
  7.2 97.8 %all-gather.5.cloned.1.call-start = ((), (), s32[]{:S(2)}) async-start(), calls=%async_computation.5 | async-start | bytes 9437184 | tf_op jit(solution)/shard_map/all_gather | solution.py:452
  19.7 114.8 %all-gather.7.cloned.1.call-start = ((), (), s32[]{:S(2)}) async-start(), calls=%async_computation.6 | async-start | bytes 2359296 | tf_op jit(solution)/shard_map/all_gather | solution.py:452
  24.7 26.3 %collective-permute-start = (bf16[256,2048]{1,0:T(8,128)(2,1)}, bf16[256,2048]{1,0:T(8,128)(2,1)S(1)}, u32[]{:S(2)}, u32[]{:S(2)}) collective-permute-start(bf16[256,2048]{1,0:T(8,128)(2,1)} %get-tuple-element.118), channel_id=1, source_target_pairs={{0,8},{8,0},{16,24},{24,16},{1,9},{9,1},{17,25},{25,17},{2,10},{10... | collective-permute-start | bytes 3145736 | tf_op jit(solution)/shard_map/ppermute | solution.py:47
  27.6 26.9 %collective-permute-start.1 = (bf16[256,2048]{1,0:T(8,128)(2,1)}, bf16[256,2048]{1,0:T(8,128)(2,1)}, u32[]{:S(2)}, u32[]{:S(2)}) collective-permute-start(bf16[256,2048]{1,0:T(8,128)(2,1)} %get-tuple-element.118), channel_id=1, source_target_pairs={{0,16},{8,24},{16,0},{24,8},{1,17},{9,25},{17,1},{25,9},{2,18},{10... | collective-permute-start | bytes 3145736 | tf_op jit(solution)/shard_map/ppermute | solution.py:47
  70.8 202.7 %all-gather.11.cloned.1.call-start = ((), (), s32[]{:S(2)}) async-start(), calls=%async_computation.8 | async-start | bytes 12976128 | tf_op jit(solution)/shard_map/all_gather | solution.py:452
  82.6 226.6 %all-gather.9.cloned.1.call-start = ((), (), s32[]{:S(2)}) async-start(), calls=%async_computation.7 | async-start | bytes 6488064 | tf_op jit(solution)/shard_map/all_gather | solution.py:452
  137.6 25.6 %collective-permute-start.7 = (bf16[256,2048]{1,0:T(8,128)(2,1)}, bf16[256,2048]{1,0:T(8,128)(2,1)}, u32[]{:S(2)}, u32[]{:S(2)}) collective-permute-start(bf16[256,2048]{1,0:T(8,128)(2,1)} %get-tuple-element.152), channel_id=1, source_target_pairs={{0,8},{8,0},{16,24},{24,16},{1,9},{9,1},{17,25},{25,17},{2,10},{10... | collective-permute-start | bytes 3145736 | tf_op jit(solution)/shard_map/ppermute | solution.py:47
  143.4 41.4 %collective-permute-start.14 = (bf16[256,2048]{1,0:T(8,128)(2,1)}, bf16[256,2048]{1,0:T(8,128)(2,1)S(1)}, u32[]{:S(2)}, u32[]{:S(2)}) collective-permute-start(bf16[256,2048]{1,0:T(8,128)(2,1)} %param.29), channel_id=1, source_target_pairs={{0,8},{8,0},{16,24},{24,16},{1,9},{9,1},{17,25},{25,17},{2,10},{10... | collective-permute-start | bytes 3145736 | tf_op jit(solution)/shard_map/ppermute | solution.py:47
  144.0 42.9 %collective-permute-start.15 = (bf16[256,2048]{1,0:T(8,128)(2,1)}, bf16[256,2048]{1,0:T(8,128)(2,1)S(1)}, u32[]{:S(2)}, u32[]{:S(2)}) collective-permute-start(bf16[256,2048]{1,0:T(8,128)(2,1)} %param.29), channel_id=1, source_target_pairs={{0,16},{8,24},{16,0},{24,8},{1,17},{9,25},{17,1},{25,9},{2,18},{10... | collective-permute-start | bytes 3145736 | tf_op jit(solution)/shard_map/ppermute | solution.py:47
  195.9 31.2 %collective-permute-start.10 = (bf16[128,2048]{1,0:T(8,128)(2,1)}, bf16[128,2048]{1,0:T(8,128)(2,1)}, u32[]{:S(2)}, u32[]{:S(2)}) collective-permute-start(bf16[128,2048]{1,0:T(8,128)(2,1)} %get-tuple-element.140), channel_id=1, source_target_pairs={{0,8},{8,0},{16,24},{24,16},{1,9},{9,1},{17,25},{25,17},{2,10},{10... | collective-permute-start | bytes 1572872 | tf_op jit(solution)/shard_map/ppermute | solution.py:47
  198.3 28.7 %collective-permute-start.12 = (bf16[128,2048]{1,0:T(8,128)(2,1)}, bf16[128,2048]{1,0:T(8,128)(2,1)}, u32[]{:S(2)}, u32[]{:S(2)}) collective-permute-start(bf16[128,2048]{1,0:T(8,128)(2,1)} %get-tuple-element.139), channel_id=1, source_target_pairs={{0,16},{8,24},{16,0},{24,8},{1,17},{9,25},{17,1},{25,9},{2,18},{10... | collective-permute-start | bytes 1572872 | tf_op jit(solution)/shard_map/ppermute | solution.py:47
  207.4 194.7 %reduce-scatter.6.cloned.1.call-start = ((), (), s32[]{:S(2)}) async-start(), calls=%async_computation.9 | async-start | bytes 6488064 | tf_op jit(solution)/shard_map/reduce_scatter | solution.py:455
  232.4 23.6 %collective-permute-start.18 = (bf16[256,2048]{1,0:T(8,128)(2,1)S(1)}, bf16[256,2048]{1,0:T(8,128)(2,1)S(1)}, u32[]{:S(2)}, u32[]{:S(2)}) collective-permute-start(bf16[256,2048]{1,0:T(8,128)(2,1)S(1)} %get-tuple-element.114), channel_id=1, source_target_pairs={{0,8},{8,0},{16,24},{24,16},{1,9},{9,1},{17,25},{25,17},{2,10},{10... | collective-permute-start | bytes 3145736 | tf_op jit(solution)/shard_map/ppermute | solution.py:47
  233.6 24.7 %collective-permute-start.19 = (bf16[256,2048]{1,0:T(8,128)(2,1)S(1)}, bf16[256,2048]{1,0:T(8,128)(2,1)S(1)}, u32[]{:S(2)}, u32[]{:S(2)}) collective-permute-start(bf16[256,2048]{1,0:T(8,128)(2,1)S(1)} %get-tuple-element.114), channel_id=1, source_target_pairs={{0,16},{8,24},{16,0},{24,8},{1,17},{9,25},{17,1},{25,9},{2,18},{10... | collective-permute-start | bytes 3145736 | tf_op jit(solution)/shard_map/ppermute | solution.py:47
  306.6 216.4 %reduce-scatter.8.cloned.1.call-start = ((), (), s32[]{:S(2)}) async-start(), calls=%async_computation.10 | async-start | bytes 12976128 | tf_op jit(solution)/shard_map/reduce_scatter | solution.py:455
  358.2 229.2 %reduce-scatter.10.cloned.1.call-start = ((), (), s32[]{:S(2)}) async-start(), calls=%async_computation.11 | async-start | bytes 2359296 | tf_op jit(solution)/shard_map/reduce_scatter | solution.py:455
  363.2 24.6 %collective-permute-start.22 = (bf16[128,2048]{1,0:T(8,128)(2,1)S(1)}, bf16[128,2048]{1,0:T(8,128)(2,1)S(1)}, u32[]{:S(2)}, u32[]{:S(2)}) collective-permute-start(bf16[128,2048]{1,0:T(8,128)(2,1)S(1)} %get-tuple-element.138), channel_id=1, source_target_pairs={{0,8},{8,0},{16,24},{24,16},{1,9},{9,1},{17,25},{25,17},{2,10},{10... | collective-permute-start | bytes 1572872 | tf_op jit(solution)/shard_map/ppermute | solution.py:47
  363.8 24.0 %collective-permute-start.27 = (bf16[128,2048]{1,0:T(8,128)(2,1)S(1)}, bf16[128,2048]{1,0:T(8,128)(2,1)S(1)}, u32[]{:S(2)}, u32[]{:S(2)}) collective-permute-start(bf16[128,2048]{1,0:T(8,128)(2,1)S(1)} %get-tuple-element.136), channel_id=1, source_target_pairs={{0,16},{8,24},{16,0},{24,8},{1,17},{9,25},{17,1},{25,9},{2,18},{10... | collective-permute-start | bytes 1572872 | tf_op jit(solution)/shard_map/ppermute | solution.py:47
  402.1 24.5 %collective-permute-start.28 = (bf16[256,2048]{1,0:T(8,128)(2,1)}, bf16[256,2048]{1,0:T(8,128)(2,1)S(1)}, u32[]{:S(2)}, u32[]{:S(2)}) collective-permute-start(bf16[256,2048]{1,0:T(8,128)(2,1)} %get-tuple-element.74), channel_id=1, source_target_pairs={{0,8},{8,0},{16,24},{24,16},{1,9},{9,1},{17,25},{25,17},{2,10},{10... | collective-permute-start | bytes 3145736 | tf_op jit(solution)/shard_map/ppermute | solution.py:47
  403.6 24.3 %collective-permute-start.29 = (bf16[256,2048]{1,0:T(8,128)(2,1)}, bf16[256,2048]{1,0:T(8,128)(2,1)S(1)}, u32[]{:S(2)}, u32[]{:S(2)}) collective-permute-start(bf16[256,2048]{1,0:T(8,128)(2,1)} %get-tuple-element.74), channel_id=1, source_target_pairs={{0,16},{8,24},{16,0},{24,8},{1,17},{9,25},{17,1},{25,9},{2,18},{10... | collective-permute-start | bytes 3145736 | tf_op jit(solution)/shard_map/ppermute | solution.py:47
  461.8 24.9 %collective-permute-start.36 = (bf16[16,144,128]{2,1,0:T(8,128)(2,1)S(1)}, bf16[16,144,128]{2,1,0:T(8,128)(2,1)}, u32[]{:S(2)}, u32[]{:S(2)}) collective-permute-start(bf16[16,144,128]{2,1,0:T(8,128)(2,1)S(1)} %shard_map.259), channel_id=1, source_target_pairs={{2,0},{6,4},{10,8},{14,12},{18,16},{22,20},{26,24},{30,28}} | collective-permute-start | bytes 1769480 | tf_op jit(solution)/shard_map/ppermute | solution.py:365
  463.4 26.6 %collective-permute-start.33 = (bf16[128,2048]{1,0:T(8,128)(2,1)}, bf16[128,2048]{1,0:T(8,128)(2,1)S(1)}, u32[]{:S(2)}, u32[]{:S(2)}) collective-permute-start(bf16[128,2048]{1,0:T(8,128)(2,1)} %get-tuple-element.130), channel_id=1, source_target_pairs={{0,8},{8,0},{16,24},{24,16},{1,9},{9,1},{17,25},{25,17},{2,10},{10... | collective-permute-start | bytes 1572872 | tf_op jit(solution)/shard_map/ppermute | solution.py:47
  463.9 26.0 %collective-permute-start.39 = (bf16[128,2048]{1,0:T(8,128)(2,1)}, bf16[128,2048]{1,0:T(8,128)(2,1)S(1)}, u32[]{:S(2)}, u32[]{:S(2)}) collective-permute-start(bf16[128,2048]{1,0:T(8,128)(2,1)} %get-tuple-element.127), channel_id=1, source_target_pairs={{0,16},{8,24},{16,0},{24,8},{1,17},{9,25},{17,1},{25,9},{2,18},{10... | collective-permute-start | bytes 1572872 | tf_op jit(solution)/shard_map/ppermute | solution.py:47
  488.6 29.8 %collective-permute-start.41 = (bf16[256,2048]{1,0:T(8,128)(2,1)S(1)}, bf16[256,2048]{1,0:T(8,128)(2,1)S(1)}, u32[]{:S(2)}, u32[]{:S(2)}) collective-permute-start(bf16[256,2048]{1,0:T(8,128)(2,1)S(1)} %bitcast.96), channel_id=1, source_target_pairs={{0,8},{8,0},{16,24},{24,16},{1,9},{9,1},{17,25},{25,17},{2,10},{10... | collective-permute-start | bytes 3145736 | tf_op jit(solution)/shard_map/ppermute | solution.py:47
  520.9 178.8 %reduce-scatter.14.cloned.1.call-start = ((), (), s32[]{:S(2)}) async-start(), calls=%async_computation.13 | async-start | bytes 4718592 | tf_op jit(solution)/shard_map/reduce_scatter | solution.py:455
  525.8 23.9 %collective-permute-start.42 = (bf16[256,1408]{1,0:T(8,128)(2,1)}, bf16[256,1408]{1,0:T(8,128)(2,1)}, u32[]{:S(2)}, u32[]{:S(2)}) collective-permute-start(bf16[256,1408]{1,0:T(8,128)(2,1)} %get-tuple-element.156), channel_id=1, source_target_pairs={{0,8},{8,0},{16,24},{24,16},{1,9},{9,1},{17,25},{25,17},{2,10},{10... | collective-permute-start | bytes 2162696 | tf_op jit(solution)/shard_map/ppermute | solution.py:47
  557.6 144.2 %reduce-scatter.12.cloned.1.call-start = ((), (), s32[]{:S(2)}) async-start(), calls=%async_computation.12 | async-start | bytes 4718592 | tf_op jit(solution)/shard_map/reduce_scatter | solution.py:455
  601.6 25.3 %collective-permute-start.47 = (bf16[128,2048]{1,0:T(8,128)(2,1)S(1)}, bf16[128,2048]{1,0:T(8,128)(2,1)S(1)}, u32[]{:S(2)}, u32[]{:S(2)}) collective-permute-start(bf16[128,2048]{1,0:T(8,128)(2,1)S(1)} %get-tuple-element.124), channel_id=1, source_target_pairs={{0,16},{8,24},{16,0},{24,8},{1,17},{9,25},{17,1},{25,9},{2,18},{10... | collective-permute-start | bytes 1572872 | tf_op jit(solution)/shard_map/ppermute | solution.py:47
  602.5 25.4 %collective-permute-start.49 = (bf16[128,2048]{1,0:T(8,128)(2,1)S(1)}, bf16[128,2048]{1,0:T(8,128)(2,1)S(1)}, u32[]{:S(2)}, u32[]{:S(2)}) collective-permute-start(bf16[128,2048]{1,0:T(8,128)(2,1)S(1)} %get-tuple-element.123), channel_id=1, source_target_pairs={{0,8},{8,0},{16,24},{24,16},{1,9},{9,1},{17,25},{25,17},{2,10},{10... | collective-permute-start | bytes 1572872 | tf_op jit(solution)/shard_map/ppermute | solution.py:47
  614.9 41.2 %collective-permute-start.46 = (bf16[128,2048]{1,0:T(8,128)(2,1)}, bf16[128,2048]{1,0:T(8,128)(2,1)S(1)}, u32[]{:S(2)}, u32[]{:S(2)}) collective-permute-start(bf16[128,2048]{1,0:T(8,128)(2,1)} %get-tuple-element.121), channel_id=1, source_target_pairs={{0,8},{8,0},{16,24},{24,16},{1,9},{9,1},{17,25},{25,17},{2,10},{10... | collective-permute-start | bytes 1572872 | tf_op jit(solution)/shard_map/ppermute | solution.py:47
  623.4 32.7 %collective-permute-start.51 = (bf16[128,2048]{1,0:T(8,128)(2,1)S(1)}, bf16[128,2048]{1,0:T(8,128)(2,1)S(1)}, u32[]{:S(2)}, u32[]{:S(2)}) collective-permute-start(bf16[128,2048]{1,0:T(8,128)(2,1)S(1)} %get-tuple-element.122), channel_id=1, source_target_pairs={{0,16},{8,24},{16,0},{24,8},{1,17},{9,25},{17,1},{25,9},{2,18},{10... | collective-permute-start | bytes 1572872 | tf_op jit(solution)/shard_map/ppermute | solution.py:47
  628.2 27.9 %collective-permute-start.48 = (bf16[128,2048]{1,0:T(8,128)(2,1)S(1)}, bf16[128,2048]{1,0:T(8,128)(2,1)S(1)}, u32[]{:S(2)}, u32[]{:S(2)}) collective-permute-start(bf16[128,2048]{1,0:T(8,128)(2,1)S(1)} %get-tuple-element.125), channel_id=1, source_target_pairs={{0,8},{8,0},{16,24},{24,16},{1,9},{9,1},{17,25},{25,17},{2,10},{10... | collective-permute-start | bytes 1572872 | tf_op jit(solution)/shard_map/ppermute | solution.py:47
  (99 other events, 1333.0 us)
Sparse Core Ops, SparseCore 0:
  19.8 85.1 all-gather.4
  107.2 27.2 all-gather.6
  136.7 112.7 all-gather.10
  251.5 57.6 all-gather.8
  312.0 63.5 reduce-scatter.5
  377.7 123.9 reduce-scatter.7
  521.0 34.3 reduce-scatter.9
  557.7 48.7 reduce-scatter.13
  608.8 48.1 reduce-scatter.11

commit v3 on v2

--- a/solution.py
+++ b/solution.py
@@ -47,11 +47,18 @@
     return lax.ppermute(value, "dp", [(s, s ^ bits) for s in range(count)])
 
 
-def gather_parts(own):
+def gather_begin(own):
+    return own, swap(own, 1), swap(own, 2)
+
+
+def gather_end(own, one, two):
     half = own.shape[0] // 2
-    one, two = swap(own, 1), swap(own, 2)
     top, bottom = swap(one[:half], 2), swap(two[half:], 1)
     return own, one, two, top, bottom
+
+
+def gather_parts(own):
+    return gather_end(*gather_begin(own))
 
 
 def gather_dp(own):
@@ -344,17 +351,85 @@
     )(*scalars, *args)
 
 
+def columns_kernel(left_ref, right_ref, out_ref):
+    out_ref[...] = mm(left_ref[...], right_ref[...])
+
+
+def columns(left, right, first, count):
+    rows, depth = left.shape
+    return call(
+        columns_kernel, (count,), (),
+        [
+            pl.BlockSpec((rows, depth), lambda n: (0, 0)),
+            pl.BlockSpec((depth, 256), lambda n: (0, n + first)),
+        ],
+        pl.BlockSpec((rows, 256), lambda n: (0, n)),
+        jax.ShapeDtypeStruct((rows, 256 * count), F32), (left, right), 2e9 * count,
+    )
+
+
+def rows_kernel(left_ref, right_ref, beside_ref, gain_ref, out_ref, sum_ref):
+    out = dot_last(left_ref[...], right_ref[...])
+    out_ref[...] = out.astype(BF)
+    sum_ref[...] = jnp.sum(out * beside_ref[...].astype(F32), axis=0, keepdims=True) / gain_ref[...]
+
+
+def against_rows(left, right, beside, gain):
+    rows, depth = left.shape
+    wide = right.shape[0]
+    block = pl.BlockSpec((rows, 256), lambda n: (0, n))
+    line = pl.BlockSpec((1, 256), lambda n: (0, n))
+    return call(
+        rows_kernel, (wide // 256,), (),
+        [
+            pl.BlockSpec((rows, depth), lambda n: (0, 0)),
+            pl.BlockSpec((256, depth), lambda n: (n, 0)),
+            block,
+            line,
+        ],
+        [block, line],
+        [jax.ShapeDtypeStruct((rows, wide), BF), jax.ShapeDtypeStruct((1, wide), F32)],
+        (left, right, beside, gain), 8e9,
+    )
+
+
 def join(near, far):
     pairs = near.shape[0]
     block = pl.BlockSpec((pairs // 2,) + near.shape[1:], lambda s: (s, 0, 0))
     return call(join_kernel, (2,), (), [block, block], block, jax.ShapeDtypeStruct(near.shape, BF), (near, far))
 
 
+def pick_kernel(heads, place, *refs):
+    *mats, last, out = refs
+    k = pl.program_id(0)
+    half, wide = last.shape[0], out.shape[1] - 4 * heads * 128
+    for n, mat in enumerate(mats):
+        out[:, pl.ds(pl.multiple_of((n * heads + k) * 128, 128), 128)] = mat[...]
+
+    @pl.when(k == 0)
+    def _():
+        for n in range(4):
+            out[half * n : half * (n + 1), 4 * heads * 128 :] = last[:, wide * n : wide * (n + 1)]
+
+
+def picked(mats, last, heads):
+    dp = lax.axis_index("dp")
+    place = jnp.stack([(dp & 1) * 2 * heads + (dp >> 1), dp]).astype(jnp.int32)
+    rows, width = mats[0].shape
+    column = pl.BlockSpec((rows, 128), lambda k, place: (0, place[0] + 2 * k))
+    return call(
+        functools.partial(pick_kernel, heads), (heads,), (place,),
+        [column] * 4 + [pl.BlockSpec((rows // 4, width), lambda k, place: (place[1], 0))],
+        pl.BlockSpec((rows, width + width // 4), lambda k, place: (0, 0)),
+        jax.ShapeDtypeStruct((rows, width + width // 4), BF), (*mats, last),
+    )
+
+
 def equal_halves(tokens):
     return lax.axis_size("seq") * tokens == 2 * MIN_LEN and MIN_LEN == 4 * tokens
 
 
-def reached(pack, forward, tokens):
+def reached(pack, forward, tokens, beside):
     count = lax.axis_size("seq")
     place = lax.axis_index("seq")
     if equal_halves(tokens):
@@ -368,11 +443,11 @@
 
         near = hop(pack, ((0, 1), (2, 3)))
         pair = join(pack, near)
-        third = hop(pair, ((1, 3),))
+        third = later(hop(pair, ((1, 3),)), beside(pair))
         second = hop(third, ((3, 2),))
         far = jnp.where((place & 3) == order[3], third, second)
         there = (place & 1) == (order[1] & 1)
-        return near, far, there.astype(jnp.int32)[None], (pair, third)
+        return near, far, there.astype(jnp.int32)[None]
     every = lax.all_gather(pack, "seq")
     shape = (pack.shape[0], 128, pack.shape[2])
 
@@ -384,7 +459,8 @@
 
     total = lax.fori_loop(0, count, one, jnp.zeros(shape, F32))
     total = jnp.concatenate([total, jnp.zeros_like(total[:, :16])], axis=1).astype(BF)
-    return total, jnp.zeros_like(total), jnp.ones((1,), jnp.int32), (total, total)
+    total = later(total, beside(total))
+    return total, jnp.zeros_like(total), jnp.ones((1,), jnp.int32)
 
 
 def everywhere(value):
@@ -459,7 +535,13 @@
         full = gather_dp(value)
         return [full[k * rows : (k + 1) * rows] for k in range(4)]
 
-    w4 = gather_seq(jnp.concatenate([of_heads(w, 1) for w in (w_f, w_i, w_q, w_g)], axis=1))
+    natural = w_o.shape[0] == 2 * head_dim
+    if natural:
+        both = gather_seq(picked((w_f, w_i, w_q, w_g), w_o, heads))
+        halves = both[:, width:].reshape(seqs, 4, head_dim // 2, mine)
+        halves = halves.transpose(0, 2, 1, 3).reshape(-1, width)
+    else:
+        both = gather_seq(jnp.concatenate([of_heads(w, 1) for w in (w_f, w_i, w_q, w_g)], axis=1))
 
     x = block_input.astype(F32)
     r1 = lax.rsqrt(jnp.mean(x * x, axis=-1, keepdims=True) + EPS)
@@ -473,21 +555,11 @@
         starts = jnp.stack([starts] + [swap(starts, k) for k in (1, 2, 3)])
         h = later(h, starts)
     h_all = gather_dp(h)
-    w_o, out_own = later((w_o, out_grad), h_all)
-    natural = w_o.shape[0] == 2 * head_dim
-    if natural:
-        part = lax.dynamic_slice_in_dim(w_o, dp * (head_dim // 2), head_dim // 2, 0)
-        wo = gather_seq(part)
-    else:
-        wo = of_heads(gather_seq(w_o), 0)
-
-    og_all = gather_dp(out_own)
-    z = mm(h_all, w4)
+    og_all = gather_dp(later(out_grad, h_all))
+    blocks = 2 * mine // 256
+    z_fv = columns(h_all, later(both, og_all), 0, blocks)
     w_gate, w_up = later((w_gate, w_up), h_all)
     wgu = gather_seq(jnp.concatenate([of_hidden(w_gate), of_hidden(w_up)], axis=1))
-    w_down = later(w_down, z)
-    wd = gather_seq(lax.dynamic_slice_in_dim(w_down, dp * chunk, chunk, 0))
-
     bound = of_heads(lower_bound, 0)[None]
     gain = group_gain[None]
 
@@ -498,33 +570,46 @@
     thin = jax.ShapeDtypeStruct((rows, mine), BF)
     packed = jax.ShapeDtypeStruct((pairs, 144, 128), BF)
     one = across(tokens, mine)
-    fl, vl, ql, gl = (across(tokens, mine, k) for k in range(4))
+    fl, vl = ql, gl = across(tokens, mine, 0), across(tokens, mine, 1)
     pack_spec, state_spec = states(144, heads), states(128, heads)
 
     pack = call(
         functools.partial(end_kernel, count, heads), grid, (starts,),
-        [fl, vl, fixed(mine)], pack_spec, packed, (z, z, bound), 2e9,
-    )
-    near, far, whole, _ = reached(pack, True, tokens)
-    intra, qs = call(
-        functools.partial(intra_kernel, count, heads), grid, (starts,),
-        [fl, vl, ql, fixed(mine)], [one, one], [wide, thin], (z, z, z, bound), 3e9,
-    )
-    if natural:
-        halves = later(wo, pack)
-        own = lax.dynamic_slice_in_dim(halves, low_bit * (mine // 2), mine // 2, 0)
-        give = lax.dynamic_slice_in_dim(halves, (1 - low_bit) * (mine // 2), mine // 2, 0)
-        wo = pair_halves(own, swap(give, 1), low_bit, heads)
+        [fl, vl, fixed(mine)], pack_spec, packed, (z_fv, z_fv, bound), 2e9,
+    )
+    def within(pair):
+        if natural:
+            own = lax.dynamic_slice_in_dim(halves, low_bit * (mine // 2), mine // 2, 0)
+            give = lax.dynamic_slice_in_dim(halves, (1 - low_bit) * (mine // 2), mine // 2, 0)
+            give = later(give, pair)
+            got = swap(give, 1)
+            wo = pair_halves(own, got, low_bit, heads)
+        else:
+            wo = of_heads(gather_seq(w_o), 0)
+            got = give = wo
+        z_qg = columns(h_all, later(both, give), blocks, blocks)
+        intra, qs = call(
+            functools.partial(intra_kernel, count, heads), grid, (starts,),
+            [fl, vl, ql, fixed(mine)], [one, one], [wide, thin],
+            (z_fv, z_fv, later(z_qg, got), bound), 3e9,
+        )
+        kept.extend((wo, z_qg, intra, qs))
+        return intra
+
+    kept = []
+    near, far, whole = reached(pack, True, tokens, within)
+    wo, z_qg, intra, qs = kept
+    w_down = later(w_down, z_qg)
+    wd = gather_seq(lax.dynamic_slice_in_dim(w_down, dp * chunk, chunk, 0))
     mixed, on, enter = call(
         functools.partial(mixed_kernel, heads), grid, (whole,),
         [one, one, gl, fixed(128), pack_spec, pack_spec],
         [one, one, state_spec],
         [wide, thin, jax.ShapeDtypeStruct((pairs, 128, 128), F32)],
-        (intra, qs, z, gain, near, far),
+        (intra, qs, z_qg, gain, near, far),
     )
 
     branch = scatter_dp(mm(on, wo, BF))
-    branch, og_all = lax.optimization_barrier((branch, og_all))
     y = x + branch
     r2 = lax.rsqrt(jnp.mean(y * y, axis=-1, keepdims=True) + EPS)
     h2_all = gather_dp((y * r2 * ffn_norm_gain).astype(BF))
@@ -558,47 +643,52 @@
         [one, gl, one, one, fixed(128), pack_spec],
         [one, one, pack_spec, fixed(128)],
         [wide, thin, packed, jax.ShapeDtypeStruct((1, 128), F32)],
-        (d_on, z, mixed, qs, gain, pack),
-    )
-    near, far, whole, passed = reached(d_pack, False, tokens)
-    out_part, o_part = later((out_part, o_part), passed[0])
-    onward, at_hand = scatter_begin(out_part)
-    result = (y + scatter_end(later(onward, passed[1]), at_hand)).astype(BF)
-
-    if natural:
-        cut = o_part.reshape(heads, 2, head_dim // 2, width)
-        own = lax.dynamic_index_in_dim(cut, low_bit, 1, False).reshape(mine // 2, width)
-        give = lax.dynamic_index_in_dim(cut, 1 - low_bit, 1, False).reshape(mine // 2, width)
-        got = later(swap(give, 1), result)
-        o_full = jnp.where(
-            low_bit == 0,
-            jnp.concatenate([own, got], axis=0),
-            jnp.concatenate([got, own], axis=0),
-        )
-    else:
-        none = jnp.zeros_like(o_part)
-        o_full = to_heads([o_part, none, none, none], 0)
+        (d_on, z_qg, mixed, qs, gain, pack),
+    )
+    def moves(pair):
+        if natural:
+            cut = o_part.reshape(heads, 2, head_dim // 2, width)
+            own = lax.dynamic_index_in_dim(cut, low_bit, 1, False).reshape(mine // 2, width)
+            give = lax.dynamic_index_in_dim(cut, 1 - low_bit, 1, False).reshape(mine // 2, width)
+            got = later(swap(give, 1), pair)
+            o_full = jnp.where(
+                low_bit == 0,
+                jnp.concatenate([own, got], axis=0),
+                jnp.concatenate([got, own], axis=0),
+            )
+        else:
+            none = jnp.zeros_like(o_part)
+            o_full = got = to_heads([o_part, none, none, none], 0)
+        onward, at_hand = scatter_begin(later(out_part, got))
+        sent.extend((o_full, onward, at_hand))
+        return onward
+
+    sent = []
+    near, far, whole = reached(d_pack, False, tokens, moves)
+    o_full, onward, at_hand = sent
     o_rows = scatter_seq(o_full)
-
-    near, far = later((near, far), result, o_full, gu_rows)
+    result = (y + scatter_end(onward, at_hand)).astype(BF)
+
+    near, far = later((near, far), o_full, gu_rows)
     dz, d_bound = call(
         functools.partial(back_kernel, count, heads), grid, (starts, whole),
         [fl, vl, ql, fixed(mine), one, one, state_spec, pack_spec, pack_spec],
         [across(tokens, 4 * mine), fixed(mine)],
         [jax.ShapeDtypeStruct((rows, 4 * mine), BF), jax.ShapeDtypeStruct((1, mine), F32)],
-        (z, z, z, bound, d_gz, d_mixed, enter, near, far), 8e9,
-    )
-
-    gate_parts, up_parts = gather_parts(gu_rows[:, :ff]), gather_parts(gu_rows[:, ff:])
-    fv_part = dot_first(h_all, later(dz, gate_parts[1:3])[:, : 2 * mine], BF)
-    fv_rows = scatter_seq(fv_part)
-    h_part = dot_last(later(dz, fv_part, up_parts[1:3]), w4, BF)
-    d_h = scatter_dp(h_part)
-    dz, o_rows = later((dz, o_rows), h_part)
-    qg_part = dot_first(h_all, dz[:, 2 * mine :], BF)
-    qg_rows = scatter_seq(qg_part)
-    fv_rows = later(fv_rows, gate_parts[1:], up_parts[1:], d_h)
-    down_parts = gather_parts(later(down_rows, d_h))
+        (z_fv, z_fv, z_qg, bound, d_gz, d_mixed, enter, near, far), 8e9,
+    )
+
+    gate_parts, up_parts = gather_begin(gu_rows[:, :ff]), gather_begin(gu_rows[:, ff:])
+    z_part = dot_first(h_all, later(dz, result, gate_parts, up_parts), BF)
+    z_rows = scatter_seq(z_part)
+    h_part, d_norm_gain = against_rows(later(dz, z_part), both, h_all, norm_gain[None])
+    down_parts = gather_begin(later(down_rows, z_part))
+    h_part, down_parts = lax.optimization_barrier((h_part, down_parts))
+    onward, at_hand = scatter_begin(h_part)
+    gate_parts, up_parts, down_parts, o_rows = later((gate_parts, up_parts, down_parts, o_rows), onward)
+    gate_parts, up_parts, down_parts = (gather_end(*v) for v in (gate_parts, up_parts, down_parts))
+    d_h = scatter_end(onward, at_hand)
+    z_rows = later(z_rows, gate_parts, up_parts, down_parts, d_h)
 
     order = jnp.arange(4, dtype=jnp.int32) ^ dp.astype(jnp.int32)
 
@@ -617,7 +707,9 @@
         )
 
     if natural:
-        grad_o = jnp.concatenate(absolute(blocks_dp(o_rows)), axis=0).astype(F32)
+        o_parts = gather_parts(o_rows)
+        o_all = o_parts[:3] + (jnp.concatenate(o_parts[3:], axis=0),)
+        grad_o = jnp.concatenate(absolute(o_all), axis=0).astype(F32)
     else:
         grad_o = lax.psum(o_rows.astype(F32), "dp")
     down_all = down_parts[:3] + (jnp.concatenate(down_parts[3:], axis=0),)
@@ -626,16 +718,15 @@
     [grad_gate] = whole_rows(gate_parts, join_hidden, ff, chunk % 16 == 0)
     [grad_up] = whole_rows(up_parts, join_hidden, ff, chunk % 16 == 0)
     join_heads = functools.partial(heads_kernel, heads)
-    grad_f, grad_i = whole_rows(gather_parts(fv_rows), join_heads, mine, True)
-    grad_q, grad_g = whole_rows(gather_parts(later(qg_rows, fv_rows)), join_heads, mine, True)
-
-    d_norm_gain = jnp.sum(d_h * x * r1, axis=0)
+    grad_f, grad_i, grad_q, grad_g = whole_rows(gather_parts(z_rows), join_heads, mine, True)
+
     u1 = d_h * norm_gain
     d_x = d_y + r1 * u1 - x * (r1 * r1 * r1) * jnp.mean(u1 * x, axis=-1, keepdims=True)
 
     zero = jnp.zeros((mine,), F32)
     d_bound = to_heads([d_bound[0], zero, zero, zero], 0)
-    small = everywhere(jnp.concatenate([d_norm_gain, d_ffn_gain, d_bound, d_gain[0]]))
+    small = jnp.concatenate([d_norm_gain[0], d_ffn_gain, d_bound, d_gain[0]])
+    small = everywhere(later(small, onward))
     return (
         result,
         d_x.astype(BF),

time: 747 us -> 721 us (0.965)
  matrix products: 139 us -> 108 us
  waiting for transfers between devices: 307 us -> 277 us
  Pallas kernels: 61 us -> 90.8 us
  other arithmetic: 41.4 us -> 50.8 us
    pallas_call x11 -> x14, Pallas kernels: 61 us -> 90.8 us  [call(): pl.pallas_call(kernel, grid_spec=pltpu.PrefetchScalarGridSpec(num_scalar_...]
    all_gather x4 -> x3, waiting for transfers between devices: 28.6 us -> 0.33 us  [gather_seq(): return lax.all_gather(value, 'seq', axis=0, tiled=True)]
    dot_general x4 -> x3, matrix products: 43.9 us -> 29.2 us  [mm(): return jnp.dot(left, right, preferred_element_type=F32).astype(kind)]
    dot_general x4 -> x3, matrix products: 48.2 us -> 34.3 us  [dot_last(): lax.dot_general(left, right, (((1,), (1,)), ((), ())), preferred_element_...]
    ppermute x66 -> x62, waiting for transfers between devices: 250 us -> 240 us  [swap(): return lax.ppermute(value, 'dp', [(s, s ^ bits) for s in range(count)])]
    ppermute x66 -> x62, starting transfers between devices: 81.4 us -> 77.3 us  [swap(): return lax.ppermute(value, 'dp', [(s, s ^ bits) for s in range(count)])]
    dot_general x5 -> x4, matrix products: 47.1 us -> 44.5 us  [dot_first(): lax.dot_general(left, right, (((0,), (0,)), ((), ())), preferred_element_...]
    unnamed x125 -> x155, local copies, waits for them, and re-layouts: 41.9 us -> 39.5 us
  transfers between devices with their start and end apart: 86 -> 80, of which waited for: 47 -> 46; matrix products, arithmetic and copies ran while one was open for 31% -> 30% of each run, Pallas kernels for 8% -> 12%
where the time goes in v3:
time: 721 us; the launch traced here: 711 us
  waiting for transfers between devices  277 us (38%)
  matrix products  108 us (15%)
  starting transfers between devices  93.9 us (13%)
  Pallas kernels  90.8 us (13%)
  local copies, waits for them, and re-layouts  74.9 us (10%)
  other arithmetic  50.8 us (7%)
  between operations  15.5 us (2%)
    ppermute x62, waiting for transfers between devices, swap(): return lax.ppermute(value, 'dp', [(s, s ^ bits) for s in range(count)])  240 us
    pallas_call x14, Pallas kernels, call(): pl.pallas_call(kernel, grid_spec=pltpu.PrefetchScalarGridSpec(num_scalar_...  90.8 us
    ppermute x62, starting transfers between devices, swap(): return lax.ppermute(value, 'dp', [(s, s ^ bits) for s in range(count)])  77.3 us
    dot_general x4, matrix products, dot_first(): lax.dot_general(left, right, (((0,), (0,)), ((), ())), preferred_element_...  44.5 us
    unnamed x155, local copies, waits for them, and re-layouts  39.5 us
    dot_general x3, matrix products, dot_last(): lax.dot_general(left, right, (((1,), (1,)), ((), ())), preferred_element_...  34.3 us
    dot_general x3, matrix products, mm(): return jnp.dot(left, right, preferred_element_type=F32).astype(kind)  29.2 us
    ppermute x6, waiting for transfers between devices, hop(): lax.ppermute(value, 'seq', [(f + order[a], f + order[b]) for f in first f...  18 us
  transfers between devices with their start and end apart: 80, of which 46 were waited for; matrix products, arithmetic and copies ran while one was open for 30% of the time, Pallas kernels for 12%

profile of v3, /device:TPU:0, one launch (start us, length us, event | category | flops | bytes accessed | tf_op | source)
XLA Modules:
  0.0 711.1 jit_solution(14683306130617236927)
XLA Ops:
  25.3 21.8 %collective-permute-done = bf16[256,2048]{1,0:T(8,128)(2,1)S(1)} collective-permute-done((bf16[256,2048]{1,0:T(8,128)(2,1)}, bf16[256,2048]{1,0:T(8,128)(2,1)S(1)}, u32[]{:S(2)}, u32[]{:S(2)}) %collective-permute-start) | collective-permute-done | bytes 1048608 | tf_op jit(solution)/shard_map/ppermute | solution.py:47
  80.1 20.5 %collective-permute-done.4 = bf16[256,2048]{1,0:T(8,128)(2,1)} collective-permute-done((bf16[256,2048]{1,0:T(8,128)(2,1)}, bf16[256,2048]{1,0:T(8,128)(2,1)}, u32[]{:S(2)}, u32[]{:S(2)}) %collective-permute-start.4) | collective-permute-done | bytes 1048608 | tf_op jit(solution)/shard_map/ppermute | solution.py:47
  118.2 7.8 %shard_map.255.f_ref.v_ref = f32[1024,1024]{1,0:T(8,128)S(1)} custom-call(bf16[1024,2048]{1,0:T(8,128)(2,1)} %constant_dynamic-update-slice_fusion.left_ref.beside_ref, bf16[2048,2560]{1,0:T(8,128)(2,1)} %all-gather.4.cloned.1.call-done.right_ref), custom_call_target="tpu_custom_call" | custom-call | flops 80000000 | bytes 65536 | tf_op jit(solution)/shard_map/pallas_call | solution.py:343
  126.0 6.0 shard_map.256.near_ref.pack_ref
  144.2 7.9 %shard_map.258.q_ref.g_ref = f32[1024,1024]{1,0:T(8,128)S(1)} custom-call(bf16[1024,2048]{1,0:T(8,128)(2,1)} %constant_dynamic-update-slice_fusion.left_ref.beside_ref, bf16[2048,2560]{1,0:T(8,128)(2,1)} %all-gather.4.cloned.1.call-done.right_ref), custom_call_target="tpu_custom_call" | custom-call | flops 80000000 | bytes 65536 | tf_op jit(solution)/shard_map/pallas_call | solution.py:343
  154.0 10.9 %collective-permute-done.9 = bf16[256,2048]{1,0:T(8,128)(2,1)S(1)} collective-permute-done((bf16[256,2048]{1,0:T(8,128)(2,1)S(1)}, bf16[256,2048]{1,0:T(8,128)(2,1)S(1)}, u32[]{:S(2)}, u32[]{:S(2)}) %collective-permute-start.9) | collective-permute-done | bytes 1048608 | tf_op jit(solution)/shard_map/ppermute | solution.py:47
  164.9 11.8 %shard_map.259 = (f32[1024,512]{1,0:T(8,128)S(1)}, bf16[1024,512]{1,0:T(8,128)(2,1)S(1)}) custom-call(s32[4,2]{1,0:T(4,128)S(1)} %broadcast_in_dim.36.starts, f32[1024,1024]{1,0:T(8,128)} %copy-done.2, f32[1024,1024]{1,0:T(8,128)} %copy-done.2, f32[1024,1024]{1,0:T(8,128)} %copy-done.3, f32[1,512]{1,0:T(1,128)S(1)} %dynamic-slice_bitcast_fusion.b_ref), custom_call_target="tpu_custom_call" | custom-call | flops 30000000 | bytes 65536 | tf_op jit(solution)/shard_map/pallas_call | solution.py:343
  199.0 11.1 %collective-permute-done.13 = bf16[128,2048]{1,0:T(8,128)(2,1)} collective-permute-done((bf16[128,2048]{1,0:T(8,128)(2,1)}, bf16[128,2048]{1,0:T(8,128)(2,1)}, u32[]{:S(2)}, u32[]{:S(2)}) %collective-permute-start.13) | collective-permute-done | bytes 524320 | tf_op jit(solution)/shard_map/ppermute | solution.py:47
  222.8 7.9 %collective-permute-done.14 = bf16[128,2048]{1,0:T(8,128)(2,1)} collective-permute-done((bf16[128,2048]{1,0:T(8,128)(2,1)}, bf16[128,2048]{1,0:T(8,128)(2,1)}, u32[]{:S(2)}, u32[]{:S(2)}) %collective-permute-start.14) | collective-permute-done | bytes 524320 | tf_op jit(solution)/shard_map/ppermute | solution.py:47
  237.1 20.5 %collective-permute-done.18 = bf16[256,2048]{1,0:T(8,128)(2,1)S(1)} collective-permute-done((bf16[256,2048]{1,0:T(8,128)(2,1)S(1)}, bf16[256,2048]{1,0:T(8,128)(2,1)S(1)}, u32[]{:S(2)}, u32[]{:S(2)}) %collective-permute-start.18) | collective-permute-done | bytes 1048608 | tf_op jit(solution)/shard_map/ppermute | solution.py:47
  262.8 6.7 collective-permute-done.20
  271.2 17.3 %fusion.20 = f32[1024,2816]{1,0:T(8,128)S(1)} fusion(bf16[1024,2048]{1,0:T(8,128)(2,1)} %constant_dynamic-update-slice_fusion.10, bf16[2048,2816]{0,1:T(8,128)(2,1)} %all-gather.8.cloned.1.call-done), kind=kOutput, calls=%fused_computation.141 | convolution fusion | flops 11811160064 | bytes 27262976 | tf_op jit(solution)/shard_map/dot_general | solution.py:30
  294.3 10.7 %convolution_convert_fusion.2 = bf16[1408,2048]{1,0:T(8,128)(2,1)} fusion(bf16[1024,1408]{1,0:T(8,128)(2,1)S(1)} %multiply_convert_fusion.2, bf16[1024,2048]{1,0:T(8,128)(2,1)} %constant_dynamic-update-slice_fusion.5), kind=kOutput, calls=%fused_computation.2 | convolution fusion | flops 5908463616 | bytes 12845056 | tf_op jit(solution)/shard_map/dot_general | solution.py:34
  305.2 14.3 %multiply_convert_fusion.1 = (bf16[1024,1408]{1,0:T(8,128)(2,1)S(1)}, bf16[1024,1408]{1,0:T(8,128)(2,1)S(1)}) fusion(f32[1024,2816]{1,0:T(8,128)} %copy-done.27, bf16[1024,2048]{1,0:T(8,128)(2,1)} %constant_dynamic-update-slice_fusion.5, bf16[1408,2048]{1,0:T(8,128)(2,1)} %all-gather.6.cloned.1.call-done), kind=kOutput, calls=%fused_computation.5 | convolution fusion | flops 5924323328 | bytes 27262976 | tf_op jit(solution)/shard_map/dot_general | solution.py:40
  319.9 16.3 %convolution_convert_fusion.3 = bf16[1024,2048]{1,0:T(8,128)(2,1)} fusion(bf16[2048,2816]{0,1:T(8,128)(2,1)} %all-gather.8.cloned.1.call-done, bf16[1024,1408]{1,0:T(8,128)(2,1)S(1)} %get-tuple-element.145, bf16[1024,1408]{1,0:T(8,128)(2,1)S(1)} %get-tuple-element.144), kind=kOutput, calls=%fused_computation.14 | convolution fusion | flops 11824791552 | bytes 21495808 | tf_op jit(solution)/shard_map/dot_general | solution.py:40
  336.3 17.9 %convolution_convert_fusion = bf16[2048,2816]{1,0:T(8,128)(2,1)} fusion(bf16[1024,2048]{1,0:T(8,128)(2,1)} %constant_dynamic-update-slice_fusion.10, bf16[1024,2816]{1,0:T(8,128)(2,1)S(1)} %pad_maximum_fusion), kind=kOutput, calls=%fused_computation | convolution fusion | flops 11816927232 | bytes 21495808 | tf_op jit(solution)/shard_map/dot_general | solution.py:34
  361.3 10.8 %collective-permute-done.23 = bf16[128,2048]{1,0:T(8,128)(2,1)S(1)} collective-permute-done((bf16[128,2048]{1,0:T(8,128)(2,1)S(1)}, bf16[128,2048]{1,0:T(8,128)(2,1)S(1)}, u32[]{:S(2)}, u32[]{:S(2)}) %collective-permute-start.23) | collective-permute-done | bytes 524320 | tf_op jit(solution)/shard_map/ppermute | solution.py:47
  377.6 6.2 collective-permute-done.22
  383.8 7.6 %collective-permute-done.24 = bf16[128,2048]{1,0:T(8,128)(2,1)} collective-permute-done((bf16[128,2048]{1,0:T(8,128)(2,1)}, bf16[128,2048]{1,0:T(8,128)(2,1)}, u32[]{:S(2)}, u32[]{:S(2)}) %collective-permute-start.24) | collective-permute-done | bytes 524320 | tf_op jit(solution)/shard_map/ppermute | solution.py:47
  398.8 9.6 %convolution_convert_fusion.4 = bf16[1024,2048]{1,0:T(8,128)(2,1)S(1)} fusion(bf16[1024,1408]{1,0:T(8,128)(2,1)} %copy-done.33, bf16[1408,2048]{1,0:T(8,128)(2,1)} %all-gather.6.cloned.1.call-done), kind=kOutput, calls=%fused_computation.15 | convolution fusion | flops 5907677184 | bytes 12845056 | tf_op jit(solution)/shard_map/dot_general | solution.py:30
  408.4 11.5 %collective-permute-done.28 = bf16[256,2048]{1,0:T(8,128)(2,1)S(1)} collective-permute-done((bf16[256,2048]{1,0:T(8,128)(2,1)}, bf16[256,2048]{1,0:T(8,128)(2,1)S(1)}, u32[]{:S(2)}, u32[]{:S(2)}) %collective-permute-start.28) | collective-permute-done | bytes 1048608 | tf_op jit(solution)/shard_map/ppermute | solution.py:47
  424.1 6.1 collective-permute-done.30
  450.9 5.5 collective-permute-done.32
  465.7 7.2 %collective-permute-done.35 = bf16[128,2048]{1,0:T(8,128)(2,1)} collective-permute-done((bf16[128,2048]{1,0:T(8,128)(2,1)}, bf16[128,2048]{1,0:T(8,128)(2,1)}, u32[]{:S(2)}, u32[]{:S(2)}) %collective-permute-start.35) | collective-permute-done | bytes 524320 | tf_op jit(solution)/shard_map/ppermute | solution.py:47
  479.9 15.3 %collective-permute-done.40 = bf16[16,144,128]{2,1,0:T(8,128)(2,1)} collective-permute-done((bf16[16,144,128]{2,1,0:T(8,128)(2,1)S(1)}, bf16[16,144,128]{2,1,0:T(8,128)(2,1)}, u32[]{:S(2)}, u32[]{:S(2)}) %collective-permute-start.40) | collective-permute-done | bytes 589856 | tf_op jit(solution)/shard_map/ppermute | solution.py:440
  512.3 16.4 %shard_map.263 = (bf16[1024,2048]{1,0:T(8,128)(2,1)}, f32[1,512]{1,0:T(1,128)S(1)}) custom-call(s32[4,2]{1,0:T(4,128)S(1)} %broadcast_in_dim.36.starts, s32[1]{0:T(128)} %bitcast.20.whole, f32[1024,1024]{1,0:T(8,128)} %copy-done.2, f32[1024,1024]{1,0:T(8,128)} %copy-done.2, f32[1024,1024]{1,0:T(8,128)} %copy-done.3, ...), custom_call_target="tpu_custom_call" | custom-call | flops 80000000 | bytes 65536 | tf_op jit(solution)/shard_map/pallas_call | solution.py:343
  528.7 5.8 collective-permute-done.44
  536.6 13.5 %convolution_convert_fusion.1 = bf16[2048,2048]{1,0:T(8,128)(2,1)} fusion(bf16[1024,2048]{1,0:T(8,128)(2,1)S(1)} %copy-done.25, bf16[1024,2048]{1,0:T(8,128)(2,1)} %get-tuple-element.105.left_ref), kind=kOutput, calls=%fused_computation.1 | convolution fusion | flops 8594128896 | bytes 16777216 | tf_op jit(solution)/shard_map/dot_general | solution.py:34
  553.2 14.8 %shard_map.264 = (bf16[1024,2048]{1,0:T(8,128)(2,1)S(1)}, f32[1,2048]{1,0:T(1,128)S(1)}) custom-call(bf16[1024,2048]{1,0:T(8,128)(2,1)} %get-tuple-element.105.left_ref, bf16[2048,2560]{1,0:T(8,128)(2,1)} %all-gather.4.cloned.1.call-done.right_ref, bf16[1024,2048]{1,0:T(8,128)(2,1)} %constant_dynamic-update-slice_fusion.left_ref.beside_ref, ...), custom_call_target="tpu_custom_call" | custom-call | flops 80000000 | bytes 65536 | tf_op jit(solution)/shard_map/pallas_call | solution.py:343
  571.4 7.3 %collective-permute-done.49 = bf16[128,2048]{1,0:T(8,128)(2,1)S(1)} collective-permute-done((bf16[128,2048]{1,0:T(8,128)(2,1)S(1)}, bf16[128,2048]{1,0:T(8,128)(2,1)S(1)}, u32[]{:S(2)}, u32[]{:S(2)}) %collective-permute-start.49) | collective-permute-done | bytes 524320 | tf_op jit(solution)/shard_map/ppermute | solution.py:47
  616.5 6.0 collective-permute-done.62
  671.3 13.2 %collective-permute-done.65 = bf16[256,2048]{1,0:T(8,128)(2,1)S(1)} collective-permute-done((bf16[256,2048]{1,0:T(8,128)(2,1)}, bf16[256,2048]{1,0:T(8,128)(2,1)S(1)}, u32[]{:S(2)}, u32[]{:S(2)}) %collective-permute-start.65) | collective-permute-done | bytes 1048608 | tf_op jit(solution)/shard_map/ppermute | solution.py:47
  (402 shorter events, 329.3 us)
Async XLA Ops:
  7.2 111.0 %all-gather.4.cloned.1.call-start = ((), (), s32[]{:S(2)}) async-start(), calls=%async_computation.4 | async-start | bytes 11796480 | tf_op jit(solution)/shard_map/all_gather | solution.py:528
  15.9 255.3 %all-gather.8.cloned.1.call-start = ((), (), s32[]{:S(2)}) async-start(), calls=%async_computation.6 | async-start | bytes 12976128 | tf_op jit(solution)/shard_map/all_gather | solution.py:528
  20.9 26.3 %collective-permute-start = (bf16[256,2048]{1,0:T(8,128)(2,1)}, bf16[256,2048]{1,0:T(8,128)(2,1)S(1)}, u32[]{:S(2)}, u32[]{:S(2)}) collective-permute-start(bf16[256,2048]{1,0:T(8,128)(2,1)} %get-tuple-element.143), channel_id=1, source_target_pairs={{0,8},{8,0},{16,24},{24,16},{1,9},{9,1},{17,25},{25,17},{2,10},{10... | collective-permute-start | bytes 3145736 | tf_op jit(solution)/shard_map/ppermute | solution.py:47
  23.8 26.9 %collective-permute-start.1 = (bf16[256,2048]{1,0:T(8,128)(2,1)}, bf16[256,2048]{1,0:T(8,128)(2,1)}, u32[]{:S(2)}, u32[]{:S(2)}) collective-permute-start(bf16[256,2048]{1,0:T(8,128)(2,1)} %get-tuple-element.143), channel_id=1, source_target_pairs={{0,16},{8,24},{16,0},{24,8},{1,17},{9,25},{17,1},{25,9},{2,18},{10... | collective-permute-start | bytes 3145736 | tf_op jit(solution)/shard_map/ppermute | solution.py:47
  77.2 228.0 %all-gather.6.cloned.1.call-start = ((), (), s32[]{:S(2)}) async-start(), calls=%async_computation.5 | async-start | bytes 6488064 | tf_op jit(solution)/shard_map/all_gather | solution.py:528
  78.8 26.1 %collective-permute-start.5 = (bf16[256,2048]{1,0:T(8,128)(2,1)}, bf16[256,2048]{1,0:T(8,128)(2,1)}, u32[]{:S(2)}, u32[]{:S(2)}) collective-permute-start(bf16[256,2048]{1,0:T(8,128)(2,1)} %param.29), channel_id=1, source_target_pairs={{0,16},{8,24},{16,0},{24,8},{1,17},{9,25},{17,1},{25,9},{2,18},{10... | collective-permute-start | bytes 3145736 | tf_op jit(solution)/shard_map/ppermute | solution.py:47
  141.2 23.7 %collective-permute-start.9 = (bf16[256,2048]{1,0:T(8,128)(2,1)S(1)}, bf16[256,2048]{1,0:T(8,128)(2,1)S(1)}, u32[]{:S(2)}, u32[]{:S(2)}) collective-permute-start(bf16[256,2048]{1,0:T(8,128)(2,1)S(1)} %get-tuple-element.75), channel_id=1, source_target_pairs={{0,8},{8,0},{16,24},{24,16},{1,9},{9,1},{17,25},{25,17},{2,10},{10... | collective-permute-start | bytes 3145736 | tf_op jit(solution)/shard_map/ppermute | solution.py:47
  142.7 36.3 %collective-permute-start.10 = (bf16[16,144,128]{2,1,0:T(8,128)(2,1)S(1)}, bf16[16,144,128]{2,1,0:T(8,128)(2,1)}, u32[]{:S(2)}, u32[]{:S(2)}) collective-permute-start(bf16[16,144,128]{2,1,0:T(8,128)(2,1)S(1)} %shard_map.257), channel_id=1, source_target_pairs={{1,3},{5,7},{9,11},{13,15},{17,19},{21,23},{25,27},{29,31}} | collective-permute-start | bytes 1769480 | tf_op jit(solution)/shard_map/ppermute | solution.py:440
  197.9 24.9 %collective-permute-start.12 = (bf16[128,2048]{1,0:T(8,128)(2,1)}, bf16[128,2048]{1,0:T(8,128)(2,1)}, u32[]{:S(2)}, u32[]{:S(2)}) collective-permute-start(bf16[128,2048]{1,0:T(8,128)(2,1)} %get-tuple-element.164), channel_id=1, source_target_pairs={{0,8},{8,0},{16,24},{24,16},{1,9},{9,1},{17,25},{25,17},{2,10},{10... | collective-permute-start | bytes 1572872 | tf_op jit(solution)/shard_map/ppermute | solution.py:47
  198.5 24.4 %collective-permute-start.17 = (bf16[128,2048]{1,0:T(8,128)(2,1)}, bf16[128,2048]{1,0:T(8,128)(2,1)}, u32[]{:S(2)}, u32[]{:S(2)}) collective-permute-start(bf16[128,2048]{1,0:T(8,128)(2,1)} %get-tuple-element.165), channel_id=1, source_target_pairs={{0,16},{8,24},{16,0},{24,8},{1,17},{9,25},{17,1},{25,9},{2,18},{10... | collective-permute-start | bytes 1572872 | tf_op jit(solution)/shard_map/ppermute | solution.py:47
  217.5 179.6 %reduce-scatter.5.cloned.1.call-start = ((), (), s32[]{:S(2)}) async-start(), calls=%async_computation.7 | async-start | bytes 6488064 | tf_op jit(solution)/shard_map/reduce_scatter | solution.py:531
  236.5 23.8 %collective-permute-start.19 = (bf16[256,2048]{1,0:T(8,128)(2,1)S(1)}, bf16[256,2048]{1,0:T(8,128)(2,1)S(1)}, u32[]{:S(2)}, u32[]{:S(2)}) collective-permute-start(bf16[256,2048]{1,0:T(8,128)(2,1)S(1)} %get-tuple-element.139), channel_id=1, source_target_pairs={{0,16},{8,24},{16,0},{24,8},{1,17},{9,25},{17,1},{25,9},{2,18},{10... | collective-permute-start | bytes 3145736 | tf_op jit(solution)/shard_map/ppermute | solution.py:47
  305.0 196.7 %reduce-scatter.7.cloned.1.call-start = ((), (), s32[]{:S(2)}) async-start(), calls=%async_computation.8 | async-start | bytes 12976128 | tf_op jit(solution)/shard_map/reduce_scatter | solution.py:531
  354.1 231.3 %reduce-scatter.11.cloned.1.call-start = ((), (), s32[]{:S(2)}) async-start(), calls=%async_computation.10 | async-start | bytes 2359296 | tf_op jit(solution)/shard_map/reduce_scatter | solution.py:531
  358.8 25.0 %collective-permute-start.22 = (bf16[128,2048]{1,0:T(8,128)(2,1)}, bf16[128,2048]{1,0:T(8,128)(2,1)S(1)}, u32[]{:S(2)}, u32[]{:S(2)}) collective-permute-start(bf16[128,2048]{1,0:T(8,128)(2,1)} %get-tuple-element.163), channel_id=1, source_target_pairs={{0,8},{8,0},{16,24},{24,16},{1,9},{9,1},{17,25},{25,17},{2,10},{10... | collective-permute-start | bytes 1572872 | tf_op jit(solution)/shard_map/ppermute | solution.py:47
  359.7 24.1 %collective-permute-start.27 = (bf16[128,2048]{1,0:T(8,128)(2,1)}, bf16[128,2048]{1,0:T(8,128)(2,1)}, u32[]{:S(2)}, u32[]{:S(2)}) collective-permute-start(bf16[128,2048]{1,0:T(8,128)(2,1)} %get-tuple-element.161), channel_id=1, source_target_pairs={{0,16},{8,24},{16,0},{24,8},{1,17},{9,25},{17,1},{25,9},{2,18},{10... | collective-permute-start | bytes 1572872 | tf_op jit(solution)/shard_map/ppermute | solution.py:47
  462.5 201.1 %reduce-scatter.9.cloned.1.call-start = ((), (), s32[]{:S(2)}) async-start(), calls=%async_computation.9 | async-start | bytes 9437184 | tf_op jit(solution)/shard_map/reduce_scatter | solution.py:531
  462.6 32.7 %collective-permute-start.40 = (bf16[16,144,128]{2,1,0:T(8,128)(2,1)S(1)}, bf16[16,144,128]{2,1,0:T(8,128)(2,1)}, u32[]{:S(2)}, u32[]{:S(2)}) collective-permute-start(bf16[16,144,128]{2,1,0:T(8,128)(2,1)S(1)} %shard_map.262), channel_id=1, source_target_pairs={{2,0},{6,4},{10,8},{14,12},{18,16},{22,20},{26,24},{30,28}} | collective-permute-start | bytes 1769480 | tf_op jit(solution)/shard_map/ppermute | solution.py:440
  463.9 39.4 %collective-permute-start.34 = (bf16[128,2048]{1,0:T(8,128)(2,1)}, bf16[128,2048]{1,0:T(8,128)(2,1)}, u32[]{:S(2)}, u32[]{:S(2)}) collective-permute-start(bf16[128,2048]{1,0:T(8,128)(2,1)} %get-tuple-element.157), channel_id=1, source_target_pairs={{0,8},{8,0},{16,24},{24,16},{1,9},{9,1},{17,25},{25,17},{2,10},{10... | collective-permute-start | bytes 1572872 | tf_op jit(solution)/shard_map/ppermute | solution.py:47
  464.2 40.6 %collective-permute-start.39 = (bf16[128,2048]{1,0:T(8,128)(2,1)}, bf16[128,2048]{1,0:T(8,128)(2,1)}, u32[]{:S(2)}, u32[]{:S(2)}) collective-permute-start(bf16[128,2048]{1,0:T(8,128)(2,1)} %get-tuple-element.155), channel_id=1, source_target_pairs={{0,16},{8,24},{16,0},{24,8},{1,17},{9,25},{17,1},{25,9},{2,18},{10... | collective-permute-start | bytes 1572872 | tf_op jit(solution)/shard_map/ppermute | solution.py:47
  476.5 29.8 %collective-permute-start.36 = (bf16[128,2048]{1,0:T(8,128)(2,1)}, bf16[128,2048]{1,0:T(8,128)(2,1)}, u32[]{:S(2)}, u32[]{:S(2)}) collective-permute-start(bf16[128,2048]{1,0:T(8,128)(2,1)} %get-tuple-element.153), channel_id=1, source_target_pairs={{0,8},{8,0},{16,24},{24,16},{1,9},{9,1},{17,25},{25,17},{2,10},{10... | collective-permute-start | bytes 1572872 | tf_op jit(solution)/shard_map/ppermute | solution.py:47
  478.2 28.6 %collective-permute-start.38 = (bf16[128,2048]{1,0:T(8,128)(2,1)}, bf16[128,2048]{1,0:T(8,128)(2,1)}, u32[]{:S(2)}, u32[]{:S(2)}) collective-permute-start(bf16[128,2048]{1,0:T(8,128)(2,1)} %get-tuple-element.152), channel_id=1, source_target_pairs={{0,16},{8,24},{16,0},{24,8},{1,17},{9,25},{17,1},{25,9},{2,18},{10... | collective-permute-start | bytes 1572872 | tf_op jit(solution)/shard_map/ppermute | solution.py:47
  503.3 25.4 %collective-permute-start.42 = (bf16[256,1408]{1,0:T(8,128)(2,1)S(1)}, bf16[256,1408]{1,0:T(8,128)(2,1)S(1)}, u32[]{:S(2)}, u32[]{:S(2)}) collective-permute-start(bf16[256,1408]{1,0:T(8,128)(2,1)S(1)} %get-tuple-element.117), channel_id=1, source_target_pairs={{0,8},{8,0},{16,24},{24,16},{1,9},{9,1},{17,25},{25,17},{2,10},{10... | collective-permute-start | bytes 2162696 | tf_op jit(solution)/shard_map/ppermute | solution.py:47
  504.8 23.9 %collective-permute-start.43 = (bf16[256,1408]{1,0:T(8,128)(2,1)S(1)}, bf16[256,1408]{1,0:T(8,128)(2,1)S(1)}, u32[]{:S(2)}, u32[]{:S(2)}) collective-permute-start(bf16[256,1408]{1,0:T(8,128)(2,1)S(1)} %get-tuple-element.117), channel_id=1, source_target_pairs={{0,16},{8,24},{16,0},{24,8},{1,17},{9,25},{17,1},{25,9},{2,18},{10... | collective-permute-start | bytes 2162696 | tf_op jit(solution)/shard_map/ppermute | solution.py:47
  506.3 28.2 %collective-permute-start.44 = (bf16[256,1408]{1,0:T(8,128)(2,1)S(1)}, bf16[256,1408]{1,0:T(8,128)(2,1)S(1)}, u32[]{:S(2)}, u32[]{:S(2)}) collective-permute-start(bf16[256,1408]{1,0:T(8,128)(2,1)S(1)} %get-tuple-element.120), channel_id=1, source_target_pairs={{0,8},{8,0},{16,24},{24,16},{1,9},{9,1},{17,25},{25,17},{2,10},{10... | collective-permute-start | bytes 2162696 | tf_op jit(solution)/shard_map/ppermute | solution.py:47
  506.9 28.9 %collective-permute-start.45 = (bf16[256,1408]{1,0:T(8,128)(2,1)S(1)}, bf16[256,1408]{1,0:T(8,128)(2,1)S(1)}, u32[]{:S(2)}, u32[]{:S(2)}) collective-permute-start(bf16[256,1408]{1,0:T(8,128)(2,1)S(1)} %get-tuple-element.120), channel_id=1, source_target_pairs={{0,16},{8,24},{16,0},{24,8},{1,17},{9,25},{17,1},{25,9},{2,18},{10... | collective-permute-start | bytes 2162696 | tf_op jit(solution)/shard_map/ppermute | solution.py:47
  570.7 89.4 %collective-permute-start.48 = (bf16[128,2048]{1,0:T(8,128)(2,1)}, bf16[128,2048]{1,0:T(8,128)(2,1)}, u32[]{:S(2)}, u32[]{:S(2)}) collective-permute-start(bf16[128,2048]{1,0:T(8,128)(2,1)} %get-tuple-element.146), channel_id=1, source_target_pairs={{0,8},{8,0},{16,24},{24,16},{1,9},{9,1},{17,25},{25,17},{2,10},{10... | collective-permute-start | bytes 1572872 | tf_op jit(solution)/shard_map/ppermute | solution.py:47
  585.4 27.4 %collective-permute-start.69 = (bf16[64,2048]{1,0:T(8,128)(2,1)}, bf16[64,2048]{1,0:T(8,128)(2,1)S(1)}, u32[]{:S(2)}, u32[]{:S(2)}) collective-permute-start(bf16[64,2048]{1,0:T(8,128)(2,1)} %reduce-scatter.11.cloned.1.call-done), channel_id=1, source_target_pairs={{0,8},{8,0},{16,24},{24,16},{1,9},{9,1},{17,25},{25,17},{2,10},{10... | collective-permute-start | bytes 786440 | tf_op jit(solution)/shard_map/ppermute | solution.py:47
  586.9 27.4 %collective-permute-start.71 = (bf16[64,2048]{1,0:T(8,128)(2,1)}, bf16[64,2048]{1,0:T(8,128)(2,1)S(1)}, u32[]{:S(2)}, u32[]{:S(2)}) collective-permute-start(bf16[64,2048]{1,0:T(8,128)(2,1)} %reduce-scatter.11.cloned.1.call-done), channel_id=1, source_target_pairs={{0,16},{8,24},{16,0},{24,8},{1,17},{9,25},{17,1},{25,9},{2,18},{10... | collective-permute-start | bytes 786440 | tf_op jit(solution)/shard_map/ppermute | solution.py:47
  591.4 24.4 %collective-permute-start.61 = (bf16[128,1408]{1,0:T(8,128)(2,1)S(1)}, bf16[128,1408]{1,0:T(8,128)(2,1)S(1)}, u32[]{:S(2)}, u32[]{:S(2)}) collective-permute-start(bf16[128,1408]{1,0:T(8,128)(2,1)S(1)} %slice.245), channel_id=1, source_target_pairs={{0,16},{8,24},{16,0},{24,8},{1,17},{9,25},{17,1},{25,9},{2,18},{10... | collective-permute-start | bytes 1081352 | tf_op jit(solution)/shard_map/ppermute | solution.py:47
  612.8 47.3 %collective-permute-start.53 = (bf16[128,2048]{1,0:T(8,128)(2,1)S(1)}, bf16[128,2048]{1,0:T(8,128)(2,1)S(1)}, u32[]{:S(2)}, u32[]{:S(2)}) collective-permute-start(bf16[128,2048]{1,0:T(8,128)(2,1)S(1)} %copy-done.56), channel_id=1, source_target_pairs={{0,16},{8,24},{16,0},{24,8},{1,17},{9,25},{17,1},{25,9},{2,18},{10... | collective-permute-start | bytes 1572872 | tf_op jit(solution)/shard_map/ppermute | solution.py:47
  614.2 45.9 %collective-permute-start.50 = (bf16[128,2048]{1,0:T(8,128)(2,1)}, bf16[128,2048]{1,0:T(8,128)(2,1)S(1)}, u32[]{:S(2)}, u32[]{:S(2)}) collective-permute-start(bf16[128,2048]{1,0:T(8,128)(2,1)} %get-tuple-element.150), channel_id=1, source_target_pairs={{0,8},{8,0},{16,24},{24,16},{1,9},{9,1},{17,25},{25,17},{2,10},{10... | collective-permute-start | bytes 1572872 | tf_op jit(solution)/shard_map/ppermute | solution.py:47
  (112 other events, 1525.3 us)
Sparse Core Ops, SparseCore 0:
  16.0 102.0 all-gather.3
  120.3 109.1 all-gather.7
  231.7 62.5 all-gather.5
  305.1 70.2 reduce-scatter.4
  377.6 123.9 reduce-scatter.6
  504.4 33.7 reduce-scatter.10
  550.2 89.5 reduce-scatter.8

commit v4 on v3

--- a/solution.py
+++ b/solution.py
@@ -338,8 +338,8 @@
     return pl.BlockSpec((1, width), lambda s, *_: (0, 0))
 
 
-def call(kernel, grid, scalars, in_specs, out_specs, out_shape, args, flops=1e9):
-    params = pltpu.CompilerParams(vmem_limit_bytes=48 * 1024 * 1024)
+def call(kernel, grid, scalars, in_specs, out_specs, out_shape, args, flops=1e9, vmem=48):
+    params = pltpu.CompilerParams(vmem_limit_bytes=vmem * 1024 * 1024)
     return pl.pallas_call(
         kernel,
         grid_spec=pltpu.PrefetchScalarGridSpec(
@@ -421,7 +421,7 @@
         functools.partial(pick_kernel, heads), (heads,), (place,),
         [column] * 4 + [pl.BlockSpec((rows // 4, width), lambda k, place: (place[1], 0))],
         pl.BlockSpec((rows, width + width // 4), lambda k, place: (0, 0)),
-        jax.ShapeDtypeStruct((rows, width + width // 4), BF), (*mats, last),
+        jax.ShapeDtypeStruct((rows, width + width // 4), BF), (*mats, last), vmem=62,
     )
 
 
@@ -582,16 +582,15 @@
             own = lax.dynamic_slice_in_dim(halves, low_bit * (mine // 2), mine // 2, 0)
             give = lax.dynamic_slice_in_dim(halves, (1 - low_bit) * (mine // 2), mine // 2, 0)
             give = later(give, pair)
-            got = swap(give, 1)
-            wo = pair_halves(own, got, low_bit, heads)
+            wo = pair_halves(own, swap(give, 1), low_bit, heads)
         else:
             wo = of_heads(gather_seq(w_o), 0)
-            got = give = wo
+            give = wo
         z_qg = columns(h_all, later(both, give), blocks, blocks)
         intra, qs = call(
             functools.partial(intra_kernel, count, heads), grid, (starts,),
             [fl, vl, ql, fixed(mine)], [one, one], [wide, thin],
-            (z_fv, z_fv, later(z_qg, got), bound), 3e9,
+            (z_fv, z_fv, z_qg, bound), 3e9,
         )
         kept.extend((wo, z_qg, intra, qs))
         return intra
@@ -643,7 +642,7 @@
         [one, gl, one, one, fixed(128), pack_spec],
         [one, one, pack_spec, fixed(128)],
         [wide, thin, packed, jax.ShapeDtypeStruct((1, 128), F32)],
-        (d_on, z_qg, mixed, qs, gain, pack),
+        (d_on, z_qg, mixed, qs, gain, pack), 1e13,
     )
     def moves(pair):
         if natural:
@@ -669,7 +668,7 @@
     o_rows = scatter_seq(o_full)
     result = (y + scatter_end(onward, at_hand)).astype(BF)
 
-    near, far = later((near, far), o_full, gu_rows)
+    near, far = later((near, far), o_full, result)
     dz, d_bound = call(
         functools.partial(back_kernel, count, heads), grid, (starts, whole),
         [fl, vl, ql, fixed(mine), one, one, state_spec, pack_spec, pack_spec],
@@ -678,17 +677,29 @@
         (z_fv, z_fv, z_qg, bound, d_gz, d_mixed, enter, near, far), 8e9,
     )
 
-    gate_parts, up_parts = gather_begin(gu_rows[:, :ff]), gather_begin(gu_rows[:, ff:])
-    z_part = dot_first(h_all, later(dz, result, gate_parts, up_parts), BF)
+    gu_parts = gather_begin(later(gu_rows, result))
+    z_part = dot_first(h_all, later(dz, result, gu_parts), BF)
     z_rows = scatter_seq(z_part)
     h_part, d_norm_gain = against_rows(later(dz, z_part), both, h_all, norm_gain[None])
     down_parts = gather_begin(later(down_rows, z_part))
     h_part, down_parts = lax.optimization_barrier((h_part, down_parts))
     onward, at_hand = scatter_begin(h_part)
-    gate_parts, up_parts, down_parts, o_rows = later((gate_parts, up_parts, down_parts, o_rows), onward)
-    gate_parts, up_parts, down_parts = (gather_end(*v) for v in (gate_parts, up_parts, down_parts))
+    gu_parts, down_parts = later((gu_parts, down_parts), onward)
+    gu_parts, down_parts = gather_end(*gu_parts), gather_end(*down_parts)
     d_h = scatter_end(onward, at_hand)
-    z_rows = later(z_rows, gate_parts, up_parts, down_parts, d_h)
+
+    zero = jnp.zeros((mine,), F32)
+    d_bound = to_heads([d_bound[0], zero, zero, zero], 0)
+    small = jnp.concatenate([d_norm_gain[0], d_ffn_gain, d_bound, d_gain[0]])
+    small, o_rows = later((small, o_rows), d_h)
+    small = everywhere(small)
+    if natural:
+        o_all = (o_rows, swap(o_rows, 1), swap(o_rows, 2), swap(o_rows, 3))
+        grad_o = jnp.concatenate(absolute(o_all), axis=0).astype(F32)
+    else:
+        o_all = ()
+        grad_o = lax.psum(o_rows.astype(F32), "dp")
+    z_rows = later(z_rows, gu_parts, down_parts, d_h, small, o_all)
 
     order = jnp.arange(4, dtype=jnp.int32) ^ dp.astype(jnp.int32)
 
@@ -697,7 +708,11 @@
         count = parts[0].shape[1] // columns
         blocks = jnp.concatenate(parts, axis=0).reshape(4, part, count * columns)
         if not flat:
-            return [to_hidden([blocks[k] for k in range(4)]).astype(F32)]
+            cut = [blocks[k] for k in range(4)]
+            return [
+                to_hidden([v[:, k * columns : (k + 1) * columns] for v in cut]).astype(F32)
+                for k in range(count)
+            ]
         tall = min(64, part)
         out = jax.ShapeDtypeStruct((part, total), F32)
         return call(
@@ -706,27 +721,16 @@
             [pl.BlockSpec((tall, total), lambda s, *_: (s, 0))] * count, [out] * count, (blocks,),
         )
 
-    if natural:
-        o_parts = gather_parts(o_rows)
-        o_all = o_parts[:3] + (jnp.concatenate(o_parts[3:], axis=0),)
-        grad_o = jnp.concatenate(absolute(o_all), axis=0).astype(F32)
-    else:
-        grad_o = lax.psum(o_rows.astype(F32), "dp")
     down_all = down_parts[:3] + (jnp.concatenate(down_parts[3:], axis=0),)
     grad_down = jnp.concatenate(absolute(down_all), axis=0).astype(F32)
     join_hidden = functools.partial(hidden_kernel, chunk, seqs)
-    [grad_gate] = whole_rows(gate_parts, join_hidden, ff, chunk % 16 == 0)
-    [grad_up] = whole_rows(up_parts, join_hidden, ff, chunk % 16 == 0)
+    grad_gate, grad_up = whole_rows(gu_parts, join_hidden, ff, chunk % 16 == 0)
     join_heads = functools.partial(heads_kernel, heads)
     grad_f, grad_i, grad_q, grad_g = whole_rows(gather_parts(z_rows), join_heads, mine, True)
 
     u1 = d_h * norm_gain
     d_x = d_y + r1 * u1 - x * (r1 * r1 * r1) * jnp.mean(u1 * x, axis=-1, keepdims=True)
 
-    zero = jnp.zeros((mine,), F32)
-    d_bound = to_heads([d_bound[0], zero, zero, zero], 0)
-    small = jnp.concatenate([d_norm_gain[0], d_ffn_gain, d_bound, d_gain[0]])
-    small = everywhere(later(small, onward))
     return (
         result,
         d_x.astype(BF),

time: 721 us -> 702 us (0.974)
  starting transfers between devices: 93.9 us -> 81.7 us
    ppermute x62 -> x57, waiting for transfers between devices: 240 us -> 256 us  [swap(): return lax.ppermute(value, 'dp', [(s, s ^ bits) for s in range(count)])]
    ppermute x6, waiting for transfers between devices: 18 us -> 4.41 us  [hop(): lax.ppermute(value, 'seq', [(f + order[a], f + order[b]) for f in first f...]
    ppermute x62 -> x57, starting transfers between devices: 77.3 us -> 65.5 us  [swap(): return lax.ppermute(value, 'dp', [(s, s ^ bits) for s in range(count)])]
    all_gather x3, waiting for transfers between devices: 0.33 us -> 10.4 us  [gather_seq(): return lax.all_gather(value, 'seq', axis=0, tiled=True)]
    unnamed x155 -> x128, local copies, waits for them, and re-layouts: 39.5 us -> 35.7 us
    pallas_call x14 -> x13, Pallas kernels: 90.8 us -> 91.2 us  [call(): pl.pallas_call(kernel, grid_spec=pltpu.PrefetchScalarGridSpec(num_scalar_...]
  transfers between devices with their start and end apart: 80 -> 75, of which waited for: 46 -> 47; matrix products, arithmetic and copies ran while one was open for 30% -> 30% of each run, Pallas kernels for 12% -> 12%
where the time goes in v4:
time: 702 us; the launch traced here: 692 us
  waiting for transfers between devices  282 us (40%)
  matrix products  108 us (15%)
  Pallas kernels  91.2 us (13%)
  starting transfers between devices  81.7 us (12%)
  local copies, waits for them, and re-layouts  69.8 us (10%)
  other arithmetic  43.9 us (6%)
  between operations  15.3 us (2%)
    ppermute x57, waiting for transfers between devices, swap(): return lax.ppermute(value, 'dp', [(s, s ^ bits) for s in range(count)])  256 us
    pallas_call x13, Pallas kernels, call(): pl.pallas_call(kernel, grid_spec=pltpu.PrefetchScalarGridSpec(num_scalar_...  91.2 us
    ppermute x57, starting transfers between devices, swap(): return lax.ppermute(value, 'dp', [(s, s ^ bits) for s in range(count)])  65.5 us
    dot_general x4, matrix products, dot_first(): lax.dot_general(left, right, (((0,), (0,)), ((), ())), preferred_element_...  44.5 us
    unnamed x128, local copies, waits for them, and re-layouts  35.7 us
    dot_general x3, matrix products, dot_last(): lax.dot_general(left, right, (((1,), (1,)), ((), ())), preferred_element_...  34.3 us
    dot_general x3, matrix products, mm(): return jnp.dot(left, right, preferred_element_type=F32).astype(kind)  29.3 us
  transfers between devices with their start and end apart: 75, of which 47 were waited for; matrix products, arithmetic and copies ran while one was open for 30% of the time, Pallas kernels for 12%

profile of v4, /device:TPU:0, one launch (start us, length us, event | category | flops | bytes accessed | tf_op | source)
XLA Modules:
  0.0 692.0 jit_solution(13807395327091240789)
XLA Ops:
  19.1 21.8 %collective-permute-done = bf16[256,2048]{1,0:T(8,128)(2,1)S(1)} collective-permute-done((bf16[256,2048]{1,0:T(8,128)(2,1)}, bf16[256,2048]{1,0:T(8,128)(2,1)S(1)}, u32[]{:S(2)}, u32[]{:S(2)}) %collective-permute-start) | collective-permute-done | bytes 1048608 | tf_op jit(solution)/shard_map/ppermute | solution.py:47
  46.6 7.8 %collective-permute-done.2 = bf16[128,2048]{1,0:T(8,128)(2,1)S(1)} collective-permute-done((bf16[128,2048]{1,0:T(8,128)(2,1)S(1)}, bf16[128,2048]{1,0:T(8,128)(2,1)S(1)}, u32[]{:S(2)}, u32[]{:S(2)}) %collective-permute-start.2) | collective-permute-done | bytes 524320 | tf_op jit(solution)/shard_map/ppermute | solution.py:47
  69.8 20.5 %collective-permute-done.4 = bf16[256,2048]{1,0:T(8,128)(2,1)S(1)} collective-permute-done((bf16[256,2048]{1,0:T(8,128)(2,1)S(1)}, bf16[256,2048]{1,0:T(8,128)(2,1)S(1)}, u32[]{:S(2)}, u32[]{:S(2)}) %collective-permute-start.4) | collective-permute-done | bytes 1048608 | tf_op jit(solution)/shard_map/ppermute | solution.py:47
  104.4 9.9 %all-gather.4.cloned.1.call-done.right_ref = bf16[2048,2560]{1,0:T(8,128)(2,1)} async-done(((bf16[256,2560]{1,0:T(8,128)(2,1)}), bf16[2048,2560]{1,0:T(8,128)(2,1)}) %all-gather.4.cloned.1.call-update) | async-done | bytes 10485776 | tf_op jit(solution)/shard_map/all_gather | solution.py:528
  114.4 7.8 %shard_map.255.f_ref.v_ref = f32[1024,1024]{1,0:T(8,128)S(1)} custom-call(bf16[1024,2048]{1,0:T(8,128)(2,1)} %constant_dynamic-update-slice_fusion.left_ref.beside_ref, bf16[2048,2560]{1,0:T(8,128)(2,1)} %all-gather.4.cloned.1.call-done.right_ref), custom_call_target="tpu_custom_call" | custom-call | flops 80000000 | bytes 65536 | tf_op jit(solution)/shard_map/pallas_call | solution.py:343
  138.8 7.9 %shard_map.258.q_ref.g_ref = f32[1024,1024]{1,0:T(8,128)S(1)} custom-call(bf16[1024,2048]{1,0:T(8,128)(2,1)} %constant_dynamic-update-slice_fusion.left_ref.beside_ref, bf16[2048,2560]{1,0:T(8,128)(2,1)} %all-gather.4.cloned.1.call-done.right_ref), custom_call_target="tpu_custom_call" | custom-call | flops 80000000 | bytes 65536 | tf_op jit(solution)/shard_map/pallas_call | solution.py:343
  148.6 11.8 %shard_map.259 = (f32[1024,512]{1,0:T(8,128)S(1)}, bf16[1024,512]{1,0:T(8,128)(2,1)S(1)}) custom-call(s32[4,2]{1,0:T(4,128)S(1)} %broadcast_in_dim.36.starts, f32[1024,1024]{1,0:T(8,128)} %copy-done.2, f32[1024,1024]{1,0:T(8,128)} %copy-done.2, f32[1024,1024]{1,0:T(8,128)} %copy-done.3, f32[1,512]{1,0:T(1,128)S(1)} %dynamic-slice_bitcast_fusion.b_ref), custom_call_target="tpu_custom_call" | custom-call | flops 30000000 | bytes 65536 | tf_op jit(solution)/shard_map/pallas_call | solution.py:343
  180.6 10.8 %collective-permute-done.13 = bf16[128,2048]{1,0:T(8,128)(2,1)S(1)} collective-permute-done((bf16[128,2048]{1,0:T(8,128)(2,1)S(1)}, bf16[128,2048]{1,0:T(8,128)(2,1)S(1)}, u32[]{:S(2)}, u32[]{:S(2)}) %collective-permute-start.13) | collective-permute-done | bytes 524320 | tf_op jit(solution)/shard_map/ppermute | solution.py:47
  204.2 9.5 %collective-permute-done.14 = bf16[128,2048]{1,0:T(8,128)(2,1)S(1)} collective-permute-done((bf16[128,2048]{1,0:T(8,128)(2,1)S(1)}, bf16[128,2048]{1,0:T(8,128)(2,1)S(1)}, u32[]{:S(2)}, u32[]{:S(2)}) %collective-permute-start.14) | collective-permute-done | bytes 524320 | tf_op jit(solution)/shard_map/ppermute | solution.py:47
  220.1 22.6 %collective-permute-done.18 = bf16[256,2048]{1,0:T(8,128)(2,1)S(1)} collective-permute-done((bf16[256,2048]{1,0:T(8,128)(2,1)S(1)}, bf16[256,2048]{1,0:T(8,128)(2,1)S(1)}, u32[]{:S(2)}, u32[]{:S(2)}) %collective-permute-start.18) | collective-permute-done | bytes 1048608 | tf_op jit(solution)/shard_map/ppermute | solution.py:47
  247.4 6.9 collective-permute-done.20
  256.0 17.4 %fusion.19 = f32[1024,2816]{1,0:T(8,128)S(1)} fusion(bf16[1024,2048]{1,0:T(8,128)(2,1)} %constant_dynamic-update-slice_fusion.10, bf16[2048,2816]{0,1:T(8,128)(2,1)} %all-gather.8.cloned.1.call-done), kind=kOutput, calls=%fused_computation.133 | convolution fusion | flops 11811160064 | bytes 27262976 | tf_op jit(solution)/shard_map/dot_general | solution.py:30
  279.1 10.7 %convolution_convert_fusion.2 = bf16[1408,2048]{1,0:T(8,128)(2,1)} fusion(bf16[1024,1408]{1,0:T(8,128)(2,1)S(1)} %multiply_convert_fusion.2, bf16[1024,2048]{1,0:T(8,128)(2,1)} %constant_dynamic-update-slice_fusion.5), kind=kOutput, calls=%fused_computation.2 | convolution fusion | flops 5908463616 | bytes 12845056 | tf_op jit(solution)/shard_map/dot_general | solution.py:34
  290.5 14.2 %multiply_convert_fusion.1 = (bf16[1024,1408]{1,0:T(8,128)(2,1)S(1)}, bf16[1024,1408]{1,0:T(8,128)(2,1)S(1)}) fusion(f32[1024,2816]{1,0:T(8,128)} %copy-done.24, bf16[1024,2048]{1,0:T(8,128)(2,1)} %constant_dynamic-update-slice_fusion.5, bf16[1408,2048]{1,0:T(8,128)(2,1)} %all-gather.6.cloned.1.call-done), kind=kOutput, calls=%fused_computation.5 | convolution fusion | flops 5924323328 | bytes 27262976 | tf_op jit(solution)/shard_map/dot_general | solution.py:40
  305.2 16.4 %convolution_convert_fusion.3 = bf16[1024,2048]{1,0:T(8,128)(2,1)} fusion(bf16[2048,2816]{0,1:T(8,128)(2,1)} %all-gather.8.cloned.1.call-done, bf16[1024,1408]{1,0:T(8,128)(2,1)S(1)} %get-tuple-element.143, bf16[1024,1408]{1,0:T(8,128)(2,1)S(1)} %get-tuple-element.142), kind=kOutput, calls=%fused_computation.14 | convolution fusion | flops 11824791552 | bytes 21495808 | tf_op jit(solution)/shard_map/dot_general | solution.py:40
  321.5 17.8 %convolution_convert_fusion = bf16[2048,2816]{1,0:T(8,128)(2,1)} fusion(bf16[1024,2048]{1,0:T(8,128)(2,1)} %constant_dynamic-update-slice_fusion.10, bf16[1024,2816]{1,0:T(8,128)(2,1)S(1)} %pad_maximum_fusion), kind=kOutput, calls=%fused_computation | convolution fusion | flops 11816927232 | bytes 21495808 | tf_op jit(solution)/shard_map/dot_general | solution.py:34
  346.6 10.7 %collective-permute-done.23 = bf16[128,2048]{1,0:T(8,128)(2,1)S(1)} collective-permute-done((bf16[128,2048]{1,0:T(8,128)(2,1)S(1)}, bf16[128,2048]{1,0:T(8,128)(2,1)S(1)}, u32[]{:S(2)}, u32[]{:S(2)}) %collective-permute-start.23) | collective-permute-done | bytes 524320 | tf_op jit(solution)/shard_map/ppermute | solution.py:47
  363.4 6.7 collective-permute-done.22
  370.1 10.3 %collective-permute-done.24 = bf16[128,2048]{1,0:T(8,128)(2,1)} collective-permute-done((bf16[128,2048]{1,0:T(8,128)(2,1)}, bf16[128,2048]{1,0:T(8,128)(2,1)}, u32[]{:S(2)}, u32[]{:S(2)}) %collective-permute-start.24) | collective-permute-done | bytes 524320 | tf_op jit(solution)/shard_map/ppermute | solution.py:47
  388.2 9.7 %convolution_convert_fusion.4 = bf16[1024,2048]{1,0:T(8,128)(2,1)S(1)} fusion(bf16[1024,1408]{1,0:T(8,128)(2,1)} %copy-done.31, bf16[1408,2048]{1,0:T(8,128)(2,1)} %all-gather.6.cloned.1.call-done), kind=kOutput, calls=%fused_computation.15 | convolution fusion | flops 5907677184 | bytes 12845056 | tf_op jit(solution)/shard_map/dot_general | solution.py:30
  397.9 12.7 %collective-permute-done.28 = bf16[256,2048]{1,0:T(8,128)(2,1)S(1)} collective-permute-done((bf16[256,2048]{1,0:T(8,128)(2,1)}, bf16[256,2048]{1,0:T(8,128)(2,1)S(1)}, u32[]{:S(2)}, u32[]{:S(2)}) %collective-permute-start.28) | collective-permute-done | bytes 1048608 | tf_op jit(solution)/shard_map/ppermute | solution.py:47
  413.1 9.9 %collective-permute-done.30 = bf16[128,2048]{1,0:T(8,128)(2,1)S(1)} collective-permute-done((bf16[128,2048]{1,0:T(8,128)(2,1)S(1)}, bf16[128,2048]{1,0:T(8,128)(2,1)S(1)}, u32[]{:S(2)}, u32[]{:S(2)}) %collective-permute-start.30) | collective-permute-done | bytes 524320 | tf_op jit(solution)/shard_map/ppermute | solution.py:47
  442.6 7.2 %collective-permute-done.32 = bf16[256,2048]{1,0:T(8,128)(2,1)S(1)} collective-permute-done((bf16[256,2048]{1,0:T(8,128)(2,1)}, bf16[256,2048]{1,0:T(8,128)(2,1)S(1)}, u32[]{:S(2)}, u32[]{:S(2)}) %collective-permute-start.32) | collective-permute-done | bytes 1048608 | tf_op jit(solution)/shard_map/ppermute | solution.py:47
  455.1 10.8 %collective-permute-done.35 = bf16[128,2048]{1,0:T(8,128)(2,1)S(1)} collective-permute-done((bf16[128,2048]{1,0:T(8,128)(2,1)S(1)}, bf16[128,2048]{1,0:T(8,128)(2,1)S(1)}, u32[]{:S(2)}, u32[]{:S(2)}) %collective-permute-start.35) | collective-permute-done | bytes 524320 | tf_op jit(solution)/shard_map/ppermute | solution.py:47
  502.3 16.4 %shard_map.263 = (bf16[1024,2048]{1,0:T(8,128)(2,1)}, f32[1,512]{1,0:T(1,128)S(1)}) custom-call(s32[4,2]{1,0:T(4,128)S(1)} %copy-done.14, s32[1]{0:T(128)} %bitcast.20.whole, f32[1024,1024]{1,0:T(8,128)} %copy-done.2, f32[1024,1024]{1,0:T(8,128)} %copy-done.2, f32[1024,1024]{1,0:T(8,128)} %copy-done.3, f32[1,512]{1,0:T(1,128)S(1)} %copy-done.16, ...), custom_call_target="tpu_custom_call" | custom-call | flops 80000000 | bytes 65536 | tf_op jit(solution)/shard_map/pallas_call | solution.py:343
  524.3 13.5 %convolution_convert_fusion.1 = bf16[2048,2048]{1,0:T(8,128)(2,1)} fusion(bf16[1024,2048]{1,0:T(8,128)(2,1)S(1)} %copy-done.21, bf16[1024,2048]{1,0:T(8,128)(2,1)} %get-tuple-element.104.left_ref), kind=kOutput, calls=%fused_computation.1 | convolution fusion | flops 8594128896 | bytes 16777216 | tf_op jit(solution)/shard_map/dot_general | solution.py:34
  541.0 14.2 %shard_map.264 = (bf16[1024,2048]{1,0:T(8,128)(2,1)S(1)}, f32[1,2048]{1,0:T(1,128)S(1)}) custom-call(bf16[1024,2048]{1,0:T(8,128)(2,1)} %get-tuple-element.104.left_ref, bf16[2048,2560]{1,0:T(8,128)(2,1)} %all-gather.4.cloned.1.call-done.right_ref, bf16[1024,2048]{1,0:T(8,128)(2,1)} %constant_dynamic-update-slice_fusion.left_ref.beside_ref, ...), custom_call_target="tpu_custom_call" | custom-call | flops 80000000 | bytes 65536 | tf_op jit(solution)/shard_map/pallas_call | solution.py:343
  563.1 10.6 %collective-permute-done.47 = bf16[128,2048]{1,0:T(8,128)(2,1)S(1)} collective-permute-done((bf16[128,2048]{1,0:T(8,128)(2,1)S(1)}, bf16[128,2048]{1,0:T(8,128)(2,1)S(1)}, u32[]{:S(2)}, u32[]{:S(2)}) %collective-permute-start.47) | collective-permute-done | bytes 524320 | tf_op jit(solution)/shard_map/ppermute | solution.py:47
  588.8 14.4 %collective-permute-done.59 = bf16[88,2048]{1,0:T(8,128)(2,1)S(1)} collective-permute-done((bf16[88,2048]{1,0:T(8,128)(2,1)S(1)}, bf16[88,2048]{1,0:T(8,128)(2,1)S(1)}, u32[]{:S(2)}, u32[]{:S(2)}) %collective-permute-start.59) | collective-permute-done | bytes 360480 | tf_op jit(solution)/shard_map/ppermute | solution.py:47
  650.9 8.5 %shard_map.266 = (f32[256,5632]{1,0:T(8,128)}, f32[256,5632]{1,0:T(8,128)}) custom-call(s32[4]{0:T(128)S(1)} %iota_xor_fusion.order, bf16[4,256,2816]{2,1,0:T(8,128)(2,1)} %bitcast.37.blocks_ref), custom_call_target="tpu_custom_call" | custom-call | flops 10000000 | bytes 65536 | tf_op jit(solution)/shard_map/pallas_call | solution.py:343
  661.1 8.0 %collective-permute-done.64 = bf16[256,2048]{1,0:T(8,128)(2,1)S(1)} collective-permute-done((bf16[256,2048]{1,0:T(8,128)(2,1)}, bf16[256,2048]{1,0:T(8,128)(2,1)S(1)}, u32[]{:S(2)}, u32[]{:S(2)}) %collective-permute-start.64) | collective-permute-done | bytes 1048608 | tf_op jit(solution)/shard_map/ppermute | solution.py:47
  672.4 8.2 %collective-permute-done.66 = bf16[128,2048]{1,0:T(8,128)(2,1)S(1)} collective-permute-done((bf16[128,2048]{1,0:T(8,128)(2,1)S(1)}, bf16[128,2048]{1,0:T(8,128)(2,1)S(1)}, u32[]{:S(2)}, u32[]{:S(2)}) %collective-permute-start.66) | collective-permute-done | bytes 524320 | tf_op jit(solution)/shard_map/ppermute | solution.py:47
  (356 shorter events, 291.2 us)
Async XLA Ops:
  7.2 107.2 %all-gather.4.cloned.1.call-start = ((), (), s32[]{:S(2)}) async-start(), calls=%async_computation.4 | async-start | bytes 11796480 | tf_op jit(solution)/shard_map/all_gather | solution.py:528
  12.1 243.9 %all-gather.8.cloned.1.call-start = ((), (), s32[]{:S(2)}) async-start(), calls=%async_computation.6 | async-start | bytes 12976128 | tf_op jit(solution)/shard_map/all_gather | solution.py:528
  14.7 26.3 %collective-permute-start = (bf16[256,2048]{1,0:T(8,128)(2,1)}, bf16[256,2048]{1,0:T(8,128)(2,1)S(1)}, u32[]{:S(2)}, u32[]{:S(2)}) collective-permute-start(bf16[256,2048]{1,0:T(8,128)(2,1)} %get-tuple-element.141), channel_id=1, source_target_pairs={{0,8},{8,0},{16,24},{24,16},{1,9},{9,1},{17,25},{25,17},{2,10},{10... | collective-permute-start | bytes 3145736 | tf_op jit(solution)/shard_map/ppermute | solution.py:47
  17.6 25.3 %collective-permute-start.1 = (bf16[256,2048]{1,0:T(8,128)(2,1)}, bf16[256,2048]{1,0:T(8,128)(2,1)S(1)}, u32[]{:S(2)}, u32[]{:S(2)}) collective-permute-start(bf16[256,2048]{1,0:T(8,128)(2,1)} %get-tuple-element.141), channel_id=1, source_target_pairs={{0,16},{8,24},{16,0},{24,8},{1,17},{9,25},{17,1},{25,9},{2,18},{10... | collective-permute-start | bytes 3145736 | tf_op jit(solution)/shard_map/ppermute | solution.py:47
  66.6 223.9 %all-gather.6.cloned.1.call-start = ((), (), s32[]{:S(2)}) async-start(), calls=%async_computation.5 | async-start | bytes 6488064 | tf_op jit(solution)/shard_map/all_gather | solution.py:528
  68.6 24.0 %collective-permute-start.5 = (bf16[256,2048]{1,0:T(8,128)(2,1)S(1)}, bf16[256,2048]{1,0:T(8,128)(2,1)S(1)}, u32[]{:S(2)}, u32[]{:S(2)}) collective-permute-start(bf16[256,2048]{1,0:T(8,128)(2,1)S(1)} %copy-done.28), channel_id=1, source_target_pairs={{0,16},{8,24},{16,0},{24,8},{1,17},{9,25},{17,1},{25,9},{2,18},{10... | collective-permute-start | bytes 3145736 | tf_op jit(solution)/shard_map/ppermute | solution.py:47
  135.8 28.0 %collective-permute-start.11 = (bf16[256,2048]{1,0:T(8,128)(2,1)}, bf16[256,2048]{1,0:T(8,128)(2,1)}, u32[]{:S(2)}, u32[]{:S(2)}) collective-permute-start(bf16[256,2048]{1,0:T(8,128)(2,1)} %get-tuple-element.74), channel_id=1, source_target_pairs={{0,8},{8,0},{16,24},{24,16},{1,9},{9,1},{17,25},{25,17},{2,10},{10... | collective-permute-start | bytes 3145736 | tf_op jit(solution)/shard_map/ppermute | solution.py:47
  137.3 24.5 %collective-permute-start.9 = (bf16[16,144,128]{2,1,0:T(8,128)(2,1)S(1)}, bf16[16,144,128]{2,1,0:T(8,128)(2,1)}, u32[]{:S(2)}, u32[]{:S(2)}) collective-permute-start(bf16[16,144,128]{2,1,0:T(8,128)(2,1)S(1)} %shard_map.257), channel_id=1, source_target_pairs={{1,3},{5,7},{9,11},{13,15},{17,19},{21,23},{25,27},{29,31}} | collective-permute-start | bytes 1769480 | tf_op jit(solution)/shard_map/ppermute | solution.py:440
  178.6 25.6 %collective-permute-start.12 = (bf16[128,2048]{1,0:T(8,128)(2,1)}, bf16[128,2048]{1,0:T(8,128)(2,1)}, u32[]{:S(2)}, u32[]{:S(2)}) collective-permute-start(bf16[128,2048]{1,0:T(8,128)(2,1)} %get-tuple-element.162), channel_id=1, source_target_pairs={{0,8},{8,0},{16,24},{24,16},{1,9},{9,1},{17,25},{25,17},{2,10},{10... | collective-permute-start | bytes 1572872 | tf_op jit(solution)/shard_map/ppermute | solution.py:47
  180.0 24.2 %collective-permute-start.17 = (bf16[128,2048]{1,0:T(8,128)(2,1)S(1)}, bf16[128,2048]{1,0:T(8,128)(2,1)}, u32[]{:S(2)}, u32[]{:S(2)}) collective-permute-start(bf16[128,2048]{1,0:T(8,128)(2,1)S(1)} %get-tuple-element.163), channel_id=1, source_target_pairs={{0,16},{8,24},{16,0},{24,8},{1,17},{9,25},{17,1},{25,9},{2,18},{10... | collective-permute-start | bytes 1572872 | tf_op jit(solution)/shard_map/ppermute | solution.py:47
  197.7 188.4 %reduce-scatter.5.cloned.1.call-start = ((), (), s32[]{:S(2)}) async-start(), calls=%async_computation.7 | async-start | bytes 6488064 | tf_op jit(solution)/shard_map/reduce_scatter | solution.py:531
  219.0 23.7 %collective-permute-start.18 = (bf16[256,2048]{1,0:T(8,128)(2,1)S(1)}, bf16[256,2048]{1,0:T(8,128)(2,1)S(1)}, u32[]{:S(2)}, u32[]{:S(2)}) collective-permute-start(bf16[256,2048]{1,0:T(8,128)(2,1)S(1)} %get-tuple-element.137), channel_id=1, source_target_pairs={{0,8},{8,0},{16,24},{24,16},{1,9},{9,1},{17,25},{25,17},{2,10},{10... | collective-permute-start | bytes 3145736 | tf_op jit(solution)/shard_map/ppermute | solution.py:47
  219.5 23.8 %collective-permute-start.19 = (bf16[256,2048]{1,0:T(8,128)(2,1)S(1)}, bf16[256,2048]{1,0:T(8,128)(2,1)S(1)}, u32[]{:S(2)}, u32[]{:S(2)}) collective-permute-start(bf16[256,2048]{1,0:T(8,128)(2,1)S(1)} %get-tuple-element.137), channel_id=1, source_target_pairs={{0,16},{8,24},{16,0},{24,8},{1,17},{9,25},{17,1},{25,9},{2,18},{10... | collective-permute-start | bytes 3145736 | tf_op jit(solution)/shard_map/ppermute | solution.py:47
  289.8 199.8 %reduce-scatter.7.cloned.1.call-start = ((), (), s32[]{:S(2)}) async-start(), calls=%async_computation.8 | async-start | bytes 12976128 | tf_op jit(solution)/shard_map/reduce_scatter | solution.py:531
  339.4 269.3 %reduce-scatter.9.cloned.1.call-start = ((), (), s32[]{:S(2)}) async-start(), calls=%async_computation.9 | async-start | bytes 2359296 | tf_op jit(solution)/shard_map/reduce_scatter | solution.py:531
  345.5 24.6 %collective-permute-start.22 = (bf16[128,2048]{1,0:T(8,128)(2,1)}, bf16[128,2048]{1,0:T(8,128)(2,1)S(1)}, u32[]{:S(2)}, u32[]{:S(2)}) collective-permute-start(bf16[128,2048]{1,0:T(8,128)(2,1)} %get-tuple-element.161), channel_id=1, source_target_pairs={{0,8},{8,0},{16,24},{24,16},{1,9},{9,1},{17,25},{25,17},{2,10},{10... | collective-permute-start | bytes 1572872 | tf_op jit(solution)/shard_map/ppermute | solution.py:47
  346.1 24.0 %collective-permute-start.27 = (bf16[128,2048]{1,0:T(8,128)(2,1)}, bf16[128,2048]{1,0:T(8,128)(2,1)}, u32[]{:S(2)}, u32[]{:S(2)}) collective-permute-start(bf16[128,2048]{1,0:T(8,128)(2,1)} %get-tuple-element.159), channel_id=1, source_target_pairs={{0,16},{8,24},{16,0},{24,8},{1,17},{9,25},{17,1},{25,9},{2,18},{10... | collective-permute-start | bytes 1572872 | tf_op jit(solution)/shard_map/ppermute | solution.py:47
  386.1 24.4 %collective-permute-start.28 = (bf16[256,2048]{1,0:T(8,128)(2,1)}, bf16[256,2048]{1,0:T(8,128)(2,1)S(1)}, u32[]{:S(2)}, u32[]{:S(2)}) collective-permute-start(bf16[256,2048]{1,0:T(8,128)(2,1)} %get-tuple-element.86), channel_id=1, source_target_pairs={{0,8},{8,0},{16,24},{24,16},{1,9},{9,1},{17,25},{25,17},{2,10},{10... | collective-permute-start | bytes 3145736 | tf_op jit(solution)/shard_map/ppermute | solution.py:47
  387.6 24.2 %collective-permute-start.29 = (bf16[256,2048]{1,0:T(8,128)(2,1)}, bf16[256,2048]{1,0:T(8,128)(2,1)S(1)}, u32[]{:S(2)}, u32[]{:S(2)}) collective-permute-start(bf16[256,2048]{1,0:T(8,128)(2,1)} %get-tuple-element.86), channel_id=1, source_target_pairs={{0,16},{8,24},{16,0},{24,8},{1,17},{9,25},{17,1},{25,9},{2,18},{10... | collective-permute-start | bytes 3145736 | tf_op jit(solution)/shard_map/ppermute | solution.py:47
  453.7 24.7 %collective-permute-start.34 = (bf16[128,2048]{1,0:T(8,128)(2,1)}, bf16[128,2048]{1,0:T(8,128)(2,1)}, u32[]{:S(2)}, u32[]{:S(2)}) collective-permute-start(bf16[128,2048]{1,0:T(8,128)(2,1)} %get-tuple-element.155), channel_id=1, source_target_pairs={{0,8},{8,0},{16,24},{24,16},{1,9},{9,1},{17,25},{25,17},{2,10},{10... | collective-permute-start | bytes 1572872 | tf_op jit(solution)/shard_map/ppermute | solution.py:47
  454.2 24.2 %collective-permute-start.39 = (bf16[128,2048]{1,0:T(8,128)(2,1)}, bf16[128,2048]{1,0:T(8,128)(2,1)}, u32[]{:S(2)}, u32[]{:S(2)}) collective-permute-start(bf16[128,2048]{1,0:T(8,128)(2,1)} %get-tuple-element.153), channel_id=1, source_target_pairs={{0,16},{8,24},{16,0},{24,8},{1,17},{9,25},{17,1},{25,9},{2,18},{10... | collective-permute-start | bytes 1572872 | tf_op jit(solution)/shard_map/ppermute | solution.py:47
  472.9 173.0 %reduce-scatter.11.cloned.1.call-start = ((), (), s32[]{:S(2)}) async-start(), calls=%async_computation.10 | async-start | bytes 9437184 | tf_op jit(solution)/shard_map/reduce_scatter | solution.py:531
  489.5 33.3 %collective-permute-start.42 = (bf16[256,2816]{1,0:T(8,128)(2,1)}, bf16[256,2816]{1,0:T(8,128)(2,1)}, u32[]{:S(2)}, u32[]{:S(2)}) collective-permute-start(bf16[256,2816]{1,0:T(8,128)(2,1)} %reduce-scatter.7.cloned.1.call-done), channel_id=1, source_target_pairs={{0,8},{8,0},{16,24},{24,16},{1,9},{9,1},{17,25},{25,17},{2,10},{10... | collective-permute-start | bytes 4325384 | tf_op jit(solution)/shard_map/ppermute | solution.py:47
  491.0 33.3 %collective-permute-start.43 = (bf16[256,2816]{1,0:T(8,128)(2,1)}, bf16[256,2816]{1,0:T(8,128)(2,1)}, u32[]{:S(2)}, u32[]{:S(2)}) collective-permute-start(bf16[256,2816]{1,0:T(8,128)(2,1)} %reduce-scatter.7.cloned.1.call-done), channel_id=1, source_target_pairs={{0,16},{8,24},{16,0},{24,8},{1,17},{9,25},{17,1},{25,9},{2,18},{10... | collective-permute-start | bytes 4325384 | tf_op jit(solution)/shard_map/ppermute | solution.py:47
  561.0 44.1 %collective-permute-start.46 = (bf16[128,2048]{1,0:T(8,128)(2,1)S(1)}, bf16[128,2048]{1,0:T(8,128)(2,1)S(1)}, u32[]{:S(2)}, u32[]{:S(2)}) collective-permute-start(bf16[128,2048]{1,0:T(8,128)(2,1)S(1)} %get-tuple-element.144), channel_id=1, source_target_pairs={{0,8},{8,0},{16,24},{24,16},{1,9},{9,1},{17,25},{25,17},{2,10},{10... | collective-permute-start | bytes 1572872 | tf_op jit(solution)/shard_map/ppermute | solution.py:47
  562.1 44.3 %collective-permute-start.51 = (bf16[128,2048]{1,0:T(8,128)(2,1)S(1)}, bf16[128,2048]{1,0:T(8,128)(2,1)S(1)}, u32[]{:S(2)}, u32[]{:S(2)}) collective-permute-start(bf16[128,2048]{1,0:T(8,128)(2,1)S(1)} %get-tuple-element.145), channel_id=1, source_target_pairs={{0,16},{8,24},{16,0},{24,8},{1,17},{9,25},{17,1},{25,9},{2,18},{10... | collective-permute-start | bytes 1572872 | tf_op jit(solution)/shard_map/ppermute | solution.py:47
  575.1 32.2 %collective-permute-start.48 = (bf16[128,2048]{1,0:T(8,128)(2,1)S(1)}, bf16[128,2048]{1,0:T(8,128)(2,1)S(1)}, u32[]{:S(2)}, u32[]{:S(2)}) collective-permute-start(bf16[128,2048]{1,0:T(8,128)(2,1)S(1)} %get-tuple-element.148), channel_id=1, source_target_pairs={{0,8},{8,0},{16,24},{24,16},{1,9},{9,1},{17,25},{25,17},{2,10},{10... | collective-permute-start | bytes 1572872 | tf_op jit(solution)/shard_map/ppermute | solution.py:47
  576.1 31.2 %collective-permute-start.50 = (bf16[128,2048]{1,0:T(8,128)(2,1)S(1)}, bf16[128,2048]{1,0:T(8,128)(2,1)S(1)}, u32[]{:S(2)}, u32[]{:S(2)}) collective-permute-start(bf16[128,2048]{1,0:T(8,128)(2,1)S(1)} %get-tuple-element.149), channel_id=1, source_target_pairs={{0,16},{8,24},{16,0},{24,8},{1,17},{9,25},{17,1},{25,9},{2,18},{10... | collective-permute-start | bytes 1572872 | tf_op jit(solution)/shard_map/ppermute | solution.py:47
  577.1 26.1 %collective-permute-start.59 = (bf16[88,2048]{1,0:T(8,128)(2,1)S(1)}, bf16[88,2048]{1,0:T(8,128)(2,1)S(1)}, u32[]{:S(2)}, u32[]{:S(2)}) collective-permute-start(bf16[88,2048]{1,0:T(8,128)(2,1)S(1)} %slice.225), channel_id=1, source_target_pairs={{0,16},{8,24},{16,0},{24,8},{1,17},{9,25},{17,1},{25,9},{2,18},{10... | collective-permute-start | bytes 1081352 | tf_op jit(solution)/shard_map/ppermute | solution.py:47
  605.1 36.9 %collective-permute-start.57 = (bf16[128,2816]{1,0:T(8,128)(2,1)}, bf16[128,2816]{1,0:T(8,128)(2,1)}, u32[]{:S(2)}, u32[]{:S(2)}) collective-permute-start(bf16[128,2816]{1,0:T(8,128)(2,1)} %slice.223), channel_id=1, source_target_pairs={{0,16},{8,24},{16,0},{24,8},{1,17},{9,25},{17,1},{25,9},{2,18},{10... | collective-permute-start | bytes 2162696 | tf_op jit(solution)/shard_map/ppermute | solution.py:47
  606.4 37.7 %collective-permute-start.58 = (bf16[128,2816]{1,0:T(8,128)(2,1)}, bf16[128,2816]{1,0:T(8,128)(2,1)}, u32[]{:S(2)}, u32[]{:S(2)}) collective-permute-start(bf16[128,2816]{1,0:T(8,128)(2,1)} %slice.224), channel_id=1, source_target_pairs={{0,8},{8,0},{16,24},{24,16},{1,9},{9,1},{17,25},{25,17},{2,10},{10... | collective-permute-start | bytes 2162696 | tf_op jit(solution)/shard_map/ppermute | solution.py:47
  647.4 23.4 %collective-permute-start.65 = (bf16[256,2048]{1,0:T(8,128)(2,1)}, bf16[256,2048]{1,0:T(8,128)(2,1)S(1)}, u32[]{:S(2)}, u32[]{:S(2)}) collective-permute-start(bf16[256,2048]{1,0:T(8,128)(2,1)} %reduce-scatter.11.cloned.1.call-done), channel_id=1, source_target_pairs={{0,16},{8,24},{16,0},{24,8},{1,17},{9,25},{17,1},{25,9},{2,18},{10... | collective-permute-start | bytes 3145736 | tf_op jit(solution)/shard_map/ppermute | solution.py:47
  (95 other events, 1438.5 us)
Sparse Core Ops, SparseCore 0:
  12.2 102.0 all-gather.3
  116.5 109.5 all-gather.7
  228.4 62.1 all-gather.5
  293.2 76.3 reduce-scatter.4
  371.8 117.6 reduce-scatter.6
  492.2 36.2 reduce-scatter.8
  537.9 97.6 reduce-scatter.10

commit v5 on v4

--- a/solution.py
+++ b/solution.py
@@ -463,16 +463,6 @@
     return total, jnp.zeros_like(total), jnp.ones((1,), jnp.int32)
 
 
-def everywhere(value):
-    for axis in ("seq", "dp"):
-        bit = 1
-        while bit < lax.axis_size(axis):
-            pairs = [(s, s ^ bit) for s in range(lax.axis_size(axis))]
-            value = value + lax.ppermute(value, axis, pairs)
-            bit *= 2
-    return value
-
-
 def shards(
     block_input,
     lengths,
@@ -678,35 +668,42 @@
     )
 
     gu_parts = gather_begin(later(gu_rows, result))
-    z_part = dot_first(h_all, later(dz, result, gu_parts), BF)
-    z_rows = scatter_seq(z_part)
-    h_part, d_norm_gain = against_rows(later(dz, z_part), both, h_all, norm_gain[None])
-    down_parts = gather_begin(later(down_rows, z_part))
+    dz = later(dz, result, gu_parts)
+    fv_part = dot_first(h_all, dz[:, : 2 * mine], BF)
+    fv_rows = scatter_seq(later(fv_part, o_rows))
+    h_part, d_norm_gain = against_rows(later(dz, fv_part), both, h_all, norm_gain[None])
+    down_parts = gather_begin(later(down_rows, fv_part))
     h_part, down_parts = lax.optimization_barrier((h_part, down_parts))
     onward, at_hand = scatter_begin(h_part)
-    gu_parts, down_parts = later((gu_parts, down_parts), onward)
-    gu_parts, down_parts = gather_end(*gu_parts), gather_end(*down_parts)
-    d_h = scatter_end(onward, at_hand)
 
     zero = jnp.zeros((mine,), F32)
     d_bound = to_heads([d_bound[0], zero, zero, zero], 0)
     small = jnp.concatenate([d_norm_gain[0], d_ffn_gain, d_bound, d_gain[0]])
-    small, o_rows = later((small, o_rows), d_h)
-    small = everywhere(small)
+    extra = jnp.pad(small, (0, 32 * mine - small.shape[0])).astype(BF).reshape(1, 16, 2 * mine)
+    qg_part = dot_first(h_all, later(dz, h_part)[:, 2 * mine :], BF)
+    qg_part = jnp.concatenate(
+        [qg_part.reshape(seqs, -1, 2 * mine), jnp.broadcast_to(extra, (seqs,) + extra.shape[1:])], axis=1
+    )
+    z_rows = scatter_seq(qg_part.reshape(-1, 2 * mine))
+
+    gu_parts, down_parts, o_rows = later((gu_parts, down_parts, o_rows), onward)
+    gu_parts, down_parts = gather_end(*gu_parts), gather_end(*down_parts)
+    d_h = scatter_end(onward, at_hand)
     if natural:
+        o_rows = later(o_rows, d_h)
         o_all = (o_rows, swap(o_rows, 1), swap(o_rows, 2), swap(o_rows, 3))
         grad_o = jnp.concatenate(absolute(o_all), axis=0).astype(F32)
     else:
-        o_all = ()
         grad_o = lax.psum(o_rows.astype(F32), "dp")
-    z_rows = later(z_rows, gu_parts, down_parts, d_h, small, o_all)
+    fv_parts = gather_parts(later(fv_rows, down_parts))
+    qg_parts = gather_parts(later(z_rows, fv_parts[1:3], d_h))
 
     order = jnp.arange(4, dtype=jnp.int32) ^ dp.astype(jnp.int32)
 
-    def whole_rows(parts, kernel, columns, flat):
-        part, total = parts[0].shape[0], 4 * columns
+    def whole_rows(parts, kernel, columns, flat, part=None):
+        part, total = part or parts[0].shape[0], 4 * columns
         count = parts[0].shape[1] // columns
-        blocks = jnp.concatenate(parts, axis=0).reshape(4, part, count * columns)
+        blocks = jnp.concatenate(parts, axis=0).reshape(4, -1, count * columns)
         if not flat:
             cut = [blocks[k] for k in range(4)]
             return [
@@ -726,7 +723,10 @@
     join_hidden = functools.partial(hidden_kernel, chunk, seqs)
     grad_gate, grad_up = whole_rows(gu_parts, join_hidden, ff, chunk % 16 == 0)
     join_heads = functools.partial(heads_kernel, heads)
-    grad_f, grad_i, grad_q, grad_g = whole_rows(gather_parts(z_rows), join_heads, mine, True)
+    grad_f, grad_i = whole_rows(fv_parts, join_heads, mine, True)
+    grad_q, grad_g = whole_rows(qg_parts, join_heads, mine, True, fv_rows.shape[0])
+    small = jnp.concatenate(qg_parts, axis=0).reshape(4, -1, 2 * mine)[:, fv_rows.shape[0] :]
+    small = jnp.sum(small.astype(F32), axis=0).reshape(-1)
 
     u1 = d_h * norm_gain
     d_x = d_y + r1 * u1 - x * (r1 * r1 * r1) * jnp.mean(u1 * x, axis=-1, keepdims=True)
@@ -740,7 +740,7 @@
         grad_i,
         grad_g,
         small[2 * width : 3 * width],
-        small[3 * width :],
+        small[3 * width : 3 * width + head_dim],
         grad_o,
         small[width : 2 * width],
         grad_gate,

time: 702 us -> 702 us (level)
  waiting for transfers between devices: 282 us -> 293 us
  local copies, waits for them, and re-layouts: 69.8 us -> 61.8 us
    ppermute x57 -> x61, waiting for transfers between devices: 256 us -> 275 us  [swap(): return lax.ppermute(value, 'dp', [(s, s ^ bits) for s in range(count)])]
    ppermute x5 -> x0, waiting for transfers between devices: 10.2 us -> none  [everywhere(): value = value + lax.ppermute(value, axis, pairs)]
    unnamed x128 -> x131, local copies, waits for them, and re-layouts: 35.7 us -> 31.9 us
    ppermute x57 -> x61, starting transfers between devices: 65.5 us -> 68.3 us  [swap(): return lax.ppermute(value, 'dp', [(s, s ^ bits) for s in range(count)])]
    dot_general x4 -> x5, matrix products: 44.5 us -> 46.4 us  [dot_first(): lax.dot_general(left, right, (((0,), (0,)), ((), ())), preferred_element_...]
    pallas_call x13 -> x14, Pallas kernels: 91.2 us -> 90.7 us  [call(): pl.pallas_call(kernel, grid_spec=pltpu.PrefetchScalarGridSpec(num_scalar_...]
  transfers between devices with their start and end apart: 75 -> 75, of which waited for: 47 -> 45; matrix products, arithmetic and copies ran while one was open for 30% -> 28% of each run, Pallas kernels for 12% -> 12%
where the time goes in v5:
time: 702 us; the launch traced here: 696 us
  waiting for transfers between devices  293 us (42%)
  matrix products  110 us (16%)
  Pallas kernels  90.7 us (13%)
  starting transfers between devices  81.7 us (12%)
  local copies, waits for them, and re-layouts  61.8 us (9%)
  other arithmetic  43.1 us (6%)
  between operations  15.4 us (2%)
    ppermute x61, waiting for transfers between devices, swap(): return lax.ppermute(value, 'dp', [(s, s ^ bits) for s in range(count)])  275 us
    pallas_call x14, Pallas kernels, call(): pl.pallas_call(kernel, grid_spec=pltpu.PrefetchScalarGridSpec(num_scalar_...  90.7 us
    ppermute x61, starting transfers between devices, swap(): return lax.ppermute(value, 'dp', [(s, s ^ bits) for s in range(count)])  68.3 us
    dot_general x5, matrix products, dot_first(): lax.dot_general(left, right, (((0,), (0,)), ((), ())), preferred_element_...  46.4 us
    dot_general x3, matrix products, dot_last(): lax.dot_general(left, right, (((1,), (1,)), ((), ())), preferred_element_...  34.3 us
    unnamed x131, local copies, waits for them, and re-layouts  31.9 us
    dot_general x3, matrix products, mm(): return jnp.dot(left, right, preferred_element_type=F32).astype(kind)  29.4 us
  transfers between devices with their start and end apart: 75, of which 45 were waited for; matrix products, arithmetic and copies ran while one was open for 28% of the time, Pallas kernels for 12%

profile of v5, /device:TPU:0, one launch (start us, length us, event | category | flops | bytes accessed | tf_op | source)
XLA Modules:
  0.0 695.5 jit_solution(6738741643778709339)
XLA Ops:
  19.1 21.8 %collective-permute-done = bf16[256,2048]{1,0:T(8,128)(2,1)S(1)} collective-permute-done((bf16[256,2048]{1,0:T(8,128)(2,1)}, bf16[256,2048]{1,0:T(8,128)(2,1)S(1)}, u32[]{:S(2)}, u32[]{:S(2)}) %collective-permute-start) | collective-permute-done | bytes 1048608 | tf_op jit(solution)/shard_map/ppermute | solution.py:47
  46.5 7.8 %collective-permute-done.2 = bf16[128,2048]{1,0:T(8,128)(2,1)S(1)} collective-permute-done((bf16[128,2048]{1,0:T(8,128)(2,1)S(1)}, bf16[128,2048]{1,0:T(8,128)(2,1)S(1)}, u32[]{:S(2)}, u32[]{:S(2)}) %collective-permute-start.2) | collective-permute-done | bytes 524320 | tf_op jit(solution)/shard_map/ppermute | solution.py:47
  69.7 20.5 %collective-permute-done.4 = bf16[256,2048]{1,0:T(8,128)(2,1)S(1)} collective-permute-done((bf16[256,2048]{1,0:T(8,128)(2,1)S(1)}, bf16[256,2048]{1,0:T(8,128)(2,1)S(1)}, u32[]{:S(2)}, u32[]{:S(2)}) %collective-permute-start.4) | collective-permute-done | bytes 1048608 | tf_op jit(solution)/shard_map/ppermute | solution.py:47
  104.3 10.1 %all-gather.4.cloned.1.call-done.right_ref = bf16[2048,2560]{1,0:T(8,128)(2,1)} async-done(((bf16[256,2560]{1,0:T(8,128)(2,1)}), bf16[2048,2560]{1,0:T(8,128)(2,1)}) %all-gather.4.cloned.1.call-update) | async-done | bytes 10485776 | tf_op jit(solution)/shard_map/all_gather | solution.py:518
  114.4 7.8 %shard_map.255.f_ref.v_ref = f32[1024,1024]{1,0:T(8,128)S(1)} custom-call(bf16[1024,2048]{1,0:T(8,128)(2,1)} %constant_dynamic-update-slice_fusion.left_ref.beside_ref, bf16[2048,2560]{1,0:T(8,128)(2,1)} %all-gather.4.cloned.1.call-done.right_ref), custom_call_target="tpu_custom_call" | custom-call | flops 80000000 | bytes 65536 | tf_op jit(solution)/shard_map/pallas_call | solution.py:343
  138.8 7.9 %shard_map.258.q_ref.g_ref = f32[1024,1024]{1,0:T(8,128)S(1)} custom-call(bf16[1024,2048]{1,0:T(8,128)(2,1)} %constant_dynamic-update-slice_fusion.left_ref.beside_ref, bf16[2048,2560]{1,0:T(8,128)(2,1)} %all-gather.4.cloned.1.call-done.right_ref), custom_call_target="tpu_custom_call" | custom-call | flops 80000000 | bytes 65536 | tf_op jit(solution)/shard_map/pallas_call | solution.py:343
  148.6 11.8 %shard_map.259 = (f32[1024,512]{1,0:T(8,128)S(1)}, bf16[1024,512]{1,0:T(8,128)(2,1)S(1)}) custom-call(s32[4,2]{1,0:T(4,128)S(1)} %broadcast_in_dim.43.starts, f32[1024,1024]{1,0:T(8,128)} %copy-done.2, f32[1024,1024]{1,0:T(8,128)} %copy-done.2, f32[1024,1024]{1,0:T(8,128)} %copy-done.3, f32[1,512]{1,0:T(1,128)S(1)} %dynamic-slice_bitcast_fusion.b_ref), custom_call_target="tpu_custom_call" | custom-call | flops 30000000 | bytes 65536 | tf_op jit(solution)/shard_map/pallas_call | solution.py:343
  180.4 10.8 %collective-permute-done.13 = bf16[128,2048]{1,0:T(8,128)(2,1)S(1)} collective-permute-done((bf16[128,2048]{1,0:T(8,128)(2,1)S(1)}, bf16[128,2048]{1,0:T(8,128)(2,1)S(1)}, u32[]{:S(2)}, u32[]{:S(2)}) %collective-permute-start.13) | collective-permute-done | bytes 524320 | tf_op jit(solution)/shard_map/ppermute | solution.py:47
  204.0 9.5 %collective-permute-done.14 = bf16[128,2048]{1,0:T(8,128)(2,1)S(1)} collective-permute-done((bf16[128,2048]{1,0:T(8,128)(2,1)S(1)}, bf16[128,2048]{1,0:T(8,128)(2,1)S(1)}, u32[]{:S(2)}, u32[]{:S(2)}) %collective-permute-start.14) | collective-permute-done | bytes 524320 | tf_op jit(solution)/shard_map/ppermute | solution.py:47
  219.8 22.5 %collective-permute-done.18 = bf16[256,2048]{1,0:T(8,128)(2,1)S(1)} collective-permute-done((bf16[256,2048]{1,0:T(8,128)(2,1)S(1)}, bf16[256,2048]{1,0:T(8,128)(2,1)S(1)}, u32[]{:S(2)}, u32[]{:S(2)}) %collective-permute-start.18) | collective-permute-done | bytes 1048608 | tf_op jit(solution)/shard_map/ppermute | solution.py:47
  247.1 6.9 collective-permute-done.20
  255.7 17.3 %fusion.31 = f32[1024,2816]{1,0:T(8,128)S(1)} fusion(bf16[1024,2048]{1,0:T(8,128)(2,1)} %constant_dynamic-update-slice_fusion.10, bf16[2048,2816]{0,1:T(8,128)(2,1)} %all-gather.8.cloned.1.call-done), kind=kOutput, calls=%fused_computation.161 | convolution fusion | flops 11811160064 | bytes 27262976 | tf_op jit(solution)/shard_map/dot_general | solution.py:30
  278.8 10.7 %convolution_convert_fusion.1 = bf16[1408,2048]{1,0:T(8,128)(2,1)} fusion(bf16[1024,1408]{1,0:T(8,128)(2,1)S(1)} %multiply_convert_fusion.2, bf16[1024,2048]{1,0:T(8,128)(2,1)} %constant_dynamic-update-slice_fusion.5), kind=kOutput, calls=%fused_computation.1 | convolution fusion | flops 5908463616 | bytes 12845056 | tf_op jit(solution)/shard_map/dot_general | solution.py:34
  290.5 14.2 %multiply_convert_fusion.1 = (bf16[1024,1408]{1,0:T(8,128)(2,1)S(1)}, bf16[1024,1408]{1,0:T(8,128)(2,1)S(1)}) fusion(f32[1024,2816]{1,0:T(8,128)} %copy-done.27, bf16[1024,2048]{1,0:T(8,128)(2,1)} %constant_dynamic-update-slice_fusion.5, bf16[1408,2048]{1,0:T(8,128)(2,1)} %all-gather.6.cloned.1.call-done), kind=kOutput, calls=%fused_computation.4 | convolution fusion | flops 5924323328 | bytes 27262976 | tf_op jit(solution)/shard_map/dot_general | solution.py:40
  305.2 16.3 %convolution_convert_fusion.2 = bf16[1024,2048]{1,0:T(8,128)(2,1)} fusion(bf16[2048,2816]{0,1:T(8,128)(2,1)} %all-gather.8.cloned.1.call-done, bf16[1024,1408]{1,0:T(8,128)(2,1)S(1)} %get-tuple-element.149, bf16[1024,1408]{1,0:T(8,128)(2,1)S(1)} %get-tuple-element.148), kind=kOutput, calls=%fused_computation.14 | convolution fusion | flops 11824791552 | bytes 21495808 | tf_op jit(solution)/shard_map/dot_general | solution.py:40
  321.5 17.9 %convolution_convert_fusion = bf16[2048,2816]{1,0:T(8,128)(2,1)} fusion(bf16[1024,2048]{1,0:T(8,128)(2,1)} %constant_dynamic-update-slice_fusion.10, bf16[1024,2816]{1,0:T(8,128)(2,1)S(1)} %pad_maximum_fusion), kind=kOutput, calls=%fused_computation | convolution fusion | flops 11816927232 | bytes 21495808 | tf_op jit(solution)/shard_map/dot_general | solution.py:34
  346.4 10.7 %collective-permute-done.23 = bf16[128,2048]{1,0:T(8,128)(2,1)S(1)} collective-permute-done((bf16[128,2048]{1,0:T(8,128)(2,1)S(1)}, bf16[128,2048]{1,0:T(8,128)(2,1)S(1)}, u32[]{:S(2)}, u32[]{:S(2)}) %collective-permute-start.23) | collective-permute-done | bytes 524320 | tf_op jit(solution)/shard_map/ppermute | solution.py:47
  369.9 10.4 %collective-permute-done.24 = bf16[128,2048]{1,0:T(8,128)(2,1)} collective-permute-done((bf16[128,2048]{1,0:T(8,128)(2,1)}, bf16[128,2048]{1,0:T(8,128)(2,1)}, u32[]{:S(2)}, u32[]{:S(2)}) %collective-permute-start.24) | collective-permute-done | bytes 524320 | tf_op jit(solution)/shard_map/ppermute | solution.py:47
  388.0 9.7 %convolution_convert_fusion.3 = bf16[1024,2048]{1,0:T(8,128)(2,1)S(1)} fusion(bf16[1024,1408]{1,0:T(8,128)(2,1)} %copy-done.34, bf16[1408,2048]{1,0:T(8,128)(2,1)} %all-gather.6.cloned.1.call-done), kind=kOutput, calls=%fused_computation.15 | convolution fusion | flops 5907677184 | bytes 12845056 | tf_op jit(solution)/shard_map/dot_general | solution.py:30
  397.7 12.7 %collective-permute-done.28 = bf16[256,2048]{1,0:T(8,128)(2,1)S(1)} collective-permute-done((bf16[256,2048]{1,0:T(8,128)(2,1)}, bf16[256,2048]{1,0:T(8,128)(2,1)S(1)}, u32[]{:S(2)}, u32[]{:S(2)}) %collective-permute-start.28) | collective-permute-done | bytes 1048608 | tf_op jit(solution)/shard_map/ppermute | solution.py:47
  412.9 9.9 %collective-permute-done.30 = bf16[128,2048]{1,0:T(8,128)(2,1)S(1)} collective-permute-done((bf16[128,2048]{1,0:T(8,128)(2,1)S(1)}, bf16[128,2048]{1,0:T(8,128)(2,1)S(1)}, u32[]{:S(2)}, u32[]{:S(2)}) %collective-permute-start.30) | collective-permute-done | bytes 524320 | tf_op jit(solution)/shard_map/ppermute | solution.py:47
  442.4 7.3 %collective-permute-done.32 = bf16[256,2048]{1,0:T(8,128)(2,1)S(1)} collective-permute-done((bf16[256,2048]{1,0:T(8,128)(2,1)}, bf16[256,2048]{1,0:T(8,128)(2,1)S(1)}, u32[]{:S(2)}, u32[]{:S(2)}) %collective-permute-start.32) | collective-permute-done | bytes 1048608 | tf_op jit(solution)/shard_map/ppermute | solution.py:47
  458.0 8.2 %collective-permute-done.35 = bf16[128,2048]{1,0:T(8,128)(2,1)} collective-permute-done((bf16[128,2048]{1,0:T(8,128)(2,1)}, bf16[128,2048]{1,0:T(8,128)(2,1)}, u32[]{:S(2)}, u32[]{:S(2)}) %collective-permute-start.35) | collective-permute-done | bytes 524320 | tf_op jit(solution)/shard_map/ppermute | solution.py:47
  502.8 16.1 %shard_map.263 = (bf16[1024,2048]{1,0:T(8,128)(2,1)}, f32[1,512]{1,0:T(1,128)S(1)}) custom-call(s32[4,2]{1,0:T(4,128)S(1)} %copy-done.16, s32[1]{0:T(128)} %bitcast.20.whole, f32[1024,1024]{1,0:T(8,128)} %copy-done.2, f32[1024,1024]{1,0:T(8,128)} %copy-done.2, f32[1024,1024]{1,0:T(8,128)} %copy-done.3, f32[1,512]{1,0:T(1,128)S(1)} %copy-done.18, ...), custom_call_target="tpu_custom_call" | custom-call | flops 80000000 | bytes 65536 | tf_op jit(solution)/shard_map/pallas_call | solution.py:343
  523.6 7.9 %convolution_convert_fusion.6 = bf16[2048,1024]{1,0:T(8,128)(2,1)} fusion(bf16[1024,2048]{1,0:T(8,128)(2,1)S(1)} %copy-done.24, bf16[1024,2048]{1,0:T(8,128)(2,1)} %get-tuple-element.112.left_ref), kind=kOutput, calls=%fused_computation.18 | convolution fusion | flops 4297064448 | bytes 10485760 | tf_op jit(solution)/shard_map/dot_general | solution.py:34
  535.0 14.4 %shard_map.264 = (bf16[1024,2048]{1,0:T(8,128)(2,1)S(1)}, f32[1,2048]{1,0:T(1,128)S(1)}) custom-call(bf16[1024,2048]{1,0:T(8,128)(2,1)} %get-tuple-element.112.left_ref, bf16[2048,2560]{1,0:T(8,128)(2,1)} %all-gather.4.cloned.1.call-done.right_ref, bf16[1024,2048]{1,0:T(8,128)(2,1)} %constant_dynamic-update-slice_fusion.left_ref.beside_ref, ...), custom_call_target="tpu_custom_call" | custom-call | flops 80000000 | bytes 65536 | tf_op jit(solution)/shard_map/pallas_call | solution.py:343
  551.7 7.5 %convolution_convert_fusion.5 = bf16[2048,1024]{1,0:T(8,128)(2,1)S(1)} fusion(bf16[1024,2048]{1,0:T(8,128)(2,1)} %constant_dynamic-update-slice_fusion.left_ref.beside_ref, bf16[1024,2048]{1,0:T(8,128)(2,1)} %get-tuple-element.112.left_ref), kind=kOutput, calls=%fused_computation.17 | convolution fusion | flops 4297064448 | bytes 10485760 | tf_op jit(solution)/shard_map/dot_general | solution.py:34
  567.9 10.5 %collective-permute-done.47 = bf16[128,2048]{1,0:T(8,128)(2,1)S(1)} collective-permute-done((bf16[128,2048]{1,0:T(8,128)(2,1)S(1)}, bf16[128,2048]{1,0:T(8,128)(2,1)S(1)}, u32[]{:S(2)}, u32[]{:S(2)}) %collective-permute-start.47) | collective-permute-done | bytes 524320 | tf_op jit(solution)/shard_map/ppermute | solution.py:47
  588.6 8.7 %collective-permute-done.52 = bf16[88,2048]{1,0:T(8,128)(2,1)S(1)} collective-permute-done((bf16[88,2048]{1,0:T(8,128)(2,1)S(1)}, bf16[88,2048]{1,0:T(8,128)(2,1)S(1)}, u32[]{:S(2)}, u32[]{:S(2)}) %collective-permute-start.52) | collective-permute-done | bytes 360480 | tf_op jit(solution)/shard_map/ppermute | solution.py:47
  618.1 15.0 %collective-permute-done.65 = bf16[128,2816]{1,0:T(8,128)(2,1)S(1)} collective-permute-done((bf16[128,2816]{1,0:T(8,128)(2,1)S(1)}, bf16[128,2816]{1,0:T(8,128)(2,1)S(1)}, u32[]{:S(2)}, u32[]{:S(2)}) %collective-permute-start.65) | collective-permute-done | bytes 720928 | tf_op jit(solution)/shard_map/ppermute | solution.py:47
  643.0 9.4 %collective-permute-done.54 = bf16[256,1024]{1,0:T(8,128)(2,1)S(1)} collective-permute-done((bf16[256,1024]{1,0:T(8,128)(2,1)}, bf16[256,1024]{1,0:T(8,128)(2,1)S(1)}, u32[]{:S(2)}, u32[]{:S(2)}) %collective-permute-start.54) | collective-permute-done | bytes 524320 | tf_op jit(solution)/shard_map/ppermute | solution.py:47
  661.8 10.3 %collective-permute-done.61 = bf16[128,1024]{1,0:T(8,128)(2,1)S(1)} collective-permute-done((bf16[128,1024]{1,0:T(8,128)(2,1)S(1)}, bf16[128,1024]{1,0:T(8,128)(2,1)S(1)}, u32[]{:S(2)}, u32[]{:S(2)}) %collective-permute-start.61) | collective-permute-done | bytes 262176 | tf_op jit(solution)/shard_map/ppermute | solution.py:47
  (365 shorter events, 297.5 us)
Async XLA Ops:
  7.2 107.2 %all-gather.4.cloned.1.call-start = ((), (), s32[]{:S(2)}) async-start(), calls=%async_computation.5 | async-start | bytes 11796480 | tf_op jit(solution)/shard_map/all_gather | solution.py:518
  12.1 243.6 %all-gather.8.cloned.1.call-start = ((), (), s32[]{:S(2)}) async-start(), calls=%async_computation.7 | async-start | bytes 12976128 | tf_op jit(solution)/shard_map/all_gather | solution.py:518
  14.7 26.3 %collective-permute-start = (bf16[256,2048]{1,0:T(8,128)(2,1)}, bf16[256,2048]{1,0:T(8,128)(2,1)S(1)}, u32[]{:S(2)}, u32[]{:S(2)}) collective-permute-start(bf16[256,2048]{1,0:T(8,128)(2,1)} %get-tuple-element.147), channel_id=1, source_target_pairs={{0,8},{8,0},{16,24},{24,16},{1,9},{9,1},{17,25},{25,17},{2,10},{10... | collective-permute-start | bytes 3145736 | tf_op jit(solution)/shard_map/ppermute | solution.py:47
  17.6 25.3 %collective-permute-start.1 = (bf16[256,2048]{1,0:T(8,128)(2,1)}, bf16[256,2048]{1,0:T(8,128)(2,1)S(1)}, u32[]{:S(2)}, u32[]{:S(2)}) collective-permute-start(bf16[256,2048]{1,0:T(8,128)(2,1)} %get-tuple-element.147), channel_id=1, source_target_pairs={{0,16},{8,24},{16,0},{24,8},{1,17},{9,25},{17,1},{25,9},{2,18},{10... | collective-permute-start | bytes 3145736 | tf_op jit(solution)/shard_map/ppermute | solution.py:47
  66.6 223.9 %all-gather.6.cloned.1.call-start = ((), (), s32[]{:S(2)}) async-start(), calls=%async_computation.6 | async-start | bytes 6488064 | tf_op jit(solution)/shard_map/all_gather | solution.py:518
  67.0 23.1 %collective-permute-start.4 = (bf16[256,2048]{1,0:T(8,128)(2,1)S(1)}, bf16[256,2048]{1,0:T(8,128)(2,1)S(1)}, u32[]{:S(2)}, u32[]{:S(2)}) collective-permute-start(bf16[256,2048]{1,0:T(8,128)(2,1)S(1)} %copy-done.31), channel_id=1, source_target_pairs={{0,8},{8,0},{16,24},{24,16},{1,9},{9,1},{17,25},{25,17},{2,10},{10... | collective-permute-start | bytes 3145736 | tf_op jit(solution)/shard_map/ppermute | solution.py:47
  68.5 24.0 %collective-permute-start.5 = (bf16[256,2048]{1,0:T(8,128)(2,1)S(1)}, bf16[256,2048]{1,0:T(8,128)(2,1)S(1)}, u32[]{:S(2)}, u32[]{:S(2)}) collective-permute-start(bf16[256,2048]{1,0:T(8,128)(2,1)S(1)} %copy-done.31), channel_id=1, source_target_pairs={{0,16},{8,24},{16,0},{24,8},{1,17},{9,25},{17,1},{25,9},{2,18},{10... | collective-permute-start | bytes 3145736 | tf_op jit(solution)/shard_map/ppermute | solution.py:47
  135.8 27.8 %collective-permute-start.11 = (bf16[256,2048]{1,0:T(8,128)(2,1)}, bf16[256,2048]{1,0:T(8,128)(2,1)}, u32[]{:S(2)}, u32[]{:S(2)}) collective-permute-start(bf16[256,2048]{1,0:T(8,128)(2,1)} %get-tuple-element.77), channel_id=1, source_target_pairs={{0,8},{8,0},{16,24},{24,16},{1,9},{9,1},{17,25},{25,17},{2,10},{10... | collective-permute-start | bytes 3145736 | tf_op jit(solution)/shard_map/ppermute | solution.py:47
  137.3 24.5 %collective-permute-start.9 = (bf16[16,144,128]{2,1,0:T(8,128)(2,1)S(1)}, bf16[16,144,128]{2,1,0:T(8,128)(2,1)}, u32[]{:S(2)}, u32[]{:S(2)}) collective-permute-start(bf16[16,144,128]{2,1,0:T(8,128)(2,1)S(1)} %shard_map.257), channel_id=1, source_target_pairs={{1,3},{5,7},{9,11},{13,15},{17,19},{21,23},{25,27},{29,31}} | collective-permute-start | bytes 1769480 | tf_op jit(solution)/shard_map/ppermute | solution.py:440
  178.4 25.6 %collective-permute-start.12 = (bf16[128,2048]{1,0:T(8,128)(2,1)}, bf16[128,2048]{1,0:T(8,128)(2,1)}, u32[]{:S(2)}, u32[]{:S(2)}) collective-permute-start(bf16[128,2048]{1,0:T(8,128)(2,1)} %get-tuple-element.168), channel_id=1, source_target_pairs={{0,8},{8,0},{16,24},{24,16},{1,9},{9,1},{17,25},{25,17},{2,10},{10... | collective-permute-start | bytes 1572872 | tf_op jit(solution)/shard_map/ppermute | solution.py:47
  179.8 24.2 %collective-permute-start.17 = (bf16[128,2048]{1,0:T(8,128)(2,1)S(1)}, bf16[128,2048]{1,0:T(8,128)(2,1)}, u32[]{:S(2)}, u32[]{:S(2)}) collective-permute-start(bf16[128,2048]{1,0:T(8,128)(2,1)S(1)} %get-tuple-element.169), channel_id=1, source_target_pairs={{0,16},{8,24},{16,0},{24,8},{1,17},{9,25},{17,1},{25,9},{2,18},{10... | collective-permute-start | bytes 1572872 | tf_op jit(solution)/shard_map/ppermute | solution.py:47
  197.5 188.4 %reduce-scatter.6.cloned.1.call-start = ((), (), s32[]{:S(2)}) async-start(), calls=%async_computation.8 | async-start | bytes 6488064 | tf_op jit(solution)/shard_map/reduce_scatter | solution.py:521
  218.7 23.7 %collective-permute-start.18 = (bf16[256,2048]{1,0:T(8,128)(2,1)S(1)}, bf16[256,2048]{1,0:T(8,128)(2,1)S(1)}, u32[]{:S(2)}, u32[]{:S(2)}) collective-permute-start(bf16[256,2048]{1,0:T(8,128)(2,1)S(1)} %get-tuple-element.143), channel_id=1, source_target_pairs={{0,8},{8,0},{16,24},{24,16},{1,9},{9,1},{17,25},{25,17},{2,10},{10... | collective-permute-start | bytes 3145736 | tf_op jit(solution)/shard_map/ppermute | solution.py:47
  219.3 23.8 %collective-permute-start.19 = (bf16[256,2048]{1,0:T(8,128)(2,1)S(1)}, bf16[256,2048]{1,0:T(8,128)(2,1)S(1)}, u32[]{:S(2)}, u32[]{:S(2)}) collective-permute-start(bf16[256,2048]{1,0:T(8,128)(2,1)S(1)} %get-tuple-element.143), channel_id=1, source_target_pairs={{0,16},{8,24},{16,0},{24,8},{1,17},{9,25},{17,1},{25,9},{2,18},{10... | collective-permute-start | bytes 3145736 | tf_op jit(solution)/shard_map/ppermute | solution.py:47
  289.5 199.9 %reduce-scatter.8.cloned.1.call-start = ((), (), s32[]{:S(2)}) async-start(), calls=%async_computation.9 | async-start | bytes 12976128 | tf_op jit(solution)/shard_map/reduce_scatter | solution.py:521
  339.4 192.2 %reduce-scatter.12.cloned.1.call-start = ((), (), s32[]{:S(2)}) async-start(), calls=%async_computation.11 | async-start | bytes 2359296 | tf_op jit(solution)/shard_map/reduce_scatter | solution.py:521
  345.3 24.5 %collective-permute-start.22 = (bf16[128,2048]{1,0:T(8,128)(2,1)}, bf16[128,2048]{1,0:T(8,128)(2,1)S(1)}, u32[]{:S(2)}, u32[]{:S(2)}) collective-permute-start(bf16[128,2048]{1,0:T(8,128)(2,1)} %get-tuple-element.167), channel_id=1, source_target_pairs={{0,8},{8,0},{16,24},{24,16},{1,9},{9,1},{17,25},{25,17},{2,10},{10... | collective-permute-start | bytes 1572872 | tf_op jit(solution)/shard_map/ppermute | solution.py:47
  345.9 24.0 %collective-permute-start.27 = (bf16[128,2048]{1,0:T(8,128)(2,1)}, bf16[128,2048]{1,0:T(8,128)(2,1)}, u32[]{:S(2)}, u32[]{:S(2)}) collective-permute-start(bf16[128,2048]{1,0:T(8,128)(2,1)} %get-tuple-element.165), channel_id=1, source_target_pairs={{0,16},{8,24},{16,0},{24,8},{1,17},{9,25},{17,1},{25,9},{2,18},{10... | collective-permute-start | bytes 1572872 | tf_op jit(solution)/shard_map/ppermute | solution.py:47
  386.0 24.4 %collective-permute-start.28 = (bf16[256,2048]{1,0:T(8,128)(2,1)}, bf16[256,2048]{1,0:T(8,128)(2,1)S(1)}, u32[]{:S(2)}, u32[]{:S(2)}) collective-permute-start(bf16[256,2048]{1,0:T(8,128)(2,1)} %get-tuple-element.89), channel_id=1, source_target_pairs={{0,8},{8,0},{16,24},{24,16},{1,9},{9,1},{17,25},{25,17},{2,10},{10... | collective-permute-start | bytes 3145736 | tf_op jit(solution)/shard_map/ppermute | solution.py:47
  387.4 24.2 %collective-permute-start.29 = (bf16[256,2048]{1,0:T(8,128)(2,1)}, bf16[256,2048]{1,0:T(8,128)(2,1)S(1)}, u32[]{:S(2)}, u32[]{:S(2)}) collective-permute-start(bf16[256,2048]{1,0:T(8,128)(2,1)} %get-tuple-element.89), channel_id=1, source_target_pairs={{0,16},{8,24},{16,0},{24,8},{1,17},{9,25},{17,1},{25,9},{2,18},{10... | collective-permute-start | bytes 3145736 | tf_op jit(solution)/shard_map/ppermute | solution.py:47
  456.0 183.2 %reduce-scatter.14.cloned.1.call-start = ((), (), s32[]{:S(2)}) async-start(), calls=%async_computation.12 | async-start | bytes 4718592 | tf_op jit(solution)/shard_map/reduce_scatter | solution.py:521
  489.5 32.5 %collective-permute-start.42 = (bf16[256,2816]{1,0:T(8,128)(2,1)}, bf16[256,2816]{1,0:T(8,128)(2,1)}, u32[]{:S(2)}, u32[]{:S(2)}) collective-permute-start(bf16[256,2816]{1,0:T(8,128)(2,1)} %reduce-scatter.8.cloned.1.call-done), channel_id=1, source_target_pairs={{0,8},{8,0},{16,24},{24,16},{1,9},{9,1},{17,25},{25,17},{2,10},{10... | collective-permute-start | bytes 4325384 | tf_op jit(solution)/shard_map/ppermute | solution.py:47
  491.0 32.6 %collective-permute-start.43 = (bf16[256,2816]{1,0:T(8,128)(2,1)}, bf16[256,2816]{1,0:T(8,128)(2,1)}, u32[]{:S(2)}, u32[]{:S(2)}) collective-permute-start(bf16[256,2816]{1,0:T(8,128)(2,1)} %reduce-scatter.8.cloned.1.call-done), channel_id=1, source_target_pairs={{0,16},{8,24},{16,0},{24,8},{1,17},{9,25},{17,1},{25,9},{2,18},{10... | collective-permute-start | bytes 4325384 | tf_op jit(solution)/shard_map/ppermute | solution.py:47
  531.6 122.1 %reduce-scatter.10.cloned.1.call-start = ((), (), s32[]{:S(2)}) async-start(), calls=%async_computation.10 | async-start | bytes 5013504 | tf_op jit(solution)/shard_map/reduce_scatter | solution.py:521
  566.1 36.7 %collective-permute-start.46 = (bf16[128,2048]{1,0:T(8,128)(2,1)S(1)}, bf16[128,2048]{1,0:T(8,128)(2,1)S(1)}, u32[]{:S(2)}, u32[]{:S(2)}) collective-permute-start(bf16[128,2048]{1,0:T(8,128)(2,1)S(1)} %get-tuple-element.150), channel_id=1, source_target_pairs={{0,8},{8,0},{16,24},{24,16},{1,9},{9,1},{17,25},{25,17},{2,10},{10... | collective-permute-start | bytes 1572872 | tf_op jit(solution)/shard_map/ppermute | solution.py:47
  567.3 36.4 %collective-permute-start.51 = (bf16[128,2048]{1,0:T(8,128)(2,1)S(1)}, bf16[128,2048]{1,0:T(8,128)(2,1)S(1)}, u32[]{:S(2)}, u32[]{:S(2)}) collective-permute-start(bf16[128,2048]{1,0:T(8,128)(2,1)S(1)} %get-tuple-element.151), channel_id=1, source_target_pairs={{0,16},{8,24},{16,0},{24,8},{1,17},{9,25},{17,1},{25,9},{2,18},{10... | collective-permute-start | bytes 1572872 | tf_op jit(solution)/shard_map/ppermute | solution.py:47
  587.4 22.9 %collective-permute-start.48 = (bf16[128,2048]{1,0:T(8,128)(2,1)S(1)}, bf16[128,2048]{1,0:T(8,128)(2,1)S(1)}, u32[]{:S(2)}, u32[]{:S(2)}) collective-permute-start(bf16[128,2048]{1,0:T(8,128)(2,1)S(1)} %get-tuple-element.154), channel_id=1, source_target_pairs={{0,8},{8,0},{16,24},{24,16},{1,9},{9,1},{17,25},{25,17},{2,10},{10... | collective-permute-start | bytes 1572872 | tf_op jit(solution)/shard_map/ppermute | solution.py:47
  599.0 34.1 %collective-permute-start.65 = (bf16[128,2816]{1,0:T(8,128)(2,1)S(1)}, bf16[128,2816]{1,0:T(8,128)(2,1)S(1)}, u32[]{:S(2)}, u32[]{:S(2)}) collective-permute-start(bf16[128,2816]{1,0:T(8,128)(2,1)S(1)} %slice.262), channel_id=1, source_target_pairs={{0,16},{8,24},{16,0},{24,8},{1,17},{9,25},{17,1},{25,9},{2,18},{10... | collective-permute-start | bytes 2162696 | tf_op jit(solution)/shard_map/ppermute | solution.py:47
  602.8 30.4 %collective-permute-start.66 = (bf16[128,2816]{1,0:T(8,128)(2,1)S(1)}, bf16[128,2816]{1,0:T(8,128)(2,1)S(1)}, u32[]{:S(2)}, u32[]{:S(2)}) collective-permute-start(bf16[128,2816]{1,0:T(8,128)(2,1)S(1)} %slice.263), channel_id=1, source_target_pairs={{0,8},{8,0},{16,24},{24,16},{1,9},{9,1},{17,25},{25,17},{2,10},{10... | collective-permute-start | bytes 2162696 | tf_op jit(solution)/shard_map/ppermute | solution.py:47
  612.9 28.5 %collective-permute-start.62 = (bf16[64,2048]{1,0:T(8,128)(2,1)S(1)}, bf16[64,2048]{1,0:T(8,128)(2,1)S(1)}, u32[]{:S(2)}, u32[]{:S(2)}) collective-permute-start(bf16[64,2048]{1,0:T(8,128)(2,1)S(1)} %copy-done.42), channel_id=1, source_target_pairs={{0,24},{8,16},{16,8},{24,0},{1,25},{9,17},{17,9},{25,1},{2,26},{10... | collective-permute-start | bytes 786440 | tf_op jit(solution)/shard_map/ppermute | solution.py:47
  614.6 26.8 %collective-permute-start.63 = (bf16[64,2048]{1,0:T(8,128)(2,1)S(1)}, bf16[64,2048]{1,0:T(8,128)(2,1)S(1)}, u32[]{:S(2)}, u32[]{:S(2)}) collective-permute-start(bf16[64,2048]{1,0:T(8,128)(2,1)S(1)} %copy-done.42), channel_id=1, source_target_pairs={{0,16},{8,24},{16,0},{24,8},{1,17},{9,25},{17,1},{25,9},{2,18},{10... | collective-permute-start | bytes 786440 | tf_op jit(solution)/shard_map/ppermute | solution.py:47
  615.3 26.1 %collective-permute-start.64 = (bf16[64,2048]{1,0:T(8,128)(2,1)S(1)}, bf16[64,2048]{1,0:T(8,128)(2,1)S(1)}, u32[]{:S(2)}, u32[]{:S(2)}) collective-permute-start(bf16[64,2048]{1,0:T(8,128)(2,1)S(1)} %copy-done.42), channel_id=1, source_target_pairs={{0,8},{8,0},{16,24},{24,16},{1,9},{9,1},{17,25},{25,17},{2,10},{10... | collective-permute-start | bytes 786440 | tf_op jit(solution)/shard_map/ppermute | solution.py:47
  (92 other events, 1437.5 us)
Sparse Core Ops, SparseCore 0:
  12.2 102.0 all-gather.3
  116.5 109.5 all-gather.7
  228.4 62.0 all-gather.5
  293.2 76.3 reduce-scatter.5
  371.7 117.6 reduce-scatter.7
  492.2 36.9 reduce-scatter.11
  531.7 55.6 reduce-scatter.13
  589.7 50.6 reduce-scatter.9

commit v6 on v5

--- a/solution.py
+++ b/solution.py
@@ -669,22 +669,22 @@
 
     gu_parts = gather_begin(later(gu_rows, result))
     dz = later(dz, result, gu_parts)
-    fv_part = dot_first(h_all, dz[:, : 2 * mine], BF)
-    fv_rows = scatter_seq(later(fv_part, o_rows))
-    h_part, d_norm_gain = against_rows(later(dz, fv_part), both, h_all, norm_gain[None])
-    down_parts = gather_begin(later(down_rows, fv_part))
+    fvq_part = dot_first(h_all, dz[:, : 3 * mine], BF)
+    fvq_rows = scatter_seq(later(fvq_part, o_rows))
+    h_part, d_norm_gain = against_rows(later(dz, fvq_part), both, h_all, norm_gain[None])
+    down_parts = gather_begin(later(down_rows, fvq_part))
     h_part, down_parts = lax.optimization_barrier((h_part, down_parts))
     onward, at_hand = scatter_begin(h_part)
 
     zero = jnp.zeros((mine,), F32)
     d_bound = to_heads([d_bound[0], zero, zero, zero], 0)
     small = jnp.concatenate([d_norm_gain[0], d_ffn_gain, d_bound, d_gain[0]])
-    extra = jnp.pad(small, (0, 32 * mine - small.shape[0])).astype(BF).reshape(1, 16, 2 * mine)
-    qg_part = dot_first(h_all, later(dz, h_part)[:, 2 * mine :], BF)
-    qg_part = jnp.concatenate(
-        [qg_part.reshape(seqs, -1, 2 * mine), jnp.broadcast_to(extra, (seqs,) + extra.shape[1:])], axis=1
-    )
-    z_rows = scatter_seq(qg_part.reshape(-1, 2 * mine))
+    extra = jnp.pad(small, (0, 16 * mine - small.shape[0])).astype(BF).reshape(1, 16, mine)
+    g_part = dot_first(h_all, later(dz, h_part)[:, 3 * mine :], BF)
+    g_part = jnp.concatenate(
+        [g_part.reshape(seqs, -1, mine), jnp.broadcast_to(extra, (seqs,) + extra.shape[1:])], axis=1
+    )
+    z_rows = scatter_seq(g_part.reshape(-1, mine))
 
     gu_parts, down_parts, o_rows = later((gu_parts, down_parts, o_rows), onward)
     gu_parts, down_parts = gather_end(*gu_parts), gather_end(*down_parts)
@@ -695,8 +695,8 @@
         grad_o = jnp.concatenate(absolute(o_all), axis=0).astype(F32)
     else:
         grad_o = lax.psum(o_rows.astype(F32), "dp")
-    fv_parts = gather_parts(later(fv_rows, down_parts))
-    qg_parts = gather_parts(later(z_rows, fv_parts[1:3], d_h))
+    fvq_parts = gather_parts(later(fvq_rows, down_parts))
+    g_parts = gather_parts(later(z_rows, fvq_parts[1:3], d_h))
 
     order = jnp.arange(4, dtype=jnp.int32) ^ dp.astype(jnp.int32)
 
@@ -723,9 +723,9 @@
     join_hidden = functools.partial(hidden_kernel, chunk, seqs)
     grad_gate, grad_up = whole_rows(gu_parts, join_hidden, ff, chunk % 16 == 0)
     join_heads = functools.partial(heads_kernel, heads)
-    grad_f, grad_i = whole_rows(fv_parts, join_heads, mine, True)
-    grad_q, grad_g = whole_rows(qg_parts, join_heads, mine, True, fv_rows.shape[0])
-    small = jnp.concatenate(qg_parts, axis=0).reshape(4, -1, 2 * mine)[:, fv_rows.shape[0] :]
+    grad_f, grad_i, grad_q = whole_rows(fvq_parts, join_heads, mine, True)
+    [grad_g] = whole_rows(g_parts, join_heads, mine, True, fvq_rows.shape[0])
+    small = jnp.concatenate(g_parts, axis=0).reshape(4, -1, mine)[:, fvq_rows.shape[0] :]
     small = jnp.sum(small.astype(F32), axis=0).reshape(-1)
 
     u1 = d_h * norm_gain

time: 702 us -> 695 us (0.990)
  waiting for transfers between devices: 293 us -> 277 us
  local copies, waits for them, and re-layouts: 61.8 us -> 70.4 us
    ppermute x61, waiting for transfers between devices: 275 us -> 251 us  [swap(): return lax.ppermute(value, 'dp', [(s, s ^ bits) for s in range(count)])]
    reduce_scatter x5, waiting for transfers between devices: 1.65 us -> 10.2 us  [scatter_seq(): lax.psum_scatter(value.astype(BF), 'seq', scatter_dimension=0, tiled=True)]
    unnamed x131 -> x135, local copies, waits for them, and re-layouts: 31.9 us -> 37.6 us
  transfers between devices with their start and end apart: 75 -> 75, of which waited for: 45 -> 47; matrix products, arithmetic and copies ran while one was open for 28% -> 29% of each run, Pallas kernels for 12% -> 12%
where the time goes in v6:
time: 695 us; the launch traced here: 689 us
  waiting for transfers between devices  277 us (40%)
  matrix products  109 us (16%)
  Pallas kernels  90.3 us (13%)
  starting transfers between devices  81.1 us (12%)
  local copies, waits for them, and re-layouts  70.4 us (10%)
  other arithmetic  45.8 us (7%)
  between operations  15.4 us (2%)
    ppermute x61, waiting for transfers between devices, swap(): return lax.ppermute(value, 'dp', [(s, s ^ bits) for s in range(count)])  251 us
    pallas_call x14, Pallas kernels, call(): pl.pallas_call(kernel, grid_spec=pltpu.PrefetchScalarGridSpec(num_scalar_...  90.3 us
    ppermute x61, starting transfers between devices, swap(): return lax.ppermute(value, 'dp', [(s, s ^ bits) for s in range(count)])  68.1 us
    dot_general x5, matrix products, dot_first(): lax.dot_general(left, right, (((0,), (0,)), ((), ())), preferred_element_...  45.3 us
    unnamed x135, local copies, waits for them, and re-layouts  37.6 us
    dot_general x3, matrix products, dot_last(): lax.dot_general(left, right, (((1,), (1,)), ((), ())), preferred_element_...  34.3 us
    dot_general x3, matrix products, mm(): return jnp.dot(left, right, preferred_element_type=F32).astype(kind)  29.4 us
  transfers between devices with their start and end apart: 75, of which 47 were waited for; matrix products, arithmetic and copies ran while one was open for 29% of the time, Pallas kernels for 12%

profile of v6, /device:TPU:0, one launch (start us, length us, event | category | flops | bytes accessed | tf_op | source)
XLA Modules:
  0.0 688.9 jit_solution(12383089910936805658)
XLA Ops:
  19.1 21.8 %collective-permute-done = bf16[256,2048]{1,0:T(8,128)(2,1)S(1)} collective-permute-done((bf16[256,2048]{1,0:T(8,128)(2,1)}, bf16[256,2048]{1,0:T(8,128)(2,1)S(1)}, u32[]{:S(2)}, u32[]{:S(2)}) %collective-permute-start) | collective-permute-done | bytes 1048608 | tf_op jit(solution)/shard_map/ppermute | solution.py:47
  46.5 7.8 %collective-permute-done.2 = bf16[128,2048]{1,0:T(8,128)(2,1)S(1)} collective-permute-done((bf16[128,2048]{1,0:T(8,128)(2,1)S(1)}, bf16[128,2048]{1,0:T(8,128)(2,1)S(1)}, u32[]{:S(2)}, u32[]{:S(2)}) %collective-permute-start.2) | collective-permute-done | bytes 524320 | tf_op jit(solution)/shard_map/ppermute | solution.py:47
  69.8 20.5 %collective-permute-done.4 = bf16[256,2048]{1,0:T(8,128)(2,1)S(1)} collective-permute-done((bf16[256,2048]{1,0:T(8,128)(2,1)S(1)}, bf16[256,2048]{1,0:T(8,128)(2,1)S(1)}, u32[]{:S(2)}, u32[]{:S(2)}) %collective-permute-start.4) | collective-permute-done | bytes 1048608 | tf_op jit(solution)/shard_map/ppermute | solution.py:47
  104.4 10.0 %all-gather.4.cloned.1.call-done.right_ref = bf16[2048,2560]{1,0:T(8,128)(2,1)} async-done(((bf16[256,2560]{1,0:T(8,128)(2,1)}), bf16[2048,2560]{1,0:T(8,128)(2,1)}) %all-gather.4.cloned.1.call-update) | async-done | bytes 10485776 | tf_op jit(solution)/shard_map/all_gather | solution.py:518
  114.4 7.8 %shard_map.255.f_ref.v_ref = f32[1024,1024]{1,0:T(8,128)S(1)} custom-call(bf16[1024,2048]{1,0:T(8,128)(2,1)} %constant_dynamic-update-slice_fusion.left_ref.beside_ref, bf16[2048,2560]{1,0:T(8,128)(2,1)} %all-gather.4.cloned.1.call-done.right_ref), custom_call_target="tpu_custom_call" | custom-call | flops 80000000 | bytes 65536 | tf_op jit(solution)/shard_map/pallas_call | solution.py:343
  138.8 7.9 %shard_map.258.q_ref.g_ref = f32[1024,1024]{1,0:T(8,128)S(1)} custom-call(bf16[1024,2048]{1,0:T(8,128)(2,1)} %constant_dynamic-update-slice_fusion.left_ref.beside_ref, bf16[2048,2560]{1,0:T(8,128)(2,1)} %all-gather.4.cloned.1.call-done.right_ref), custom_call_target="tpu_custom_call" | custom-call | flops 80000000 | bytes 65536 | tf_op jit(solution)/shard_map/pallas_call | solution.py:343
  148.6 11.8 %shard_map.259 = (f32[1024,512]{1,0:T(8,128)S(1)}, bf16[1024,512]{1,0:T(8,128)(2,1)S(1)}) custom-call(s32[4,2]{1,0:T(4,128)S(1)} %broadcast_in_dim.43.starts, f32[1024,1024]{1,0:T(8,128)} %copy-done.2, f32[1024,1024]{1,0:T(8,128)} %copy-done.2, f32[1024,1024]{1,0:T(8,128)} %copy-done.3, f32[1,512]{1,0:T(1,128)S(1)} %dynamic-slice_bitcast_fusion.b_ref), custom_call_target="tpu_custom_call" | custom-call | flops 30000000 | bytes 65536 | tf_op jit(solution)/shard_map/pallas_call | solution.py:343
  180.5 10.8 %collective-permute-done.13 = bf16[128,2048]{1,0:T(8,128)(2,1)S(1)} collective-permute-done((bf16[128,2048]{1,0:T(8,128)(2,1)S(1)}, bf16[128,2048]{1,0:T(8,128)(2,1)S(1)}, u32[]{:S(2)}, u32[]{:S(2)}) %collective-permute-start.13) | collective-permute-done | bytes 524320 | tf_op jit(solution)/shard_map/ppermute | solution.py:47
  197.7 6.4 collective-permute-done.12
  204.1 9.5 %collective-permute-done.14 = bf16[128,2048]{1,0:T(8,128)(2,1)S(1)} collective-permute-done((bf16[128,2048]{1,0:T(8,128)(2,1)S(1)}, bf16[128,2048]{1,0:T(8,128)(2,1)S(1)}, u32[]{:S(2)}, u32[]{:S(2)}) %collective-permute-start.14) | collective-permute-done | bytes 524320 | tf_op jit(solution)/shard_map/ppermute | solution.py:47
  220.0 22.6 %collective-permute-done.18 = bf16[256,2048]{1,0:T(8,128)(2,1)S(1)} collective-permute-done((bf16[256,2048]{1,0:T(8,128)(2,1)S(1)}, bf16[256,2048]{1,0:T(8,128)(2,1)S(1)}, u32[]{:S(2)}, u32[]{:S(2)}) %collective-permute-start.18) | collective-permute-done | bytes 1048608 | tf_op jit(solution)/shard_map/ppermute | solution.py:47
  247.3 6.9 %collective-permute-done.20 = bf16[128,2048]{1,0:T(8,128)(2,1)S(1)} collective-permute-done((bf16[128,2048]{1,0:T(8,128)(2,1)S(1)}, bf16[128,2048]{1,0:T(8,128)(2,1)S(1)}, u32[]{:S(2)}, u32[]{:S(2)}) %collective-permute-start.20) | collective-permute-done | bytes 524320 | tf_op jit(solution)/shard_map/ppermute | solution.py:47
  255.9 17.3 %fusion.31 = f32[1024,2816]{1,0:T(8,128)S(1)} fusion(bf16[1024,2048]{1,0:T(8,128)(2,1)} %constant_dynamic-update-slice_fusion.10, bf16[2048,2816]{0,1:T(8,128)(2,1)} %all-gather.8.cloned.1.call-done), kind=kOutput, calls=%fused_computation.158 | convolution fusion | flops 11811160064 | bytes 27262976 | tf_op jit(solution)/shard_map/dot_general | solution.py:30
  279.0 10.7 %convolution_convert_fusion.2 = bf16[1408,2048]{1,0:T(8,128)(2,1)} fusion(bf16[1024,1408]{1,0:T(8,128)(2,1)S(1)} %multiply_convert_fusion.2, bf16[1024,2048]{1,0:T(8,128)(2,1)} %constant_dynamic-update-slice_fusion.5), kind=kOutput, calls=%fused_computation.2 | convolution fusion | flops 5908463616 | bytes 12845056 | tf_op jit(solution)/shard_map/dot_general | solution.py:34
  290.5 14.2 %multiply_convert_fusion.1 = (bf16[1024,1408]{1,0:T(8,128)(2,1)S(1)}, bf16[1024,1408]{1,0:T(8,128)(2,1)S(1)}) fusion(f32[1024,2816]{1,0:T(8,128)} %copy-done.28, bf16[1024,2048]{1,0:T(8,128)(2,1)} %constant_dynamic-update-slice_fusion.5, bf16[1408,2048]{1,0:T(8,128)(2,1)} %all-gather.6.cloned.1.call-done), kind=kOutput, calls=%fused_computation.5 | convolution fusion | flops 5924323328 | bytes 27262976 | tf_op jit(solution)/shard_map/dot_general | solution.py:40
  305.2 16.4 %convolution_convert_fusion.3 = bf16[1024,2048]{1,0:T(8,128)(2,1)} fusion(bf16[2048,2816]{0,1:T(8,128)(2,1)} %all-gather.8.cloned.1.call-done, bf16[1024,1408]{1,0:T(8,128)(2,1)S(1)} %get-tuple-element.147, bf16[1024,1408]{1,0:T(8,128)(2,1)S(1)} %get-tuple-element.146), kind=kOutput, calls=%fused_computation.14 | convolution fusion | flops 11824791552 | bytes 21495808 | tf_op jit(solution)/shard_map/dot_general | solution.py:40
  321.5 17.9 %convolution_convert_fusion = bf16[2048,2816]{1,0:T(8,128)(2,1)} fusion(bf16[1024,2048]{1,0:T(8,128)(2,1)} %constant_dynamic-update-slice_fusion.10, bf16[1024,2816]{1,0:T(8,128)(2,1)S(1)} %pad_maximum_fusion), kind=kOutput, calls=%fused_computation | convolution fusion | flops 11816927232 | bytes 21495808 | tf_op jit(solution)/shard_map/dot_general | solution.py:34
  346.5 10.7 %collective-permute-done.23 = bf16[128,2048]{1,0:T(8,128)(2,1)S(1)} collective-permute-done((bf16[128,2048]{1,0:T(8,128)(2,1)S(1)}, bf16[128,2048]{1,0:T(8,128)(2,1)S(1)}, u32[]{:S(2)}, u32[]{:S(2)}) %collective-permute-start.23) | collective-permute-done | bytes 524320 | tf_op jit(solution)/shard_map/ppermute | solution.py:47
  363.3 6.6 collective-permute-done.22
  370.0 10.4 %collective-permute-done.24 = bf16[128,2048]{1,0:T(8,128)(2,1)} collective-permute-done((bf16[128,2048]{1,0:T(8,128)(2,1)}, bf16[128,2048]{1,0:T(8,128)(2,1)}, u32[]{:S(2)}, u32[]{:S(2)}) %collective-permute-start.24) | collective-permute-done | bytes 524320 | tf_op jit(solution)/shard_map/ppermute | solution.py:47
  388.1 9.7 %convolution_convert_fusion.4 = bf16[1024,2048]{1,0:T(8,128)(2,1)S(1)} fusion(bf16[1024,1408]{1,0:T(8,128)(2,1)} %copy-done.35, bf16[1408,2048]{1,0:T(8,128)(2,1)} %all-gather.6.cloned.1.call-done), kind=kOutput, calls=%fused_computation.15 | convolution fusion | flops 5907677184 | bytes 12845056 | tf_op jit(solution)/shard_map/dot_general | solution.py:30
  397.8 12.7 %collective-permute-done.28 = bf16[256,2048]{1,0:T(8,128)(2,1)S(1)} collective-permute-done((bf16[256,2048]{1,0:T(8,128)(2,1)}, bf16[256,2048]{1,0:T(8,128)(2,1)S(1)}, u32[]{:S(2)}, u32[]{:S(2)}) %collective-permute-start.28) | collective-permute-done | bytes 1048608 | tf_op jit(solution)/shard_map/ppermute | solution.py:47
  413.0 9.9 %collective-permute-done.30 = bf16[128,2048]{1,0:T(8,128)(2,1)S(1)} collective-permute-done((bf16[128,2048]{1,0:T(8,128)(2,1)S(1)}, bf16[128,2048]{1,0:T(8,128)(2,1)S(1)}, u32[]{:S(2)}, u32[]{:S(2)}) %collective-permute-start.30) | collective-permute-done | bytes 524320 | tf_op jit(solution)/shard_map/ppermute | solution.py:47
  442.4 7.3 %collective-permute-done.32 = bf16[256,2048]{1,0:T(8,128)(2,1)S(1)} collective-permute-done((bf16[256,2048]{1,0:T(8,128)(2,1)}, bf16[256,2048]{1,0:T(8,128)(2,1)S(1)}, u32[]{:S(2)}, u32[]{:S(2)}) %collective-permute-start.32) | collective-permute-done | bytes 1048608 | tf_op jit(solution)/shard_map/ppermute | solution.py:47
  455.0 10.8 %collective-permute-done.35 = bf16[128,2048]{1,0:T(8,128)(2,1)S(1)} collective-permute-done((bf16[128,2048]{1,0:T(8,128)(2,1)S(1)}, bf16[128,2048]{1,0:T(8,128)(2,1)S(1)}, u32[]{:S(2)}, u32[]{:S(2)}) %collective-permute-start.35) | collective-permute-done | bytes 524320 | tf_op jit(solution)/shard_map/ppermute | solution.py:47
  478.4 6.3 collective-permute-done.36
  502.1 16.1 %shard_map.263 = (bf16[1024,2048]{1,0:T(8,128)(2,1)}, f32[1,512]{1,0:T(1,128)S(1)}) custom-call(s32[4,2]{1,0:T(4,128)S(1)} %copy-done.17, s32[1]{0:T(128)} %bitcast.20.whole, f32[1024,1024]{1,0:T(8,128)} %copy-done.2, f32[1024,1024]{1,0:T(8,128)} %copy-done.2, f32[1024,1024]{1,0:T(8,128)} %copy-done.3, f32[1,512]{1,0:T(1,128)S(1)} %copy-done.19, ...), custom_call_target="tpu_custom_call" | custom-call | flops 80000000 | bytes 65536 | tf_op jit(solution)/shard_map/pallas_call | solution.py:343
  524.2 10.6 %convolution_convert_fusion.1 = bf16[2048,1536]{1,0:T(8,128)(2,1)} fusion(bf16[1024,2048]{1,0:T(8,128)(2,1)S(1)} %copy-done.24, bf16[1024,2048]{1,0:T(8,128)(2,1)} %get-tuple-element.111.left_ref), kind=kOutput, calls=%fused_computation.1 | convolution fusion | flops 6445596672 | bytes 13631488 | tf_op jit(solution)/shard_map/dot_general | solution.py:34
  538.2 14.2 %shard_map.264 = (bf16[1024,2048]{1,0:T(8,128)(2,1)S(1)}, f32[1,2048]{1,0:T(1,128)S(1)}) custom-call(bf16[1024,2048]{1,0:T(8,128)(2,1)} %get-tuple-element.111.left_ref, bf16[2048,2560]{1,0:T(8,128)(2,1)} %all-gather.4.cloned.1.call-done.right_ref, bf16[1024,2048]{1,0:T(8,128)(2,1)} %constant_dynamic-update-slice_fusion.left_ref.beside_ref, ...), custom_call_target="tpu_custom_call" | custom-call | flops 80000000 | bytes 65536 | tf_op jit(solution)/shard_map/pallas_call | solution.py:343
  585.2 7.1 %collective-permute-done.52 = bf16[88,2048]{1,0:T(8,128)(2,1)S(1)} collective-permute-done((bf16[88,2048]{1,0:T(8,128)(2,1)S(1)}, bf16[88,2048]{1,0:T(8,128)(2,1)S(1)}, u32[]{:S(2)}, u32[]{:S(2)}) %collective-permute-start.52) | collective-permute-done | bytes 360480 | tf_op jit(solution)/shard_map/ppermute | solution.py:47
  614.7 13.5 %collective-permute-done.65 = bf16[128,2816]{1,0:T(8,128)(2,1)S(1)} collective-permute-done((bf16[128,2816]{1,0:T(8,128)(2,1)S(1)}, bf16[128,2816]{1,0:T(8,128)(2,1)S(1)}, u32[]{:S(2)}, u32[]{:S(2)}) %collective-permute-start.65) | collective-permute-done | bytes 720928 | tf_op jit(solution)/shard_map/ppermute | solution.py:47
  638.2 9.7 %reduce-scatter.10.cloned.1.call-done = bf16[272,512]{1,0:T(8,128)(2,1)} async-done(((bf16[2176,512]{1,0:T(8,128)(2,1)}), bf16[272,512]{1,0:T(8,128)(2,1)}) %reduce-scatter.10.cloned.1.call-update) | async-done | bytes 278544 | tf_op jit(solution)/shard_map/reduce_scatter | solution.py:521
  (369 shorter events, 297.5 us)
Async XLA Ops:
  7.2 107.2 %all-gather.4.cloned.1.call-start = ((), (), s32[]{:S(2)}) async-start(), calls=%async_computation.5 | async-start | bytes 11796480 | tf_op jit(solution)/shard_map/all_gather | solution.py:518
  12.1 243.8 %all-gather.8.cloned.1.call-start = ((), (), s32[]{:S(2)}) async-start(), calls=%async_computation.7 | async-start | bytes 12976128 | tf_op jit(solution)/shard_map/all_gather | solution.py:518
  14.7 26.3 %collective-permute-start = (bf16[256,2048]{1,0:T(8,128)(2,1)}, bf16[256,2048]{1,0:T(8,128)(2,1)S(1)}, u32[]{:S(2)}, u32[]{:S(2)}) collective-permute-start(bf16[256,2048]{1,0:T(8,128)(2,1)} %get-tuple-element.145), channel_id=1, source_target_pairs={{0,8},{8,0},{16,24},{24,16},{1,9},{9,1},{17,25},{25,17},{2,10},{10... | collective-permute-start | bytes 3145736 | tf_op jit(solution)/shard_map/ppermute | solution.py:47
  17.6 25.3 %collective-permute-start.1 = (bf16[256,2048]{1,0:T(8,128)(2,1)}, bf16[256,2048]{1,0:T(8,128)(2,1)S(1)}, u32[]{:S(2)}, u32[]{:S(2)}) collective-permute-start(bf16[256,2048]{1,0:T(8,128)(2,1)} %get-tuple-element.145), channel_id=1, source_target_pairs={{0,16},{8,24},{16,0},{24,8},{1,17},{9,25},{17,1},{25,9},{2,18},{10... | collective-permute-start | bytes 3145736 | tf_op jit(solution)/shard_map/ppermute | solution.py:47
  66.6 223.9 %all-gather.6.cloned.1.call-start = ((), (), s32[]{:S(2)}) async-start(), calls=%async_computation.6 | async-start | bytes 6488064 | tf_op jit(solution)/shard_map/all_gather | solution.py:518
  68.6 24.0 %collective-permute-start.5 = (bf16[256,2048]{1,0:T(8,128)(2,1)S(1)}, bf16[256,2048]{1,0:T(8,128)(2,1)S(1)}, u32[]{:S(2)}, u32[]{:S(2)}) collective-permute-start(bf16[256,2048]{1,0:T(8,128)(2,1)S(1)} %copy-done.32), channel_id=1, source_target_pairs={{0,16},{8,24},{16,0},{24,8},{1,17},{9,25},{17,1},{25,9},{2,18},{10... | collective-permute-start | bytes 3145736 | tf_op jit(solution)/shard_map/ppermute | solution.py:47
  135.8 28.0 %collective-permute-start.11 = (bf16[256,2048]{1,0:T(8,128)(2,1)}, bf16[256,2048]{1,0:T(8,128)(2,1)}, u32[]{:S(2)}, u32[]{:S(2)}) collective-permute-start(bf16[256,2048]{1,0:T(8,128)(2,1)} %get-tuple-element.76), channel_id=1, source_target_pairs={{0,8},{8,0},{16,24},{24,16},{1,9},{9,1},{17,25},{25,17},{2,10},{10... | collective-permute-start | bytes 3145736 | tf_op jit(solution)/shard_map/ppermute | solution.py:47
  137.3 24.5 %collective-permute-start.9 = (bf16[16,144,128]{2,1,0:T(8,128)(2,1)S(1)}, bf16[16,144,128]{2,1,0:T(8,128)(2,1)}, u32[]{:S(2)}, u32[]{:S(2)}) collective-permute-start(bf16[16,144,128]{2,1,0:T(8,128)(2,1)S(1)} %shard_map.257), channel_id=1, source_target_pairs={{1,3},{5,7},{9,11},{13,15},{17,19},{21,23},{25,27},{29,31}} | collective-permute-start | bytes 1769480 | tf_op jit(solution)/shard_map/ppermute | solution.py:440
  178.5 25.6 %collective-permute-start.12 = (bf16[128,2048]{1,0:T(8,128)(2,1)}, bf16[128,2048]{1,0:T(8,128)(2,1)}, u32[]{:S(2)}, u32[]{:S(2)}) collective-permute-start(bf16[128,2048]{1,0:T(8,128)(2,1)} %get-tuple-element.166), channel_id=1, source_target_pairs={{0,8},{8,0},{16,24},{24,16},{1,9},{9,1},{17,25},{25,17},{2,10},{10... | collective-permute-start | bytes 1572872 | tf_op jit(solution)/shard_map/ppermute | solution.py:47
  180.0 24.2 %collective-permute-start.17 = (bf16[128,2048]{1,0:T(8,128)(2,1)S(1)}, bf16[128,2048]{1,0:T(8,128)(2,1)}, u32[]{:S(2)}, u32[]{:S(2)}) collective-permute-start(bf16[128,2048]{1,0:T(8,128)(2,1)S(1)} %get-tuple-element.167), channel_id=1, source_target_pairs={{0,16},{8,24},{16,0},{24,8},{1,17},{9,25},{17,1},{25,9},{2,18},{10... | collective-permute-start | bytes 1572872 | tf_op jit(solution)/shard_map/ppermute | solution.py:47
  197.7 188.4 %reduce-scatter.6.cloned.1.call-start = ((), (), s32[]{:S(2)}) async-start(), calls=%async_computation.8 | async-start | bytes 6488064 | tf_op jit(solution)/shard_map/reduce_scatter | solution.py:521
  218.9 23.7 %collective-permute-start.18 = (bf16[256,2048]{1,0:T(8,128)(2,1)S(1)}, bf16[256,2048]{1,0:T(8,128)(2,1)S(1)}, u32[]{:S(2)}, u32[]{:S(2)}) collective-permute-start(bf16[256,2048]{1,0:T(8,128)(2,1)S(1)} %get-tuple-element.141), channel_id=1, source_target_pairs={{0,8},{8,0},{16,24},{24,16},{1,9},{9,1},{17,25},{25,17},{2,10},{10... | collective-permute-start | bytes 3145736 | tf_op jit(solution)/shard_map/ppermute | solution.py:47
  219.4 23.8 %collective-permute-start.19 = (bf16[256,2048]{1,0:T(8,128)(2,1)S(1)}, bf16[256,2048]{1,0:T(8,128)(2,1)S(1)}, u32[]{:S(2)}, u32[]{:S(2)}) collective-permute-start(bf16[256,2048]{1,0:T(8,128)(2,1)S(1)} %get-tuple-element.141), channel_id=1, source_target_pairs={{0,16},{8,24},{16,0},{24,8},{1,17},{9,25},{17,1},{25,9},{2,18},{10... | collective-permute-start | bytes 3145736 | tf_op jit(solution)/shard_map/ppermute | solution.py:47
  289.7 199.8 %reduce-scatter.8.cloned.1.call-start = ((), (), s32[]{:S(2)}) async-start(), calls=%async_computation.9 | async-start | bytes 12976128 | tf_op jit(solution)/shard_map/reduce_scatter | solution.py:521
  339.5 195.4 %reduce-scatter.12.cloned.1.call-start = ((), (), s32[]{:S(2)}) async-start(), calls=%async_computation.11 | async-start | bytes 2359296 | tf_op jit(solution)/shard_map/reduce_scatter | solution.py:521
  345.4 24.6 %collective-permute-start.22 = (bf16[128,2048]{1,0:T(8,128)(2,1)}, bf16[128,2048]{1,0:T(8,128)(2,1)S(1)}, u32[]{:S(2)}, u32[]{:S(2)}) collective-permute-start(bf16[128,2048]{1,0:T(8,128)(2,1)} %get-tuple-element.165), channel_id=1, source_target_pairs={{0,8},{8,0},{16,24},{24,16},{1,9},{9,1},{17,25},{25,17},{2,10},{10... | collective-permute-start | bytes 1572872 | tf_op jit(solution)/shard_map/ppermute | solution.py:47
  346.0 24.0 %collective-permute-start.27 = (bf16[128,2048]{1,0:T(8,128)(2,1)}, bf16[128,2048]{1,0:T(8,128)(2,1)}, u32[]{:S(2)}, u32[]{:S(2)}) collective-permute-start(bf16[128,2048]{1,0:T(8,128)(2,1)} %get-tuple-element.163), channel_id=1, source_target_pairs={{0,16},{8,24},{16,0},{24,8},{1,17},{9,25},{17,1},{25,9},{2,18},{10... | collective-permute-start | bytes 1572872 | tf_op jit(solution)/shard_map/ppermute | solution.py:47
  386.0 24.4 %collective-permute-start.28 = (bf16[256,2048]{1,0:T(8,128)(2,1)}, bf16[256,2048]{1,0:T(8,128)(2,1)S(1)}, u32[]{:S(2)}, u32[]{:S(2)}) collective-permute-start(bf16[256,2048]{1,0:T(8,128)(2,1)} %get-tuple-element.88), channel_id=1, source_target_pairs={{0,8},{8,0},{16,24},{24,16},{1,9},{9,1},{17,25},{25,17},{2,10},{10... | collective-permute-start | bytes 3145736 | tf_op jit(solution)/shard_map/ppermute | solution.py:47
  387.5 24.2 %collective-permute-start.29 = (bf16[256,2048]{1,0:T(8,128)(2,1)}, bf16[256,2048]{1,0:T(8,128)(2,1)S(1)}, u32[]{:S(2)}, u32[]{:S(2)}) collective-permute-start(bf16[256,2048]{1,0:T(8,128)(2,1)} %get-tuple-element.88), channel_id=1, source_target_pairs={{0,16},{8,24},{16,0},{24,8},{1,17},{9,25},{17,1},{25,9},{2,18},{10... | collective-permute-start | bytes 3145736 | tf_op jit(solution)/shard_map/ppermute | solution.py:47
  453.5 24.8 %collective-permute-start.34 = (bf16[128,2048]{1,0:T(8,128)(2,1)}, bf16[128,2048]{1,0:T(8,128)(2,1)}, u32[]{:S(2)}, u32[]{:S(2)}) collective-permute-start(bf16[128,2048]{1,0:T(8,128)(2,1)} %get-tuple-element.159), channel_id=1, source_target_pairs={{0,8},{8,0},{16,24},{24,16},{1,9},{9,1},{17,25},{25,17},{2,10},{10... | collective-permute-start | bytes 1572872 | tf_op jit(solution)/shard_map/ppermute | solution.py:47
  454.2 24.2 %collective-permute-start.39 = (bf16[128,2048]{1,0:T(8,128)(2,1)}, bf16[128,2048]{1,0:T(8,128)(2,1)}, u32[]{:S(2)}, u32[]{:S(2)}) collective-permute-start(bf16[128,2048]{1,0:T(8,128)(2,1)} %get-tuple-element.157), channel_id=1, source_target_pairs={{0,16},{8,24},{16,0},{24,8},{1,17},{9,25},{17,1},{25,9},{2,18},{10... | collective-permute-start | bytes 1572872 | tf_op jit(solution)/shard_map/ppermute | solution.py:47
  472.8 161.4 %reduce-scatter.14.cloned.1.call-start = ((), (), s32[]{:S(2)}) async-start(), calls=%async_computation.12 | async-start | bytes 7077888 | tf_op jit(solution)/shard_map/reduce_scatter | solution.py:521
  489.5 33.3 %collective-permute-start.42 = (bf16[256,2816]{1,0:T(8,128)(2,1)}, bf16[256,2816]{1,0:T(8,128)(2,1)}, u32[]{:S(2)}, u32[]{:S(2)}) collective-permute-start(bf16[256,2816]{1,0:T(8,128)(2,1)} %reduce-scatter.8.cloned.1.call-done), channel_id=1, source_target_pairs={{0,8},{8,0},{16,24},{24,16},{1,9},{9,1},{17,25},{25,17},{2,10},{10... | collective-permute-start | bytes 4325384 | tf_op jit(solution)/shard_map/ppermute | solution.py:47
  490.9 33.3 %collective-permute-start.43 = (bf16[256,2816]{1,0:T(8,128)(2,1)}, bf16[256,2816]{1,0:T(8,128)(2,1)}, u32[]{:S(2)}, u32[]{:S(2)}) collective-permute-start(bf16[256,2816]{1,0:T(8,128)(2,1)} %reduce-scatter.8.cloned.1.call-done), channel_id=1, source_target_pairs={{0,16},{8,24},{16,0},{24,8},{1,17},{9,25},{17,1},{25,9},{2,18},{10... | collective-permute-start | bytes 4325384 | tf_op jit(solution)/shard_map/ppermute | solution.py:47
  534.8 113.1 %reduce-scatter.10.cloned.1.call-start = ((), (), s32[]{:S(2)}) async-start(), calls=%async_computation.10 | async-start | bytes 2506752 | tf_op jit(solution)/shard_map/reduce_scatter | solution.py:521
  560.7 37.2 %collective-permute-start.46 = (bf16[128,2048]{1,0:T(8,128)(2,1)}, bf16[128,2048]{1,0:T(8,128)(2,1)}, u32[]{:S(2)}, u32[]{:S(2)}) collective-permute-start(bf16[128,2048]{1,0:T(8,128)(2,1)} %get-tuple-element.148), channel_id=1, source_target_pairs={{0,8},{8,0},{16,24},{24,16},{1,9},{9,1},{17,25},{25,17},{2,10},{10... | collective-permute-start | bytes 1572872 | tf_op jit(solution)/shard_map/ppermute | solution.py:47
  561.8 37.3 %collective-permute-start.51 = (bf16[128,2048]{1,0:T(8,128)(2,1)}, bf16[128,2048]{1,0:T(8,128)(2,1)}, u32[]{:S(2)}, u32[]{:S(2)}) collective-permute-start(bf16[128,2048]{1,0:T(8,128)(2,1)} %get-tuple-element.149), channel_id=1, source_target_pairs={{0,16},{8,24},{16,0},{24,8},{1,17},{9,25},{17,1},{25,9},{2,18},{10... | collective-permute-start | bytes 1572872 | tf_op jit(solution)/shard_map/ppermute | solution.py:47
  593.7 34.5 %collective-permute-start.65 = (bf16[128,2816]{1,0:T(8,128)(2,1)S(1)}, bf16[128,2816]{1,0:T(8,128)(2,1)S(1)}, u32[]{:S(2)}, u32[]{:S(2)}) collective-permute-start(bf16[128,2816]{1,0:T(8,128)(2,1)S(1)} %slice.262), channel_id=1, source_target_pairs={{0,16},{8,24},{16,0},{24,8},{1,17},{9,25},{17,1},{25,9},{2,18},{10... | collective-permute-start | bytes 2162696 | tf_op jit(solution)/shard_map/ppermute | solution.py:47
  597.9 30.3 %collective-permute-start.66 = (bf16[128,2816]{1,0:T(8,128)(2,1)S(1)}, bf16[128,2816]{1,0:T(8,128)(2,1)S(1)}, u32[]{:S(2)}, u32[]{:S(2)}) collective-permute-start(bf16[128,2816]{1,0:T(8,128)(2,1)S(1)} %slice.263), channel_id=1, source_target_pairs={{0,8},{8,0},{16,24},{24,16},{1,9},{9,1},{17,25},{25,17},{2,10},{10... | collective-permute-start | bytes 2162696 | tf_op jit(solution)/shard_map/ppermute | solution.py:47
  609.5 27.1 %collective-permute-start.62 = (bf16[64,2048]{1,0:T(8,128)(2,1)S(1)}, bf16[64,2048]{1,0:T(8,128)(2,1)S(1)}, u32[]{:S(2)}, u32[]{:S(2)}) collective-permute-start(bf16[64,2048]{1,0:T(8,128)(2,1)S(1)} %copy-done.44), channel_id=1, source_target_pairs={{0,24},{8,16},{16,8},{24,0},{1,25},{9,17},{17,9},{25,1},{2,26},{10... | collective-permute-start | bytes 786440 | tf_op jit(solution)/shard_map/ppermute | solution.py:47
  611.3 25.3 %collective-permute-start.63 = (bf16[64,2048]{1,0:T(8,128)(2,1)S(1)}, bf16[64,2048]{1,0:T(8,128)(2,1)S(1)}, u32[]{:S(2)}, u32[]{:S(2)}) collective-permute-start(bf16[64,2048]{1,0:T(8,128)(2,1)S(1)} %copy-done.44), channel_id=1, source_target_pairs={{0,16},{8,24},{16,0},{24,8},{1,17},{9,25},{17,1},{25,9},{2,18},{10... | collective-permute-start | bytes 786440 | tf_op jit(solution)/shard_map/ppermute | solution.py:47
  612.0 24.5 %collective-permute-start.64 = (bf16[64,2048]{1,0:T(8,128)(2,1)S(1)}, bf16[64,2048]{1,0:T(8,128)(2,1)S(1)}, u32[]{:S(2)}, u32[]{:S(2)}) collective-permute-start(bf16[64,2048]{1,0:T(8,128)(2,1)S(1)} %copy-done.44), channel_id=1, source_target_pairs={{0,8},{8,0},{16,24},{24,16},{1,9},{9,1},{17,25},{25,17},{2,10},{10... | collective-permute-start | bytes 786440 | tf_op jit(solution)/shard_map/ppermute | solution.py:47
  (94 other events, 1411.5 us)
Sparse Core Ops, SparseCore 0:
  12.2 102.0 all-gather.3
  116.5 109.5 all-gather.7
  228.4 62.0 all-gather.5
  293.2 76.3 reduce-scatter.5
  371.7 117.6 reduce-scatter.7
  492.2 36.1 reduce-scatter.11
  535.0 76.1 reduce-scatter.13
  613.5 34.3 reduce-scatter.9
